TPU v7x, 32 devices: a whole 2x2x4 slice. The times are simulated.
32 devices in a mesh: sp: 16 (over z, y, core), tp: 2 (over x).
Axes of the slice: x: 2, y: 2, z: 4, core: 2. Of those that a mesh axis runs over, the one named last changes fastest.
Arguments:
- patches: bfloat16 [2048, 1536], P('sp'), may hold values from -6 to 6
- caption: bfloat16 [256, 4096], replicated, may hold values from -6 to 6
- band_table: float32 [16, 1024], P(None, 'sp'), may hold values from -6 to 6
- block_item: int32 [64], replicated, may hold values from 0 to 1, as said below
- item_band: int32 [2], replicated, may hold values from 0 to 15
- positions: int32 [2, 2048], P(None, 'sp'), may hold values from 0 to 63
- out_grad: bfloat16 [2048, 1536], P('sp'), may hold values from -6 to 6
- w_query: bfloat16 [1536, 1536], P('sp', 'tp'), may hold values from -0.15625 to 0.15625
- w_key: bfloat16 [1536, 1536], P('sp', 'tp'), may hold values from -0.15625 to 0.15625
- w_value: bfloat16 [1536, 1536], P('sp', 'tp'), may hold values from -0.15625 to 0.15625
- w_out: bfloat16 [1536, 1536], P('tp', 'sp'), may hold values from -0.15625 to 0.15625
- w_gate: bfloat16 [1536, 4096], P('sp', 'tp'), may hold values from -0.15625 to 0.15625
- w_up: bfloat16 [1536, 4096], P('sp', 'tp'), may hold values from -0.15625 to 0.15625
- w_down: bfloat16 [4096, 1536], P('tp', 'sp'), may hold values from -0.09375 to 0.09375
- w_ckey: bfloat16 [4096, 1536], P('sp', 'tp'), may hold values from -0.09375 to 0.09375
- w_cvalue: bfloat16 [4096, 1536], P('sp', 'tp'), may hold values from -0.09375 to 0.09375
- w_ada: bfloat16 [1024, 6144], P('sp'), may hold values from -0.1875 to 0.1875
- b_ada: float32 [6144], replicated, may hold values from -3 to 3
- g_attn_in: float32 [1536], replicated, may hold values from 0.5 to 1.5
- g_attn_out: float32 [1536], replicated, may hold values from 0.5 to 1.5
- g_ffn_in: float32 [1536], replicated, may hold values from 0.5 to 1.5
- g_ffn_out: float32 [1536], replicated, may hold values from 0.5 to 1.5
- g_query: float32 [1536], P('tp'), may hold values from 0.5 to 1.5
- g_key: float32 [1536], P('tp'), may hold values from 0.5 to 1.5
- g_ckey: float32 [1536], P('tp'), may hold values from 0.5 to 1.5
- cross_gate: float32 [24], P('tp'), may hold values from -1.5 to 1.5
Outputs:
- output: float32 [2048, 1536], P('sp')
- d_patches: float32 [2048, 1536], P('sp')
- d_w_query: float32 [1536, 1536], P('sp', 'tp')
- d_w_key: float32 [1536, 1536], P('sp', 'tp')
- d_w_value: float32 [1536, 1536], P('sp', 'tp')
- d_w_out: float32 [1536, 1536], P('tp', 'sp')
- d_w_gate: float32 [1536, 4096], P('sp', 'tp')
- d_w_up: float32 [1536, 4096], P('sp', 'tp')
- d_w_down: float32 [4096, 1536], P('tp', 'sp')
- d_w_ckey: float32 [4096, 1536], P('sp', 'tp')
- d_w_cvalue: float32 [4096, 1536], P('sp', 'tp')
- d_w_ada: float32 [1024, 6144], P('sp')
- d_b_ada: float32 [6144], replicated
- d_g_attn_in: float32 [1536], replicated
- d_g_attn_out: float32 [1536], replicated
- d_g_ffn_in: float32 [1536], replicated
- d_g_ffn_out: float32 [1536], replicated
- d_g_query: float32 [1536], P('tp')
- d_g_key: float32 [1536], P('tp')
- d_g_ckey: float32 [1536], P('tp')
- d_cross_gate: float32 [24], P('tp')
- d_band_table: float32 [16, 1024], P(None, 'sp')
Inputs may be any that keep to these rules, and one draw needn't show every extreme that they name: `block_item`: every item has at least one block. Items occupy consecutive places in the order that lists each device's first block of 32 tokens along sp, then each device's second block, and so on; one item holds a block on every device of sp, which one varies from draw to draw.
All inputs are finite; a program needn't handle non-finite values.
Results may differ from a plain program's by a relative error of at most 0.025.
Values may be sent and summed in bfloat16 or wider, within the bound.
A program may use at most 384 MiB of HBM per device.

v0:
```python
import math

import jax
import jax.numpy as jnp
from jax import lax
from jax.sharding import PartitionSpec as P

D = 1536
H = 24
BANDS = 16
ITEMS = 2
BLK = 32


EPS = 1e-06
NEG = -1e30
FREQ_BASE = 10000.0
HIGH = lax.Precision.HIGHEST


def shifted(block, axis, distance):
    devices = range(lax.axis_size(axis))
    route = [((i - distance) % len(devices), i) for i in devices]
    return lax.ppermute(block, axis, route)


def normed_pair(value):
    recip = lax.rsqrt(jnp.mean(value * value, axis=-1, keepdims=True) + EPS)
    return (value * recip, recip)


def normed_back(grad_hat, normal, recip):
    return recip * (grad_hat - normal * jnp.mean(grad_hat * normal, axis=-1, keepdims=True))


def rotate(value, cos_row, sin_row, cos_col, sin_col):
    quarter = value.shape[-1] // 4
    part_a = value[..., :quarter]
    part_b = value[..., quarter : 2 * quarter]
    part_c = value[..., 2 * quarter : 3 * quarter]
    part_e = value[..., 3 * quarter :]
    return jnp.concatenate(
        [
            part_a * cos_row - part_b * sin_row,
            part_a * sin_row + part_b * cos_row,
            part_c * cos_col - part_e * sin_col,
            part_c * sin_col + part_e * cos_col,
        ],
        axis=-1,
    )


def angles(positions):
    quarter = D // H // 4
    freqs = FREQ_BASE ** (-jnp.arange(quarter, dtype=jnp.float32) / quarter)
    row_angle = positions[0].astype(jnp.float32)[:, None] * freqs[None, :]
    col_angle = positions[1].astype(jnp.float32)[:, None] * freqs[None, :]
    return (
        jnp.cos(row_angle)[:, None, :],
        jnp.sin(row_angle)[:, None, :],
        jnp.cos(col_angle)[:, None, :],
        jnp.sin(col_angle)[:, None, :],
    )


def column_sums(value):
    return jnp.sum(value, axis=0)


def bdot(left, right):
    return jnp.dot(left, right, preferred_element_type=jnp.float32)


def local(
    patches,
    caption,
    band_table,
    block_item,
    item_band,
    positions,
    out_grad,
    w_query,
    w_key,
    w_value,
    w_out,
    w_gate,
    w_up,
    w_down,
    w_ckey,
    w_cvalue,
    w_ada,
    b_ada,
    g_attn_in,
    g_attn_out,
    g_ffn_in,
    g_ffn_out,
    g_query,
    g_key,
    g_ckey,
    cross_gate,
):
    head_dim = D // H
    scale = 1.0 / math.sqrt(head_dim)
    my_rank = lax.axis_index("sp")
    cycle_size = lax.axis_size("sp")
    tok_rows = patches.shape[0]
    text_count = caption.shape[0]
    blocks_dev = tok_rows // BLK
    own_items = jnp.repeat(
        lax.dynamic_slice_in_dim(block_item, my_rank * blocks_dev, blocks_dev), BLK
    )
    item_hot = (own_items[:, None] == jnp.arange(ITEMS, dtype=jnp.int32)[None, :]).astype(
        jnp.float32
    )
    band_hot = (item_band[:, None] == jnp.arange(BANDS, dtype=jnp.int32)[None, :]).astype(
        jnp.float32
    )
    cond_pre = jnp.dot(band_hot, band_table, precision=HIGH)
    cond_sig = jax.nn.sigmoid(cond_pre)
    cond_low = (cond_pre * cond_sig).astype(jnp.bfloat16)
    text_rows = w_ckey.shape[0]
    text_local = lax.dynamic_slice_in_dim(caption, my_rank * text_rows, text_rows, 1)
    mod_part = bdot(cond_low, w_ada)
    ckey_part = bdot(text_local, w_ckey)
    cval_part = bdot(text_local, w_cvalue)
    mod_sum, cap_key_raw, cap_val_raw = lax.psum((mod_part, ckey_part, cval_part), "sp")
    modulation = mod_sum + b_ada
    mod_tok = jnp.dot(item_hot, modulation, precision=HIGH)
    scale_attn = mod_tok[:, :D]
    gate_attn = mod_tok[:, D : 2 * D]
    scale_ffn = mod_tok[:, 2 * D : 3 * D]
    gate_ffn = mod_tok[:, 3 * D :]
    full_query, full_key, full_value, full_out, full_gate, full_up, full_down = (
        lax.all_gather(w_query, "sp", axis=0, tiled=True),
        lax.all_gather(w_key, "sp", axis=0, tiled=True),
        lax.all_gather(w_value, "sp", axis=0, tiled=True),
        lax.all_gather(w_out, "sp", axis=1, tiled=True),
        lax.all_gather(w_gate, "sp", axis=0, tiled=True),
        lax.all_gather(w_up, "sp", axis=0, tiled=True),
        lax.all_gather(w_down, "sp", axis=1, tiled=True),
    )
    heads_dev = full_query.shape[1] // head_dim
    cos_row, sin_row, cos_col, sin_col = angles(positions)
    patch_f = patches.astype(jnp.float32)
    hat_one, recip_one = normed_pair(patch_f)
    factor_one = g_attn_in * (1.0 + scale_attn)
    norm_in = (hat_one * factor_one).astype(jnp.bfloat16)
    query_raw = bdot(norm_in, full_query).reshape(tok_rows, heads_dev, head_dim)
    key_raw = bdot(norm_in, full_key).reshape(tok_rows, heads_dev, head_dim)
    values_low = bdot(norm_in, full_value).astype(jnp.bfloat16)
    gain_query = g_query.reshape(heads_dev, head_dim)
    gain_key = g_key.reshape(heads_dev, head_dim)
    gain_ckey = g_ckey.reshape(heads_dev, head_dim)
    query_hat, query_recip = normed_pair(query_raw)
    queries = rotate(query_hat * gain_query, cos_row, sin_row, cos_col, sin_col).astype(
        jnp.bfloat16
    )
    key_hat, key_recip = normed_pair(key_raw)
    keys_low = rotate(key_hat * gain_key, cos_row, sin_row, cos_col, sin_col).astype(jnp.bfloat16)
    keys_flat = keys_low.reshape(tok_rows, heads_dev * head_dim)
    ckey_hat, ckey_recip = normed_pair(cap_key_raw.reshape(text_count, heads_dev, head_dim))
    cap_keys = (ckey_hat * gain_ckey).astype(jnp.bfloat16)
    cap_values = cap_val_raw.astype(jnp.bfloat16).reshape(text_count, heads_dev, head_dim)
    run_max = jnp.full((heads_dev, tok_rows), NEG, jnp.float32)
    accum = jnp.zeros((tok_rows, heads_dev, head_dim), jnp.float32)
    key_piece = lax.all_gather(keys_flat, "sp", axis=0, tiled=True)
    value_piece = lax.all_gather(values_low, "sp", axis=0, tiled=True)
    count = key_piece.shape[0]
    key_piece = key_piece.reshape(count, heads_dev, head_dim)
    value_piece = value_piece.reshape(count, heads_dev, head_dim)
    key_items = jnp.repeat(block_item, BLK)
    same = (own_items[:, None] == key_items[None, :])[None]
    scores = (
        jnp.einsum("qhd,khd->hqk", queries, key_piece, preferred_element_type=jnp.float32) * scale
    )
    scores = jnp.where(same, scores, NEG)
    new_max = jnp.maximum(run_max, jnp.max(scores, axis=-1))
    weights = jnp.where(same, jnp.exp(scores - new_max[..., None]), 0.0)
    shrink = jnp.exp(run_max - new_max)
    run_sum = jnp.sum(weights, axis=-1)
    accum = accum * shrink.T[:, :, None] + jnp.einsum(
        "hqk,khd->qhd",
        weights.astype(jnp.bfloat16),
        value_piece,
        preferred_element_type=jnp.float32,
    )
    run_max, run_sum, accum = (new_max, run_sum, accum)
    attn_self = accum / run_sum.T[:, :, None]
    log_total = run_max + jnp.log(run_sum)
    cross_scores = (
        jnp.einsum("qhd,khd->hqk", queries, cap_keys, preferred_element_type=jnp.float32) * scale
    )
    cross_exp = jnp.exp(cross_scores - jnp.max(cross_scores, axis=-1, keepdims=True))
    cross_probs = cross_exp / jnp.sum(cross_exp, axis=-1, keepdims=True)
    cross_low = cross_probs.astype(jnp.bfloat16)
    attn_cross = jnp.einsum(
        "hqk,khd->qhd", cross_low, cap_values, preferred_element_type=jnp.float32
    )
    gate_tanh = jnp.tanh(cross_gate)
    mixed = (
        (attn_self + gate_tanh[None, :, None] * attn_cross)
        .astype(jnp.bfloat16)
        .reshape(tok_rows, heads_dev * head_dim)
    )
    attn_branch = lax.psum(bdot(mixed, full_out).astype(jnp.bfloat16), "tp").astype(jnp.float32)
    hat_two, recip_two = normed_pair(attn_branch)
    tanh_one = jnp.tanh(gate_attn)
    resid = patch_f + tanh_one * hat_two * g_attn_out
    hat_three, recip_three = normed_pair(resid)
    factor_three = g_ffn_in * (1.0 + scale_ffn)
    norm_ffn = (hat_three * factor_three).astype(jnp.bfloat16)
    gate_val = bdot(norm_ffn, full_gate)
    up_val = bdot(norm_ffn, full_up)
    gate_sig = jax.nn.sigmoid(gate_val)
    hidden = (gate_val * gate_sig * up_val).astype(jnp.bfloat16)
    ffn_branch = lax.psum(bdot(hidden, full_down).astype(jnp.bfloat16), "tp").astype(jnp.float32)
    hat_four, recip_four = normed_pair(ffn_branch)
    tanh_two = jnp.tanh(gate_ffn)
    output = resid + tanh_two * hat_four * g_ffn_out
    grad_out = out_grad.astype(jnp.float32)
    grad_gate_ffn = grad_out * hat_four * g_ffn_out * (1.0 - tanh_two * tanh_two)
    grad_four = grad_out * tanh_two
    grad_g_ffn_out = column_sums(grad_four * hat_four)
    grad_ffn = normed_back(grad_four * g_ffn_out, hat_four, recip_four).astype(jnp.bfloat16)
    grad_w_down = bdot(hidden.T, grad_ffn)
    grad_hidden = bdot(grad_ffn, full_down.T)
    grad_gate = (grad_hidden * up_val * gate_sig * (1.0 + gate_val * (1.0 - gate_sig))).astype(
        jnp.bfloat16
    )
    grad_up = (grad_hidden * gate_val * gate_sig).astype(jnp.bfloat16)
    grad_w_gate = bdot(norm_ffn.T, grad_gate)
    grad_w_up = bdot(norm_ffn.T, grad_up)
    grad_norm_ffn = lax.psum(
        (bdot(grad_gate, full_gate.T) + bdot(grad_up, full_up.T)).astype(jnp.bfloat16), "tp"
    ).astype(jnp.float32)
    grad_scale_ffn = grad_norm_ffn * hat_three * g_ffn_in
    grad_g_ffn_in = column_sums(grad_norm_ffn * hat_three * (1.0 + scale_ffn))
    grad_resid = grad_out + normed_back(grad_norm_ffn * factor_three, hat_three, recip_three)
    grad_gate_attn = grad_resid * hat_two * g_attn_out * (1.0 - tanh_one * tanh_one)
    grad_two = grad_resid * tanh_one
    grad_g_attn_out = column_sums(grad_two * hat_two)
    grad_attn = normed_back(grad_two * g_attn_out, hat_two, recip_two).astype(jnp.bfloat16)
    grad_w_out = bdot(mixed.T, grad_attn)
    grad_mixed = (
        bdot(grad_attn, full_out.T).astype(jnp.bfloat16).reshape(tok_rows, heads_dev, head_dim)
    )
    grad_mixed_f = grad_mixed.astype(jnp.float32)
    grad_cross_gate = jnp.sum(grad_mixed_f * attn_cross, axis=(0, 2)) * (
        1.0 - gate_tanh * gate_tanh
    )
    grad_cross = (gate_tanh[None, :, None] * grad_mixed_f).astype(jnp.bfloat16)
    grad_cprobs = jnp.einsum(
        "qhd,khd->hqk", grad_cross, cap_values, preferred_element_type=jnp.float32
    )
    grad_cscores = (
        cross_probs * (grad_cprobs - jnp.sum(cross_probs * grad_cprobs, axis=-1, keepdims=True))
    ).astype(jnp.bfloat16)
    grad_query_cross = (
        jnp.einsum("hqk,khd->qhd", grad_cscores, cap_keys, preferred_element_type=jnp.float32)
        * scale
    )
    grad_ckeys_part = (
        jnp.einsum("hqk,qhd->khd", grad_cscores, queries, preferred_element_type=jnp.float32)
        * scale
    )
    grad_cvals_part = jnp.einsum(
        "hqk,qhd->khd", cross_low, grad_cross, preferred_element_type=jnp.float32
    )
    row_delta = jnp.sum(grad_mixed_f * attn_self, axis=-1).T
    zero_three = jnp.zeros((tok_rows, heads_dev, head_dim), jnp.float32)

    def key_turn(cycle_step, carry):
        key_flat, value_flat, key_grad, value_grad, query_grad = carry
        source = (my_rank - cycle_step) % cycle_size
        key_items = jnp.repeat(
            lax.dynamic_slice_in_dim(block_item, source * blocks_dev, blocks_dev), BLK
        )
        same = (own_items[:, None] == key_items[None, :])[None]
        key_piece = key_flat.reshape(tok_rows, heads_dev, head_dim)
        value_piece = value_flat.reshape(tok_rows, heads_dev, head_dim)
        scores = (
            jnp.einsum("qhd,khd->hqk", queries, key_piece, preferred_element_type=jnp.float32)
            * scale
        )
        probs = jnp.where(same, jnp.exp(scores - log_total[..., None]), 0.0)
        grad_probs = jnp.einsum(
            "qhd,khd->hqk", grad_mixed, value_piece, preferred_element_type=jnp.float32
        )
        grad_scores = (probs * (grad_probs - row_delta[..., None])).astype(jnp.bfloat16)
        query_grad = (
            query_grad
            + jnp.einsum("hqk,khd->qhd", grad_scores, key_piece, preferred_element_type=jnp.float32)
            * scale
        )
        key_grad = (
            key_grad
            + jnp.einsum(
                "hqk,qhd->khd", grad_scores, queries, preferred_element_type=jnp.float32
            ).reshape(tok_rows, -1)
            * scale
        )
        value_grad = value_grad + jnp.einsum(
            "hqk,qhd->khd",
            probs.astype(jnp.bfloat16),
            grad_mixed,
            preferred_element_type=jnp.float32,
        ).reshape(tok_rows, -1)
        key_flat, value_flat = shifted((key_flat, value_flat), "sp", 1)
        key_grad, value_grad = (
            shifted(key_grad.astype(jnp.bfloat16), "sp", 1).astype(key_grad.dtype),
            shifted(value_grad.astype(jnp.bfloat16), "sp", 1).astype(value_grad.dtype),
        )
        return (key_flat, value_flat, key_grad, value_grad, query_grad)

    zero_flat = jnp.zeros((tok_rows, heads_dev * head_dim), jnp.float32)
    cycle_out = lax.fori_loop(
        0, cycle_size, key_turn, (keys_flat, values_low, zero_flat, zero_flat, zero_three)
    )
    key_grad = cycle_out[2].reshape(tok_rows, heads_dev, head_dim)
    value_grad = cycle_out[3].reshape(tok_rows, heads_dev, head_dim)
    query_grad = cycle_out[4]
    grad_queries = (query_grad + grad_query_cross).astype(jnp.bfloat16).astype(jnp.float32)
    grad_qnorm = rotate(grad_queries, cos_row, -sin_row, cos_col, -sin_col)
    grad_g_query = jnp.sum(grad_qnorm * query_hat, axis=0).reshape(-1)
    grad_query_raw = (
        normed_back(grad_qnorm * gain_query, query_hat, query_recip)
        .astype(jnp.bfloat16)
        .reshape(tok_rows, -1)
    )
    grad_keys = key_grad.astype(jnp.bfloat16).astype(jnp.float32)
    grad_knorm = rotate(grad_keys, cos_row, -sin_row, cos_col, -sin_col)
    grad_g_key = jnp.sum(grad_knorm * key_hat, axis=0).reshape(-1)
    grad_key_raw = (
        normed_back(grad_knorm * gain_key, key_hat, key_recip)
        .astype(jnp.bfloat16)
        .reshape(tok_rows, -1)
    )
    grad_values = value_grad.astype(jnp.bfloat16).reshape(tok_rows, -1)
    grad_w_query = bdot(norm_in.T, grad_query_raw)
    grad_w_key = bdot(norm_in.T, grad_key_raw)
    grad_w_value = bdot(norm_in.T, grad_values)
    grad_norm_in = lax.psum(
        (
            bdot(grad_query_raw, full_query.T)
            + bdot(grad_key_raw, full_key.T)
            + bdot(grad_values, full_value.T)
        ).astype(jnp.bfloat16),
        "tp",
    ).astype(jnp.float32)
    grad_scale_attn = grad_norm_in * hat_one * g_attn_in
    grad_g_attn_in = column_sums(grad_norm_in * hat_one * (1.0 + scale_attn))
    grad_patches = grad_resid + normed_back(grad_norm_in * factor_one, hat_one, recip_one)
    grad_mod_tok = jnp.concatenate(
        [grad_scale_attn, grad_gate_attn, grad_scale_ffn, grad_gate_ffn], axis=1
    )
    grad_mod_part = jnp.dot(item_hot.T, grad_mod_tok, precision=HIGH)
    summed = lax.psum(
        (
            grad_mod_part,
            grad_g_attn_in,
            grad_g_attn_out,
            grad_g_ffn_in,
            grad_g_ffn_out,
            grad_g_query,
            grad_g_key,
            grad_cross_gate,
            grad_ckeys_part,
            grad_cvals_part,
        ),
        "sp",
    )
    grad_mod = summed[0]
    grad_b_ada = jnp.sum(grad_mod, axis=0)
    grad_w_ada = jnp.dot(cond_low.astype(jnp.float32).T, grad_mod, precision=HIGH)
    grad_cond_act = jnp.dot(grad_mod, w_ada.astype(jnp.float32).T, precision=HIGH)
    grad_cond_pre = grad_cond_act * cond_sig * (1.0 + cond_pre * (1.0 - cond_sig))
    grad_band_table = jnp.dot(band_hot.T, grad_cond_pre, precision=HIGH)
    grad_ckeys = summed[8].astype(jnp.bfloat16).astype(jnp.float32)
    grad_g_ckey = jnp.sum(grad_ckeys * ckey_hat, axis=0).reshape(-1)
    grad_ckey_raw = (
        normed_back(grad_ckeys * gain_ckey, ckey_hat, ckey_recip)
        .astype(jnp.bfloat16)
        .reshape(text_count, -1)
    )
    grad_w_ckey = bdot(text_local.T, grad_ckey_raw)
    grad_w_cvalue = bdot(text_local.T, summed[9].astype(jnp.bfloat16).reshape(text_count, -1))
    shard_query, shard_key, shard_value, shard_out, shard_gate, shard_up, shard_down = (
        lax.psum_scatter(grad_w_query, "sp", scatter_dimension=0, tiled=True),
        lax.psum_scatter(grad_w_key, "sp", scatter_dimension=0, tiled=True),
        lax.psum_scatter(grad_w_value, "sp", scatter_dimension=0, tiled=True),
        lax.psum_scatter(grad_w_out, "sp", scatter_dimension=1, tiled=True),
        lax.psum_scatter(grad_w_gate, "sp", scatter_dimension=0, tiled=True),
        lax.psum_scatter(grad_w_up, "sp", scatter_dimension=0, tiled=True),
        lax.psum_scatter(grad_w_down, "sp", scatter_dimension=1, tiled=True),
    )
    return (
        output,
        grad_patches,
        shard_query,
        shard_key,
        shard_value,
        shard_out,
        shard_gate,
        shard_up,
        shard_down,
        grad_w_ckey,
        grad_w_cvalue,
        grad_w_ada,
        grad_b_ada,
        summed[1],
        summed[2],
        summed[3],
        summed[4],
        summed[5],
        summed[6],
        grad_g_ckey,
        summed[7],
        grad_band_table,
    )


def solution(mesh):
    in_specs = (
        P("sp", None),
        P(),
        P(None, "sp"),
        P(),
        P(),
        P(None, "sp"),
        P("sp", None),
        P("sp", "tp"),
        P("sp", "tp"),
        P("sp", "tp"),
        P("tp", "sp"),
        P("sp", "tp"),
        P("sp", "tp"),
        P("tp", "sp"),
        P("sp", "tp"),
        P("sp", "tp"),
        P("sp", None),
        P(),
        P(),
        P(),
        P(),
        P(),
        P("tp"),
        P("tp"),
        P("tp"),
        P("tp"),
    )
    out_specs = (
        P("sp", None),
        P("sp", None),
        P("sp", "tp"),
        P("sp", "tp"),
        P("sp", "tp"),
        P("tp", "sp"),
        P("sp", "tp"),
        P("sp", "tp"),
        P("tp", "sp"),
        P("sp", "tp"),
        P("sp", "tp"),
        P("sp", None),
        P(),
        P(),
        P(),
        P(),
        P(),
        P("tp"),
        P("tp"),
        P("tp"),
        P("tp"),
        P(None, "sp"),
    )
    return jax.shard_map(local, mesh=mesh, in_specs=in_specs, out_specs=out_specs, check_vma=False)
```

profile of v0, /device:TPU:0, one launch (start us, length us, event | category | flops | bytes accessed | tf_op | source)
XLA Modules:
  0.0 1788.7 jit_solution(18283655661203513670)
XLA Ops:
  16.2 77.3 %all-reduce.19 = (f32[2,6144]{1,0:T(2,128)S(1)}, bf16[256,768]{1,0:T(8,128)(2,1)}) all-reduce(f32[2,6144]{1,0:T(2,128)S(1)} %fusion.135, f32[256,768]{1,0:T(8,128)} %fusion.108), channel_id=1, replica_groups=mesh['sp'=16,'tp'=2] {'sp'}, use_global_device_ids=true, to_apply=%region_0.0 | all-reduce | flops 208896 | bytes 1277952 | tf_op jit(solution)/shard_map/psum | solution.py:126
  112.1 85.8 %all-reduce.10.cloned.1.call-done = f32[256,12,64]{0,2,1:T(8,128)} async-done(((f32[256,12,64]{0,2,1:T(8,128)}), f32[256,12,64]{0,2,1:T(8,128)}) %all-reduce.10.cloned.1.call-update) | async-done | bytes 786448 | tf_op jit(solution)/shard_map/psum | solution.py:126
  199.2 42.3 %all-gather.10.cloned.1.call-done = bf16[1536,768]{1,0:T(8,128)(2,1)} async-done(((bf16[96,768]{1,0:T(8,128)(2,1)}), bf16[1536,768]{1,0:T(8,128)(2,1)}) %all-gather.10.cloned.1.call-update) | async-done | bytes 2359312 | tf_op jit(solution)/shard_map/all_gather | solution.py:134
  253.3 35.1 %all-gather.18.cloned.1.call-done = bf16[2048,768]{1,0:T(8,128)(2,1)} async-done(((bf16[128,768]{1,0:T(8,128)(2,1)}), bf16[2048,768]{1,0:T(8,128)(2,1)}) %all-gather.18.cloned.1.call-update) | async-done | bytes 3145744 | tf_op jit(solution)/shard_map/all_gather | solution.py:167
  293.3 43.5 %all-gather.14.cloned.1.call-done = bf16[2048,768]{0,1:T(8,128)(2,1)} async-done(((bf16[128,768]{0,1:T(8,128)(2,1)}), bf16[2048,768]{0,1:T(8,128)(2,1)}) %all-gather.14.cloned.1.call-update) | async-done | bytes 3145744 | tf_op jit(solution)/shard_map/all_gather | solution.py:166
  350.1 29.6 %all-gather.20.cloned.1.call-done = bf16[768,1536]{0,1:T(8,128)(2,1)} async-done(((bf16[768,96]{0,1:T(8,128)(2,1)}), bf16[768,1536]{0,1:T(8,128)(2,1)}) %all-gather.20.cloned.1.call-update) | async-done | bytes 2359312 | tf_op jit(solution)/shard_map/all_gather | solution.py:137
  385.4 22.3 %all-reduce.12.cloned.1.call-done = bf16[128,1536]{1,0:T(8,128)(2,1)} async-done(((bf16[128,1536]{1,0:T(8,128)(2,1)}), bf16[128,1536]{1,0:T(8,128)(2,1)}) %all-reduce.12.cloned.1.call-update) | async-done | bytes 393232 | tf_op jit(solution)/shard_map/psum | solution.py:205
  411.9 60.0 %all-gather.22.cloned.1.call-done = bf16[1536,2048]{1,0:T(8,128)(2,1)} async-done(((bf16[96,2048]{1,0:T(8,128)(2,1)}), bf16[1536,2048]{1,0:T(8,128)(2,1)}) %all-gather.22.cloned.1.call-update) | async-done | bytes 6291472 | tf_op jit(solution)/shard_map/all_gather | solution.py:138
  476.7 57.8 %all-gather.24.cloned.1.call-done = bf16[1536,2048]{1,0:T(8,128)(2,1)} async-done(((bf16[96,2048]{1,0:T(8,128)(2,1)}), bf16[1536,2048]{1,0:T(8,128)(2,1)}) %all-gather.24.cloned.1.call-update) | async-done | bytes 6291472 | tf_op jit(solution)/shard_map/all_gather | solution.py:139
  539.8 57.5 %all-gather.26.cloned.1.call-done = bf16[2048,1536]{0,1:T(8,128)(2,1)} async-done(((bf16[2048,96]{0,1:T(8,128)(2,1)}), bf16[2048,1536]{0,1:T(8,128)(2,1)}) %all-gather.26.cloned.1.call-update) | async-done | bytes 6291472 | tf_op jit(solution)/shard_map/all_gather | solution.py:140
  597.3 6.0 convolution_convert_fusion.1
  603.3 24.4 %all-reduce.14.cloned.1.call-done = bf16[128,1536]{1,0:T(8,128)(2,1)} async-done(((bf16[128,1536]{1,0:T(8,128)(2,1)}), bf16[128,1536]{1,0:T(8,128)(2,1)}) %all-reduce.14.cloned.1.call-update) | async-done | bytes 393232 | tf_op jit(solution)/shard_map/psum | solution.py:216
  653.4 16.9 all-reduce.16.cloned.1.call-done
  684.2 299.4 %while.24 = (s32[]{:T(128)}, bf16[128,768]{0,1:T(8,128)(2,1)}, bf16[128,768]{0,1:T(8,128)(2,1)}, f32[128,768]{0,1:T(8,128)}, f32[128,768]{0,1:T(8,128)S(1)}, /*i...) while((s32[]{:T(128)}, bf16[128,768]{0,1:T(8,128)(2,1)}, ...), condition=%wide.region_22.23_spmd.clone, body=%wide.region_21.22_spmd.clone.sunk | while | flops 128401424 | bytes 15188576 | solution.py:316
  1022.4 6.4 fusion.148
  1030.0 6.4 fusion.146
  1037.5 6.4 fusion.147
  1054.2 78.7 %all-reduce.20 = (bf16[256,12,64]{0,2,1:T(8,128)(2,1)}, bf16[256,12,64]{0,2,1:T(8,128)(2,1)}, f32[2,6144]{1,0:T(2,128)S(1)}, f32[1536]{0:T(1024)}, f32[1536]{0:T...) all-reduce(f32[256,12,64]{0,2,1:T(8,128)} %fusion.32, ...), channel_id=1, replica_groups=mesh['sp'=16,'tp'=2] {'sp'}, use_global_device_ids=true, to_apply=%region_35.36 | all-reduce | flops 413196 | bytes 2519136 | tf_op jit(solution)/shard_map/psum | solution.py:357
  1146.6 59.7 %reduce-scatter.10.cloned.1.call-done = f32[96,768]{1,0:T(8,128)} async-done(((f32[1536,768]{1,0:T(8,128)}), f32[96,768]{1,0:T(8,128)}) %reduce-scatter.10.cloned.1.call-update) | async-done | bytes 294928 | tf_op jit(solution)/shard_map/reduce_scatter | solution.py:389
  1206.3 79.3 %reduce-scatter.8.cloned.1.call-done = f32[96,768]{1,0:T(8,128)} async-done(((f32[1536,768]{1,0:T(8,128)}), f32[96,768]{1,0:T(8,128)}) %reduce-scatter.8.cloned.1.call-update) | async-done | bytes 294928 | tf_op jit(solution)/shard_map/reduce_scatter | solution.py:388
  1285.6 78.9 %reduce-scatter.12.cloned.1.call-done = f32[96,768]{1,0:T(8,128)} async-done(((f32[1536,768]{1,0:T(8,128)}), f32[96,768]{1,0:T(8,128)}) %reduce-scatter.12.cloned.1.call-update) | async-done | bytes 294928 | tf_op jit(solution)/shard_map/reduce_scatter | solution.py:390
  1364.5 139.0 %reduce-scatter.20.cloned.1.call-done = f32[2048,96]{0,1:T(8,128)} async-done(((f32[2048,1536]{0,1:T(8,128)}), f32[2048,96]{0,1:T(8,128)}) %reduce-scatter.20.cloned.1.call-update) | async-done | bytes 786448 | tf_op jit(solution)/shard_map/reduce_scatter | solution.py:394
  1503.5 139.0 %reduce-scatter.16.cloned.1.call-done = f32[96,2048]{1,0:T(8,128)} async-done(((f32[1536,2048]{1,0:T(8,128)}), f32[96,2048]{1,0:T(8,128)}) %reduce-scatter.16.cloned.1.call-update) | async-done | bytes 786448 | tf_op jit(solution)/shard_map/reduce_scatter | solution.py:392
  1642.5 139.1 %reduce-scatter.18.cloned.1.call-done = f32[96,2048]{1,0:T(8,128)} async-done(((f32[1536,2048]{1,0:T(8,128)}), f32[96,2048]{1,0:T(8,128)}) %reduce-scatter.18.cloned.1.call-update) | async-done | bytes 786448 | tf_op jit(solution)/shard_map/reduce_scatter | solution.py:393
  (837 shorter events, 480.0 us)
Async XLA Ops:
  7.3 89.8 %all-gather.16.cloned.1.call-start = ((), (), s32[]{:S(2)}) async-start(), calls=%async_computation.10 | async-start | bytes 2506752 | tf_op jit(solution)/shard_map/all_gather | solution.py:136
  8.0 94.3 %all-gather.12.cloned.1.call-start = ((), (), s32[]{:S(2)}) async-start(), calls=%async_computation.8 | async-start | bytes 2506752 | tf_op jit(solution)/shard_map/all_gather | solution.py:135
  8.7 189.1 %all-reduce.10.cloned.1.call-start = ((), (), s32[]{:S(2)}) async-start(), calls=%async_computation.12 | async-start | bytes 1572864 | tf_op jit(solution)/shard_map/psum | solution.py:126
  11.0 230.5 %all-gather.10.cloned.1.call-start = ((), (), s32[]{:S(2)}) async-start(), calls=%async_computation.7 | async-start | bytes 2506752 | tf_op jit(solution)/shard_map/all_gather | solution.py:134
  11.6 276.8 %all-gather.18.cloned.1.call-start = ((), (), s32[]{:S(2)}) async-start(), calls=%async_computation.11 | async-start | bytes 3342336 | tf_op jit(solution)/shard_map/all_gather | solution.py:167
  100.1 236.7 %all-gather.14.cloned.1.call-start = ((), (), s32[]{:S(2)}) async-start(), calls=%async_computation.9 | async-start | bytes 3342336 | tf_op jit(solution)/shard_map/all_gather | solution.py:166
  106.3 273.4 %all-gather.20.cloned.1.call-start = ((), (), s32[]{:S(2)}) async-start(), calls=%async_computation.13 | async-start | bytes 2506752 | tf_op jit(solution)/shard_map/all_gather | solution.py:137
  107.0 300.7 %all-reduce.12.cloned.1.call-start = ((), (), s32[]{:S(2)}) async-start(), calls=%async_computation.14 | async-start | bytes 786432 | tf_op jit(solution)/shard_map/psum | solution.py:205
  383.1 88.8 %all-gather.22.cloned.1.call-start = ((), (), s32[]{:S(2)}) async-start(), calls=%async_computation.15 | async-start | bytes 6684672 | tf_op jit(solution)/shard_map/all_gather | solution.py:138
  383.8 150.7 %all-gather.24.cloned.1.call-start = ((), (), s32[]{:S(2)}) async-start(), calls=%async_computation.16 | async-start | bytes 6684672 | tf_op jit(solution)/shard_map/all_gather | solution.py:139
  384.4 212.9 %all-gather.26.cloned.1.call-start = ((), (), s32[]{:S(2)}) async-start(), calls=%async_computation.17 | async-start | bytes 6684672 | tf_op jit(solution)/shard_map/all_gather | solution.py:140
  385.1 242.6 %all-reduce.14.cloned.1.call-start = ((), (), s32[]{:S(2)}) async-start(), calls=%async_computation.18 | async-start | bytes 786432 | tf_op jit(solution)/shard_map/psum | solution.py:216
  603.3 67.0 %all-reduce.16.cloned.1.call-start = ((), (), s32[]{:S(2)}) async-start(), calls=%async_computation.19 | async-start | bytes 786432 | tf_op jit(solution)/shard_map/psum | solution.py:233
  644.4 404.9 %all-reduce.18.cloned.1.call-start = ((), (), s32[]{:S(2)}) async-start(), calls=%async_computation.20 | async-start | bytes 786432 | tf_op jit(solution)/shard_map/psum | solution.py:342
  685.2 19.2 %collective-permute-start = (bf16[128,768]{0,1:T(8,128)(2,1)S(1)}, bf16[128,768]{0,1:T(8,128)(2,1)}, u32[]{:S(2)}, u32[]{:S(2)}) collective-permute-start(bf16[128,768]{0,1:T(8,128)(2,1)S(1)} %copy.93), channel_id=1, source_target_pairs={{30,0},{0,2},{2,4},{4,6},{6,8},{8,10},{10,12},{12,14},{14,16},{16,... | collective-permute-start | bytes 589832 | tf_op jit(solution)/shard_map/while/body/eval_jaxpr/ppermute | solution.py:24
  686.1 18.3 %collective-permute-start.1 = (bf16[128,768]{0,1:T(8,128)(2,1)S(1)}, bf16[128,768]{0,1:T(8,128)(2,1)}, u32[]{:S(2)}, u32[]{:S(2)}) collective-permute-start(bf16[128,768]{0,1:T(8,128)(2,1)S(1)} %copy.94), channel_id=1, source_target_pairs={{30,0},{0,2},{2,4},{4,6},{6,8},{8,10},{10,12},{12,14},{14,16},{16,... | collective-permute-start | bytes 589832 | tf_op jit(solution)/shard_map/while/body/eval_jaxpr/ppermute | solution.py:24
  705.3 17.6 collective-permute-start
  1008.0 138.6 %reduce-scatter.14.cloned.1.call-start = ((), (), s32[]{:S(2)}) async-start(), calls=%async_computation.24 | async-start | bytes 5013504 | tf_op jit(solution)/shard_map/reduce_scatter | solution.py:391
  1011.0 195.3 %reduce-scatter.10.cloned.1.call-start = ((), (), s32[]{:S(2)}) async-start(), calls=%async_computation.22 | async-start | bytes 5013504 | tf_op jit(solution)/shard_map/reduce_scatter | solution.py:389
  1015.0 270.6 %reduce-scatter.8.cloned.1.call-start = ((), (), s32[]{:S(2)}) async-start(), calls=%async_computation.21 | async-start | bytes 5013504 | tf_op jit(solution)/shard_map/reduce_scatter | solution.py:388
  1018.1 346.5 %reduce-scatter.12.cloned.1.call-start = ((), (), s32[]{:S(2)}) async-start(), calls=%async_computation.23 | async-start | bytes 5013504 | tf_op jit(solution)/shard_map/reduce_scatter | solution.py:390
  1021.3 482.3 %reduce-scatter.20.cloned.1.call-start = ((), (), s32[]{:S(2)}) async-start(), calls=%async_computation.27 | async-start | bytes 13369344 | tf_op jit(solution)/shard_map/reduce_scatter | solution.py:394
  1028.9 613.6 %reduce-scatter.16.cloned.1.call-start = ((), (), s32[]{:S(2)}) async-start(), calls=%async_computation.25 | async-start | bytes 13369344 | tf_op jit(solution)/shard_map/reduce_scatter | solution.py:392
  1036.4 745.2 %reduce-scatter.18.cloned.1.call-start = ((), (), s32[]{:S(2)}) async-start(), calls=%async_computation.26 | async-start | bytes 13369344 | tf_op jit(solution)/shard_map/reduce_scatter | solution.py:393
  (194 other events, 3515.0 us)
Sparse Core Ops, SparseCore 0:
  10.4 47.3 all-gather.15
  60.0 42.2 all-gather.11
  106.3 91.5 all-reduce.9
  200.3 41.1 all-gather.9
  244.4 43.9 all-gather.17
  290.7 46.0 all-gather.13
  339.3 40.3 all-gather.19
  383.2 24.5 all-reduce.11
  410.0 61.8 all-gather.21
  474.0 60.4 all-gather.23
  536.8 60.4 all-gather.25
  603.4 24.3 all-reduce.13
  644.5 25.7 all-reduce.15
  1008.1 23.6 all-reduce.17
  1036.5 90.6 reduce-scatter.13
  1131.5 74.7 reduce-scatter.9
  1211.0 74.5 reduce-scatter.7
  1289.9 74.5 reduce-scatter.11
  1369.7 133.7 reduce-scatter.19
  1508.6 133.8 reduce-scatter.15
  1647.7 133.8 reduce-scatter.17
where the time goes:
time: 1800 us; the launch traced here: 1790 us
  waiting for transfers between devices  1200 us (67%)
  matrix products  200 us (11%)
  blocking collectives  156 us (9%)
  other arithmetic  115 us (6%)
  local copies, waits for them, and re-layouts  92.6 us (5%)
    reduce_scatter x1, waiting for transfers between devices, local(): lax.psum_scatter(grad_w_up, 'sp', scatter_dimension=0, tiled=True)  139 us
    reduce_scatter x1, waiting for transfers between devices, local(): lax.psum_scatter(grad_w_down, 'sp', scatter_dimension=1, tiled=True)  139 us
    reduce_scatter x1, waiting for transfers between devices, local(): lax.psum_scatter(grad_w_gate, 'sp', scatter_dimension=0, tiled=True)  139 us
    psum x1, waiting for transfers between devices, local(): lax.psum((mod_part, ckey_part, cval_part), 'sp')  85.8 us
    ppermute x64, waiting for transfers between devices, shifted(): return lax.ppermute(block, axis, route)  84.7 us
    dot_general x26, matrix products, bdot(): return jnp.dot(left, right, preferred_element_type=jnp.float32)  82.5 us
    reduce_scatter x1, waiting for transfers between devices, local(): lax.psum_scatter(grad_w_query, 'sp', scatter_dimension=0, tiled=True)  79.3 us
    reduce_scatter x1, waiting for transfers between devices, local(): lax.psum_scatter(grad_w_value, 'sp', scatter_dimension=0, tiled=True)  78.9 us
  transfers between devices with their start and end apart: 85, of which 50 were waited for; matrix products, arithmetic and copies ran while one was open for 18% of the time, Pallas kernels for 0%

commit v1 on v0

v1 whole, which is shorter than its diff:
```python
import math

import jax
import jax.numpy as jnp
from jax import lax
from jax.sharding import PartitionSpec as P

BANDS = 16
ITEMS = 2
BLK = 32
HEAD = 64
EPS = 1e-06
NEG = -1e30
FREQ_BASE = 10000.0
HIGH = lax.Precision.HIGHEST
BF = jnp.bfloat16
F32 = jnp.float32
SPLIT = 4


def groups_of(cycle_size):
    lanes = cycle_size // SPLIT
    along_z = [[z * lanes + g for z in range(SPLIT)] for g in range(lanes)]
    along_g = [[z * lanes + g for g in range(lanes)] for z in range(SPLIT)]
    return along_z, along_g


def normed_pair(value):
    recip = lax.rsqrt(jnp.mean(value * value, axis=-1, keepdims=True) + EPS)
    return value * recip, recip


def normed_back(grad_hat, normal, recip):
    return recip * (grad_hat - normal * jnp.mean(grad_hat * normal, axis=-1, keepdims=True))


def rotate(value, cos_row, sin_row, cos_col, sin_col):
    quarter = value.shape[-1] // 4
    part_a = value[..., :quarter]
    part_b = value[..., quarter : 2 * quarter]
    part_c = value[..., 2 * quarter : 3 * quarter]
    part_e = value[..., 3 * quarter :]
    return jnp.concatenate(
        [
            part_a * cos_row - part_b * sin_row,
            part_a * sin_row + part_b * cos_row,
            part_c * cos_col - part_e * sin_col,
            part_c * sin_col + part_e * cos_col,
        ],
        axis=-1,
    )


def angles(positions):
    quarter = HEAD // 4
    freqs = FREQ_BASE ** (-jnp.arange(quarter, dtype=F32) / quarter)
    row_angle = positions[0].astype(F32)[:, None] * freqs[None, :]
    col_angle = positions[1].astype(F32)[:, None] * freqs[None, :]
    return (
        jnp.cos(row_angle)[:, None, :],
        jnp.sin(row_angle)[:, None, :],
        jnp.cos(col_angle)[:, None, :],
        jnp.sin(col_angle)[:, None, :],
    )


def bdot(left, right):
    return jnp.dot(left, right, preferred_element_type=F32)


def dot_t(left, right):
    return lax.dot_general(left, right, (((1,), (1,)), ((), ())), preferred_element_type=F32)


def t_dot(left, right):
    return lax.dot_general(left, right, (((0,), (0,)), ((), ())), preferred_element_type=F32)


def local(
    patches,
    caption,
    band_table,
    block_item,
    item_band,
    positions,
    out_grad,
    w_query,
    w_key,
    w_value,
    w_out,
    w_gate,
    w_up,
    w_down,
    w_ckey,
    w_cvalue,
    w_ada,
    b_ada,
    g_attn_in,
    g_attn_out,
    g_ffn_in,
    g_ffn_out,
    g_query,
    g_key,
    g_ckey,
    cross_gate,
):
    scale = 1.0 / math.sqrt(HEAD)
    rank = lax.axis_index("sp")
    half = lax.axis_index("tp")
    cycle = lax.axis_size("sp")
    halves = lax.axis_size("tp")
    lanes = cycle // SPLIT
    along_z, along_g = groups_of(cycle)
    my_z, my_g = rank // lanes, rank % lanes
    tok_rows, width = patches.shape
    own_rows = tok_rows // halves
    text_count = caption.shape[0]
    blocks_dev = tok_rows // BLK
    wq, wf = w_query.shape[1] // SPLIT, w_gate.shape[1] // SPLIT
    heads = wq // HEAD
    sizes = (wq, wq, wq, wq, wf, wf, wf)
    starts = [sum(sizes[:i]) for i in range(8)]

    def gather_z(block):
        return lax.all_gather(block, "sp", axis_index_groups=along_z, axis=0, tiled=False)

    def gather_g(block):
        return lax.all_gather(block, "sp", axis_index_groups=along_g, axis=0, tiled=False)

    def scatter_z(block):
        return lax.psum_scatter(
            block, "sp", axis_index_groups=along_z, scatter_dimension=0, tiled=False
        )

    def scatter_g(block):
        return lax.psum_scatter(
            block, "sp", axis_index_groups=along_g, scatter_dimension=0, tiled=False
        )

    def turn_z(block):
        return lax.all_to_all(
            block, "sp", 0, 0, axis_index_groups=along_z, tiled=True
        )

    def sum_g(block):
        return lax.psum(block, "sp", axis_index_groups=along_g)

    def gather_tokens(own):
        both = lax.all_gather(own, "tp", axis=0, tiled=True)
        return gather_z(both).reshape(SPLIT * tok_rows, -1)

    def scatter_tokens(part):
        part = part.astype(BF).reshape(SPLIT, halves, own_rows, width)
        mine = lax.psum_scatter(part, "tp", scatter_dimension=1, tiled=False)
        return scatter_z(mine.astype(BF)).astype(F32)

    def by_z(block):
        rows, cols = block.shape
        return block.reshape(rows, SPLIT, cols // SPLIT).transpose(1, 0, 2)

    shards = jnp.concatenate(
        [by_z(m) for m in (w_query, w_key, w_value, w_out.T, w_gate, w_up, w_down.T)], axis=2
    )
    rows_dev = shards.shape[1]
    merged = gather_g(turn_z(shards)).transpose(1, 0, 2, 3).reshape(cycle * rows_dev, -1)
    f_query, f_key, f_value, f_out, f_gate, f_up, f_down = (
        merged[:, starts[i] : starts[i + 1]] for i in range(7)
    )

    items_all = block_item.reshape(SPLIT, lanes, blocks_dev)
    grp_items = jnp.repeat(
        lax.dynamic_index_in_dim(items_all, my_g, 1, keepdims=False).reshape(-1), BLK
    )
    key_items = jnp.repeat(items_all.transpose(1, 0, 2).reshape(-1), BLK)
    row0 = half * own_rows

    def own_part(block):
        return lax.dynamic_slice_in_dim(block, row0, own_rows, 0)

    own_items = own_part(
        jnp.repeat(lax.dynamic_slice_in_dim(block_item, rank * blocks_dev, blocks_dev), BLK)
    )

    band_hot = (item_band[:, None] == jnp.arange(BANDS, dtype=jnp.int32)[None, :]).astype(F32)
    cond_pre = jnp.dot(band_hot, band_table, precision=HIGH)
    cond_sig = jax.nn.sigmoid(cond_pre)
    cond_low = (cond_pre * cond_sig).astype(BF)
    text_rows = w_ckey.shape[0]
    text_local = lax.dynamic_slice_in_dim(caption, rank * text_rows, text_rows, 1)
    modulation = lax.psum(bdot(cond_low, w_ada), "sp") + b_ada
    cap_part = jnp.stack([by_z(bdot(text_local, w_ckey)), by_z(bdot(text_local, w_cvalue))], 1)
    cap_raw = sum_g(scatter_z(cap_part))
    ckey_hat, ckey_recip = normed_pair(cap_raw[0].reshape(text_count, heads, HEAD))

    def per_head(vector):
        return lax.dynamic_slice_in_dim(vector, my_z * wq, wq, 0).reshape(heads, HEAD)

    gain_query, gain_key, gain_ckey = per_head(g_query), per_head(g_key), per_head(g_ckey)
    gate_tanh = jnp.tanh(lax.dynamic_slice_in_dim(cross_gate, my_z * heads, heads, 0))
    cap_keys = (ckey_hat * gain_ckey).astype(BF)
    cap_values = cap_raw[1].astype(BF).reshape(text_count, heads, HEAD)

    def of_items(rows, items):
        return jnp.where(items[:, None] == 0, rows[0], rows[1])

    mod_own = of_items(modulation, own_items)
    scale_attn, gate_attn, scale_ffn, gate_ffn = (
        mod_own[:, i * width : (i + 1) * width] for i in range(4)
    )
    group_rows = SPLIT * tok_rows

    patch_f = own_part(patches).astype(F32)
    grad_out = own_part(out_grad).astype(F32)
    hat_one, recip_one = normed_pair(patch_f)
    factor_one = g_attn_in * (1.0 + scale_attn)
    norm_in = gather_tokens((hat_one * factor_one).astype(BF))
    pos_all = gather_z(positions).transpose(1, 0, 2).reshape(2, group_rows)
    cos_row, sin_row, cos_col, sin_col = angles(pos_all)
    split_heads = (group_rows, heads, HEAD)
    query_raw = bdot(norm_in, f_query).reshape(split_heads)
    key_raw = bdot(norm_in, f_key).reshape(split_heads)
    values_low = bdot(norm_in, f_value).astype(BF)
    query_hat, query_recip = normed_pair(query_raw)
    queries = rotate(query_hat * gain_query, cos_row, sin_row, cos_col, sin_col).astype(BF)
    key_hat, key_recip = normed_pair(key_raw)
    keys_low = rotate(key_hat * gain_key, cos_row, sin_row, cos_col, sin_col).astype(BF)
    all_keys, all_values = (
        gather_g(block).reshape(lanes * group_rows, heads, HEAD)
        for block in (keys_low.reshape(group_rows, wq), values_low)
    )
    same = (grp_items[:, None] == key_items[None, :])[None]
    scores = jnp.einsum("qhd,khd->hqk", queries, all_keys, preferred_element_type=F32) * scale
    scores = jnp.where(same, scores, NEG)
    exps = jnp.exp(scores - jnp.max(scores, axis=-1, keepdims=True))
    probs = exps / jnp.sum(exps, axis=-1, keepdims=True)
    probs_low = probs.astype(BF)
    attn_self = jnp.einsum("hqk,khd->qhd", probs_low, all_values, preferred_element_type=F32)
    cross_scores = (
        jnp.einsum("qhd,khd->hqk", queries, cap_keys, preferred_element_type=F32) * scale
    )
    cross_exp = jnp.exp(cross_scores - jnp.max(cross_scores, axis=-1, keepdims=True))
    cross_probs = cross_exp / jnp.sum(cross_exp, axis=-1, keepdims=True)
    cross_low = cross_probs.astype(BF)
    attn_cross = jnp.einsum("hqk,khd->qhd", cross_low, cap_values, preferred_element_type=F32)
    mixed = (attn_self + gate_tanh[None, :, None] * attn_cross).astype(BF).reshape(group_rows, wq)
    attn_branch = scatter_tokens(dot_t(mixed, f_out))

    hat_two, recip_two = normed_pair(attn_branch)
    tanh_one = jnp.tanh(gate_attn)
    resid = patch_f + tanh_one * hat_two * g_attn_out
    hat_three, recip_three = normed_pair(resid)
    factor_three = g_ffn_in * (1.0 + scale_ffn)
    norm_ffn = gather_tokens((hat_three * factor_three).astype(BF))
    gate_val = bdot(norm_ffn, f_gate)
    up_val = bdot(norm_ffn, f_up)
    gate_sig = jax.nn.sigmoid(gate_val)
    hidden = (gate_val * gate_sig * up_val).astype(BF)
    ffn_branch = scatter_tokens(dot_t(hidden, f_down))
    hat_four, recip_four = normed_pair(ffn_branch)
    tanh_two = jnp.tanh(gate_ffn)
    output = resid + tanh_two * hat_four * g_ffn_out

    grad_gate_ffn = grad_out * hat_four * g_ffn_out * (1.0 - tanh_two * tanh_two)
    grad_four = grad_out * tanh_two
    grad_g_ffn_out = jnp.sum(grad_four * hat_four, axis=0)
    grad_ffn = gather_tokens(
        normed_back(grad_four * g_ffn_out, hat_four, recip_four).astype(BF)
    )
    grad_hidden = bdot(grad_ffn, f_down)
    grad_gate = (grad_hidden * up_val * gate_sig * (1.0 + gate_val * (1.0 - gate_sig))).astype(BF)
    grad_up = (grad_hidden * gate_val * gate_sig).astype(BF)
    grad_norm_ffn = scatter_tokens(dot_t(grad_gate, f_gate) + dot_t(grad_up, f_up))
    grad_scale_ffn = grad_norm_ffn * hat_three * g_ffn_in
    grad_g_ffn_in = jnp.sum(grad_norm_ffn * hat_three * (1.0 + scale_ffn), axis=0)
    grad_resid = grad_out + normed_back(grad_norm_ffn * factor_three, hat_three, recip_three)

    grad_gate_attn = grad_resid * hat_two * g_attn_out * (1.0 - tanh_one * tanh_one)
    grad_two = grad_resid * tanh_one
    grad_g_attn_out = jnp.sum(grad_two * hat_two, axis=0)
    grad_attn = gather_tokens(normed_back(grad_two * g_attn_out, hat_two, recip_two).astype(BF))
    grad_mixed = bdot(grad_attn, f_out).astype(BF).reshape(split_heads)
    grad_mixed_f = grad_mixed.astype(F32)
    grad_cross_gate = jnp.sum(grad_mixed_f * attn_cross, axis=(0, 2)) * (
        1.0 - gate_tanh * gate_tanh
    )
    grad_cross = (gate_tanh[None, :, None] * grad_mixed_f).astype(BF)
    grad_cprobs = jnp.einsum("qhd,khd->hqk", grad_cross, cap_values, preferred_element_type=F32)
    grad_cscores = (
        cross_probs * (grad_cprobs - jnp.sum(cross_probs * grad_cprobs, axis=-1, keepdims=True))
    ).astype(BF)
    query_grad = jnp.einsum("hqk,khd->qhd", grad_cscores, cap_keys, preferred_element_type=F32)
    grad_ckeys_part = (
        jnp.einsum("hqk,qhd->khd", grad_cscores, queries, preferred_element_type=F32) * scale
    )
    grad_cvals_part = jnp.einsum(
        "hqk,qhd->khd", cross_low, grad_cross, preferred_element_type=F32
    )
    row_delta = jnp.sum(grad_mixed_f * attn_self, axis=-1).T
    grad_probs = jnp.einsum("qhd,khd->hqk", grad_mixed, all_values, preferred_element_type=F32)
    grad_scores = (probs * (grad_probs - row_delta[..., None])).astype(BF)
    query_grad = query_grad + jnp.einsum(
        "hqk,khd->qhd", grad_scores, all_keys, preferred_element_type=F32
    )
    key_part = (
        jnp.einsum("hqk,qhd->khd", grad_scores, queries, preferred_element_type=F32) * scale
    )
    value_part = jnp.einsum("hqk,qhd->khd", probs_low, grad_mixed, preferred_element_type=F32)
    key_grad, value_grad = (
        scatter_g(block.astype(BF).reshape(lanes, group_rows, wq)) for block in (key_part, value_part)
    )
    grad_queries = (query_grad * scale).astype(BF).astype(F32)
    grad_qnorm = rotate(grad_queries, cos_row, -sin_row, cos_col, -sin_col)
    grad_g_query = jnp.sum(grad_qnorm * query_hat, axis=0).reshape(-1)
    grad_query_raw = (
        normed_back(grad_qnorm * gain_query, query_hat, query_recip).astype(BF).reshape(-1, wq)
    )
    grad_keys = key_grad.astype(F32).reshape(split_heads)
    grad_knorm = rotate(grad_keys, cos_row, -sin_row, cos_col, -sin_col)
    grad_g_key = jnp.sum(grad_knorm * key_hat, axis=0).reshape(-1)
    grad_key_raw = (
        normed_back(grad_knorm * gain_key, key_hat, key_recip).astype(BF).reshape(-1, wq)
    )
    grad_values = value_grad.astype(BF)
    grad_norm_in = scatter_tokens(
        dot_t(grad_query_raw, f_query) + dot_t(grad_key_raw, f_key) + dot_t(grad_values, f_value)
    )
    grad_scale_attn = grad_norm_in * hat_one * g_attn_in
    grad_g_attn_in = jnp.sum(grad_norm_in * hat_one * (1.0 + scale_attn), axis=0)
    grad_patches = grad_resid + normed_back(grad_norm_in * factor_one, hat_one, recip_one)

    grad_merged = jnp.concatenate(
        [
            t_dot(norm_in, grad_query_raw),
            t_dot(norm_in, grad_key_raw),
            t_dot(norm_in, grad_values),
            t_dot(grad_attn, mixed),
            t_dot(norm_ffn, grad_gate),
            t_dot(norm_ffn, grad_up),
            t_dot(grad_ffn, hidden),
        ],
        axis=1,
    ).astype(BF)
    grad_merged = grad_merged.reshape(SPLIT, lanes, rows_dev, -1).transpose(1, 0, 2, 3)
    shard_grads = turn_z(scatter_g(grad_merged)).astype(F32)
    (shard_query, shard_key, shard_value, shard_out, shard_gate, shard_up, shard_down) = (
        shard_grads[:, :, starts[i] : starts[i + 1]].transpose(1, 0, 2).reshape(rows_dev, -1)
        for i in range(7)
    )

    token_sums = lax.psum(
        (
            jnp.stack(
                [
                    jnp.concatenate(
                        [
                            jnp.sum(
                                jnp.where((own_items == item)[:, None], block, 0.0), axis=0
                            )
                            for block in (
                                grad_scale_attn,
                                grad_gate_attn,
                                grad_scale_ffn,
                                grad_gate_ffn,
                            )
                        ]
                    )
                    for item in range(ITEMS)
                ]
            ),
            grad_g_attn_in,
            grad_g_attn_out,
            grad_g_ffn_in,
            grad_g_ffn_out,
        ),
        ("sp", "tp"),
    )
    head_sums = jnp.concatenate([grad_g_query, grad_g_key, grad_cross_gate])
    head_sums = gather_z(sum_g(head_sums))
    grad_ckeys = sum_g(grad_ckeys_part).astype(BF).astype(F32)
    grad_cvals = sum_g(grad_cvals_part).astype(BF).reshape(text_count, wq)
    grad_g_ckey = gather_z(jnp.sum(grad_ckeys * ckey_hat, axis=0).reshape(-1)).reshape(-1)
    grad_ckey_raw = (
        normed_back(grad_ckeys * gain_ckey, ckey_hat, ckey_recip).astype(BF).reshape(text_count, wq)
    )
    cap_grads = gather_z(jnp.stack([grad_ckey_raw, grad_cvals])).transpose(1, 2, 0, 3)
    cap_grads = cap_grads.reshape(2, text_count, SPLIT * wq)
    grad_mod = token_sums[0]
    grad_b_ada = jnp.sum(grad_mod, axis=0)
    grad_w_ada = jnp.dot(cond_low.astype(F32).T, grad_mod, precision=HIGH)
    grad_cond_act = jnp.dot(grad_mod, w_ada.astype(F32).T, precision=HIGH)
    grad_cond_pre = grad_cond_act * cond_sig * (1.0 + cond_pre * (1.0 - cond_sig))
    grad_band_table = jnp.dot(band_hot.T, grad_cond_pre, precision=HIGH)
    return (
        lax.all_gather(output, "tp", axis=0, tiled=True),
        lax.all_gather(grad_patches, "tp", axis=0, tiled=True),
        shard_query,
        shard_key,
        shard_value,
        shard_out.T,
        shard_gate,
        shard_up,
        shard_down.T,
        t_dot(text_local, cap_grads[0]),
        t_dot(text_local, cap_grads[1]),
        grad_w_ada,
        grad_b_ada,
        token_sums[1],
        token_sums[2],
        token_sums[3],
        token_sums[4],
        head_sums[:, :wq].reshape(-1),
        head_sums[:, wq : 2 * wq].reshape(-1),
        grad_g_ckey,
        head_sums[:, 2 * wq :].reshape(-1),
        grad_band_table,
    )


def solution(mesh):
    in_specs = (
        P("sp", None),
        P(),
        P(None, "sp"),
        P(),
        P(),
        P(None, "sp"),
        P("sp", None),
        P("sp", "tp"),
        P("sp", "tp"),
        P("sp", "tp"),
        P("tp", "sp"),
        P("sp", "tp"),
        P("sp", "tp"),
        P("tp", "sp"),
        P("sp", "tp"),
        P("sp", "tp"),
        P("sp", None),
        P(),
        P(),
        P(),
        P(),
        P(),
        P("tp"),
        P("tp"),
        P("tp"),
        P("tp"),
    )
    out_specs = (
        P("sp", None),
        P("sp", None),
        P("sp", "tp"),
        P("sp", "tp"),
        P("sp", "tp"),
        P("tp", "sp"),
        P("sp", "tp"),
        P("sp", "tp"),
        P("tp", "sp"),
        P("sp", "tp"),
        P("sp", "tp"),
        P("sp", None),
        P(),
        P(),
        P(),
        P(),
        P(),
        P("tp"),
        P("tp"),
        P("tp"),
        P("tp"),
        P(None, "sp"),
    )
    return jax.shard_map(local, mesh=mesh, in_specs=in_specs, out_specs=out_specs, check_vma=False)
```

time: 1800 us -> 1140 us (0.63)
  waiting for transfers between devices: 1200 us -> 638 us
  matrix products: 200 us -> 106 us
  other arithmetic: 115 us -> 42.8 us
  blocking collectives: 156 us -> 195 us
  local copies, waits for them, and re-layouts: 92.6 us -> 115 us
    reduce_scatter x7 -> x10, waiting for transfers between devices: 635 us -> 211 us  [the longest x4 108 us: scatter_z(): lax.psum_scatter(block, 'sp', axis_index_groups=along_z, scatter_dimensio...]
    all_gather x9 -> x5, waiting for transfers between devices: 327 us -> 139 us  [the longest x4 139 us: gather_z(): lax.all_gather(block, 'sp', axis_index_groups=along_z, axis=0, tiled=False)]
    unnamed x21, waiting for transfers between devices: 4.72 us -> 157 us
    all_gather x0 -> x12, blocking collectives: none -> 113 us  [the longest x4 45.7 us: gather_z(): lax.all_gather(block, 'sp', axis_index_groups=along_z, axis=0, tiled=False)]
    dot_general x112 -> x33, matrix products: 184 us -> 87 us  [the longest x10 20.3 us: bdot(): return jnp.dot(left, right, preferred_element_type=F32)]
    ppermute x64 -> x0, waiting for transfers between devices: 84.7 us -> none  [shifted(): return lax.ppermute(block, axis, route)]
    psum x2, blocking collectives: 156 us -> 82 us  [the longest x1 60.1 us: local(): modulation = lax.psum(bdot(cond_low, w_ada), 'sp') + b_ada]
    convert_element_type x71 -> x10, other arithmetic: 70 us -> 13.7 us  [the longest x1 9.09 us: local(): probs_low = probs.astype(BF)]
  transfers between devices with their start and end apart: 85 -> 21, of which waited for: 50 -> 16; matrix products, arithmetic and copies ran while one was open for 18% -> 9% of each run, Pallas kernels for 0% -> 0%
where the time goes in v1:
time: 1140 us; the launch traced here: 1120 us
  waiting for transfers between devices  638 us (56%)
  blocking collectives  195 us (17%)
  local copies, waits for them, and re-layouts  115 us (10%)
  matrix products  106 us (9%)
  other arithmetic  42.8 us (4%)
  between operations  15.9 us (1%)
  starting transfers between devices  12.3 us (1%)
    unnamed x21, waiting for transfers between devices  157 us
    all_gather x4, waiting for transfers between devices, gather_z(): lax.all_gather(block, 'sp', axis_index_groups=along_z, axis=0, tiled=False)  139 us
    psum x1, waiting for transfers between devices, local(): lax.psum((jnp.stack([jnp.concatenate([jnp.sum(jnp.where((own_items == ite...  130 us
    reduce_scatter x4, waiting for transfers between devices, scatter_z(): lax.psum_scatter(block, 'sp', axis_index_groups=along_z, scatter_dimensio...  108 us
    reduce_scatter x4, waiting for transfers between devices, scatter_tokens(): mine = lax.psum_scatter(part, 'tp', scatter_dimension=1, tiled=False)  75 us
    psum x1, blocking collectives, local(): modulation = lax.psum(bdot(cond_low, w_ada), 'sp') + b_ada  60.1 us
    all_gather x4, blocking collectives, gather_z(): lax.all_gather(block, 'sp', axis_index_groups=along_z, axis=0, tiled=False)  45.7 us
    reduce_scatter x2, waiting for transfers between devices, scatter_g(): lax.psum_scatter(block, 'sp', axis_index_groups=along_g, scatter_dimensio...  28.5 us
  transfers between devices with their start and end apart: 21, of which 16 were waited for; matrix products, arithmetic and copies ran while one was open for 9% of the time, Pallas kernels for 0%

profile of v1, /device:TPU:0, one launch (start us, length us, event | category | flops | bytes accessed | tf_op | source)
XLA Modules:
  0.0 1124.4 jit_solution(80931945887404401)
XLA Ops:
  35.9 99.3 %all-reduce.12.cloned.1.call-done = f32[4,2,256,192]{2,3,0,1:T(8,128)} async-done(((f32[4,2,256,192]{2,3,0,1:T(8,128)}), f32[4,2,256,192]{2,3,0,1:T(8,128)}) %all-reduce.12.cloned.1.call-update) | async-done | bytes 1572880
  139.9 60.1 %psum.70 = f32[2,6144]{1,0:T(2,128)S(1)} all-reduce(f32[2,6144]{1,0:T(2,128)S(1)} %fusion.124), channel_id=1, replica_groups=mesh['sp'=16,'tp'=2] {'sp'}, use_global_device_ids=true, to_apply=%region_0.1 | all-reduce | flops 12288 | bytes 98304 | tf_op jit(solution)/shard_map/psum | solution.py:190
  233.4 27.9 %all-gather.17.cloned.1.call-done = bf16[512,1536]{1,0:T(8,128)(2,1)} async-done(((bf16[128,1536]{1,0:T(8,128)(2,1)}), bf16[512,1536]{1,0:T(8,128)(2,1)}) %all-gather.17.cloned.1.call-update) | async-done | bytes 1572880 | tf_op jit(solution)/shard_map/all_gather | solution.py:125
  281.6 9.6 all-gather.2
  322.1 24.9 %reduce-scatter.17.cloned.1.call-done = bf16[4,1,64,1536]{3,2,0,1:T(8,128)(2,1)} async-done(((bf16[4,2,64,1536]{3,2,0,1:T(8,128)(2,1)}), bf16[4,1,64,1536]{3,2,0,1:T(8,128)(2,1)}) %reduce-scatter.17.cloned.1.call-update) | async-done | bytes 786448 | tf_op jit(solution)/shard_map/reduce_scatter | solution.py:154
  347.1 25.4 %reduce-scatter.19.cloned.1.call-done = bf16[1,64,1536]{2,1,0:T(8,128)(2,1)} async-done(((bf16[4,64,1536]{2,1,0:T(8,128)(2,1)}), bf16[1,64,1536]{2,1,0:T(8,128)(2,1)}) %reduce-scatter.19.cloned.1.call-update) | async-done | bytes 196624 | tf_op jit(solution)/shard_map/reduce_scatter | solution.py:131
  382.7 37.1 %all-gather.21.cloned.1.call-done = bf16[512,1536]{1,0:T(8,128)(2,1)} async-done(((bf16[128,1536]{1,0:T(8,128)(2,1)}), bf16[512,1536]{1,0:T(8,128)(2,1)}) %all-gather.21.cloned.1.call-update) | async-done | bytes 1572880 | tf_op jit(solution)/shard_map/all_gather | solution.py:125
  430.6 25.0 %reduce-scatter.21.cloned.1.call-done = bf16[4,1,64,1536]{3,2,0,1:T(8,128)(2,1)} async-done(((bf16[4,2,64,1536]{3,2,0,1:T(8,128)(2,1)}), bf16[4,1,64,1536]{3,2,0,1:T(8,128)(2,1)}) %reduce-scatter.21.cloned.1.call-update) | async-done | bytes 786448 | tf_op jit(solution)/shard_map/reduce_scatter | solution.py:154
  455.7 25.7 %reduce-scatter.23.cloned.1.call-done = bf16[1,64,1536]{2,1,0:T(8,128)(2,1)} async-done(((bf16[4,64,1536]{2,1,0:T(8,128)(2,1)}), bf16[1,64,1536]{2,1,0:T(8,128)(2,1)}) %reduce-scatter.23.cloned.1.call-update) | async-done | bytes 196624 | tf_op jit(solution)/shard_map/reduce_scatter | solution.py:131
  493.1 37.0 %all-gather.23.cloned.1.call-done = bf16[512,1536]{1,0:T(8,128)(2,1)} async-done(((bf16[128,1536]{1,0:T(8,128)(2,1)}), bf16[512,1536]{1,0:T(8,128)(2,1)}) %all-gather.23.cloned.1.call-update) | async-done | bytes 1572880 | tf_op jit(solution)/shard_map/all_gather | solution.py:125
  540.5 25.0 %reduce-scatter.25.cloned.1.call-done = bf16[4,1,64,1536]{3,2,0,1:T(8,128)(2,1)} async-done(((bf16[4,2,64,1536]{3,2,0,1:T(8,128)(2,1)}), bf16[4,1,64,1536]{3,2,0,1:T(8,128)(2,1)}) %reduce-scatter.25.cloned.1.call-update) | async-done | bytes 786448 | tf_op jit(solution)/shard_map/reduce_scatter | solution.py:154
  565.6 25.4 %reduce-scatter.27.cloned.1.call-done = bf16[1,64,1536]{2,1,0:T(8,128)(2,1)} async-done(((bf16[4,64,1536]{2,1,0:T(8,128)(2,1)}), bf16[1,64,1536]{2,1,0:T(8,128)(2,1)}) %reduce-scatter.27.cloned.1.call-update) | async-done | bytes 196624 | tf_op jit(solution)/shard_map/reduce_scatter | solution.py:131
  603.3 37.1 %all-gather.25.cloned.1.call-done = bf16[512,1536]{1,0:T(8,128)(2,1)} async-done(((bf16[128,1536]{1,0:T(8,128)(2,1)}), bf16[512,1536]{1,0:T(8,128)(2,1)}) %all-gather.25.cloned.1.call-update) | async-done | bytes 1572880 | tf_op jit(solution)/shard_map/all_gather | solution.py:125
  701.4 20.6 %reduce-scatter.31.cloned.1.call-done = bf16[1,512,192]{1,2,0:T(8,128)(2,1)} async-done(((bf16[4,512,192]{1,2,0:T(8,128)(2,1)}), bf16[1,512,192]{1,2,0:T(8,128)(2,1)}) %reduce-scatter.31.cloned.1.call-update) | async-done | bytes 196624 | tf_op jit(solution)/shard_map/reduce_scatter | solution.py:136
  752.5 11.8 %concatenate.36 = bf16[4,4,96,2304]{3,2,1,0:T(8,128)(2,1)} concatenate(bf16[4,4,96,192]{3,2,1,0:T(8,128)(2,1)} %convolution_convert_fusion.9, bf16[4,4,96,192]{3,2,1,0:T(8,128)(2,1)} %convolution_convert_fusion.8, bf16[4,4,96,192]{3,2,1,0:T(8,128)(2,1)} %convolution_convert_fusion.7, bf16[4,4,96,192]{3,2,1,0:T(8,128)(2,1)} %convolution_convert_fusion.6, ...), dimensions={3} | concatenate | bytes 14155776 | tf_op jit(solution)/shard_map/concatenate | solution.py:331
  765.5 11.3 %all_gather.91 = f32[128,1536]{1,0:T(8,128)} all-gather(f32[64,1536]{1,0:T(8,128)S(1)} %copy-done.31), channel_id=1, replica_groups=mesh['sp'=16,'tp'=2] {'tp'}, dimensions={0}, use_global_device_ids=true | all-gather | bytes 1179648 | tf_op jit(solution)/shard_map/all_gather | solution.py:394
  780.5 21.8 %all-reduce.17 = (bf16[256,3,64]{0,2,1:T(8,128)(2,1)S(1)}, bf16[256,3,64]{0,2,1:T(8,128)(2,1)S(1)}, f32[1,387]{1,0:T(1,128)S(1)}) all-reduce(f32[256,3,64]{0,2,1:T(8,128)S(1)} %convolution_bitcast_fusion.2, f32[256,3,64]{0,2,1:T(8,128)S(1)} %fusion.34, ...), channel_id=1, replica_groups={{0,2,4,6},{8,10,12,14},{16,18,20,22},{24,26,28,30},{1,3,5,7},{9,11,13,1..., use_global_device_ids=true, to_apply=%region_35.36 | all-reduce | flops 98691 | bytes 592920 | tf_op jit(solution)/shard_map/psum | solution.py:146
  802.4 11.9 %all-gather.9 = f32[4,1,387]{2,1,0:T(1,128)S(1)} all-gather(f32[1,1,387]{2,1,0:T(1,128)S(1)} %bitcast.360), channel_id=1, replica_groups={{0,8,16,24},{2,10,18,26},{4,12,20,28},{6,14,22,30},{1,9,17,25},{3,11,19..., dimensions={0}, use_global_device_ids=true | all-gather | bytes 7740 | tf_op jit(solution)/shard_map/all_gather | solution.py:125
  816.1 9.6 all-gather.10
  827.0 16.7 %all-gather.7 = bf16[8,256,192]{1,2,0:T(8,128)(2,1)S(1)} all-gather(bf16[2,256,192]{1,2,0:T(8,128)(2,1)S(1)} %pad_maximum_fusion.5), channel_id=9, replica_groups={{0,8,16,24},{2,10,18,26},{4,12,20,28},{6,14,22,30},{1,9,17,25},{3,11,19..., dimensions={0}, use_global_device_ids=true | all-gather | bytes 983040 | tf_op jit(solution)/shard_map/all_gather | solution.py:125
  846.1 57.1 %all-reduce.14.cloned.1.call-done = bf16[4,4,96,2304]{3,2,0,1:T(8,128)(2,1)} async-done(((bf16[4,4,96,2304]{3,2,0,1:T(8,128)(2,1)}), bf16[4,4,96,2304]{3,2,0,1:T(8,128)(2,1)}) %all-reduce.14.cloned.1.call-update) | async-done | bytes 7077904
  911.5 31.2 %reduce-scatter.35.cloned.1.call-done = bf16[1,64,1536]{2,1,0:T(8,128)(2,1)} async-done(((bf16[4,64,1536]{2,1,0:T(8,128)(2,1)}), bf16[1,64,1536]{2,1,0:T(8,128)(2,1)}) %reduce-scatter.35.cloned.1.call-update) | async-done | bytes 196624 | tf_op jit(solution)/shard_map/reduce_scatter | solution.py:131
  947.0 11.8 %all_gather.98 = f32[128,1536]{1,0:T(8,128)} all-gather(f32[64,1536]{1,0:T(8,128)S(1)} %fusion.80), channel_id=1, replica_groups=mesh['sp'=16,'tp'=2] {'tp'}, dimensions={0}, use_global_device_ids=true | all-gather | bytes 1179648 | tf_op jit(solution)/shard_map/all_gather | solution.py:395
  958.8 129.9 %all-reduce.16.cloned.1.call-done = (f32[2,6144]{1,0:T(2,128)}, f32[1536]{0:T(1024)}, f32[1536]{0:T(1024)}, f32[1536]{0:T(1024)}, f32[1536]{0:T(1024)}) async-done(((f32[2,6144]{1,0:T(2,128)}, f32[1536]{0:T(1024)}, f32[1536]{0:T(1024)}, f32[1536]{0:T(1024)}, f32[1536]{0:T(1024)}), (f32[2,6144]{1,0:T(2,128)}, f32[1536]{0:T(1024)}, f32[1536]{0:T(1024)}, f32[1536]{0:T(1024)}, ...) | async-done | bytes 73744 | tf_op jit(solution)/shard_map/psum | solution.py:350
  (485 shorter events, 315.1 us)
Async XLA Ops:
  26.2 111.6 %all-to-all-start = ((bf16[4,96,2304]{2,1,0:T(8,128)(2,1)}), bf16[4,96,2304]{2,1,0:T(8,128)(2,1)}, u32[]{:S(2)}, u32[]{:S(2)}) async-start(bf16[4,96,2304]{2,1,0:T(8,128)(2,1)} %copy.179), calls=%async_computation | async-start | bytes 3538944 | tf_op jit(solution)/shard_map/all_to_all | solution.py:141
  32.6 102.5 %all-reduce.12.cloned.1.call-start = ((), (), s32[]{:S(2)}) async-start(), calls=%async_computation.28 | async-start | bytes 3145728
  34.7 104.1 %copy-start.19 = (bf16[128,1536]{1,0:T(8,128)(2,1)S(1)}, bf16[128,1536]{1,0:T(8,128)(2,1)}, u32[]{:S(2)}) copy-start(bf16[128,1536]{1,0:T(8,128)(2,1)} %param.26) | copy-start | bytes 1179652
  34.7 187.5 %all-reduce.10.cloned.1.call-start = ((), (), s32[]{:S(2)}) async-start(), calls=%async_computation.12 | async-start | bytes 786432 | tf_op jit(solution)/shard_map/psum | solution.py:146
  137.7 87.1 %all-gather.19.cloned.1.call-start = ((), (), s32[]{:S(2)}) async-start(), calls=%async_computation.24 | async-start | bytes 8847360 | tf_op jit(solution)/shard_map/all_gather | solution.py:128
  138.5 122.8 %all-gather.17.cloned.1.call-start = ((), (), s32[]{:S(2)}) async-start(), calls=%async_computation.23 | async-start | bytes 1966080 | tf_op jit(solution)/shard_map/all_gather | solution.py:125
  208.7 138.3 %reduce-scatter.17.cloned.1.call-start = ((), (), s32[]{:S(2)}) async-start(), calls=%async_computation.13 | async-start | bytes 2359296 | tf_op jit(solution)/shard_map/reduce_scatter | solution.py:154
  322.1 50.4 %reduce-scatter.19.cloned.1.call-start = ((), (), s32[]{:S(2)}) async-start(), calls=%async_computation.14 | async-start | bytes 983040 | tf_op jit(solution)/shard_map/reduce_scatter | solution.py:131
  347.0 72.8 %all-gather.21.cloned.1.call-start = ((), (), s32[]{:S(2)}) async-start(), calls=%async_computation.25 | async-start | bytes 1966080 | tf_op jit(solution)/shard_map/all_gather | solution.py:125
  382.6 73.0 %reduce-scatter.21.cloned.1.call-start = ((), (), s32[]{:S(2)}) async-start(), calls=%async_computation.15 | async-start | bytes 2359296 | tf_op jit(solution)/shard_map/reduce_scatter | solution.py:154
  430.6 50.9 %reduce-scatter.23.cloned.1.call-start = ((), (), s32[]{:S(2)}) async-start(), calls=%async_computation.16 | async-start | bytes 983040 | tf_op jit(solution)/shard_map/reduce_scatter | solution.py:131
  455.7 74.4 %all-gather.23.cloned.1.call-start = ((), (), s32[]{:S(2)}) async-start(), calls=%async_computation.26 | async-start | bytes 1966080 | tf_op jit(solution)/shard_map/all_gather | solution.py:125
  492.9 72.6 %reduce-scatter.25.cloned.1.call-start = ((), (), s32[]{:S(2)}) async-start(), calls=%async_computation.17 | async-start | bytes 2359296 | tf_op jit(solution)/shard_map/reduce_scatter | solution.py:154
  540.4 50.6 %reduce-scatter.27.cloned.1.call-start = ((), (), s32[]{:S(2)}) async-start(), calls=%async_computation.18 | async-start | bytes 983040 | tf_op jit(solution)/shard_map/reduce_scatter | solution.py:131
  565.6 74.9 %all-gather.25.cloned.1.call-start = ((), (), s32[]{:S(2)}) async-start(), calls=%async_computation.27 | async-start | bytes 1966080 | tf_op jit(solution)/shard_map/all_gather | solution.py:125
  603.3 92.3 %reduce-scatter.29.cloned.1.call-start = ((), (), s32[]{:S(2)}) async-start(), calls=%async_computation.19 | async-start | bytes 983040 | tf_op jit(solution)/shard_map/reduce_scatter | solution.py:136
  673.3 48.7 %reduce-scatter.31.cloned.1.call-start = ((), (), s32[]{:S(2)}) async-start(), calls=%async_computation.20 | async-start | bytes 983040 | tf_op jit(solution)/shard_map/reduce_scatter | solution.py:136
  684.1 130.5 %reduce-scatter.33.cloned.1.call-start = ((), (), s32[]{:S(2)}) async-start(), calls=%async_computation.21 | async-start | bytes 2359296 | tf_op jit(solution)/shard_map/reduce_scatter | solution.py:154
  726.1 177.1 %all-reduce.14.cloned.1.call-start = ((), (), s32[]{:S(2)}) async-start(), calls=%async_computation.29 | async-start | bytes 14155776
  764.4 178.3 %reduce-scatter.35.cloned.1.call-start = ((), (), s32[]{:S(2)}) async-start(), calls=%async_computation.22 | async-start | bytes 983040 | tf_op jit(solution)/shard_map/reduce_scatter | solution.py:131
  906.8 189.0 %all-to-all-start.1 = ((bf16[4,96,2304]{2,1,0:T(8,128)(2,1)}), bf16[4,96,2304]{2,1,0:T(8,128)(2,1)}, u32[]{:S(2)}, u32[]{:S(2)}) async-start(bf16[4,96,2304]{2,1,0:T(8,128)(2,1)} %dynamic-slice_bitcast_fusion), calls=%async_computation.11 | async-start | bytes 3538944 | tf_op jit(solution)/shard_map/all_to_all | solution.py:141
  911.5 177.2 %all-reduce.16.cloned.1.call-start = ((), (), s32[]{:S(2)}) async-start(), calls=%async_computation.30 | async-start | bytes 163840 | tf_op jit(solution)/shard_map/psum | solution.py:350
  945.1 145.1 %copy-start.106 = (f32[2,64]{1,0:T(2,128)S(1)}, f32[2,64]{1,0:T(2,128)}, u32[]{:S(2)}) copy-start(f32[2,64]{1,0:T(2,128)} %copy-done.105) | copy-start | bytes 1540
  945.8 146.3 %copy-start.117 = (s32[2]{0:T(128)S(1)}, s32[2]{0:T(128)}, u32[]{:S(2)}) copy-start(s32[2]{0:T(128)} %param.30) | copy-start | bytes 28
  (120 other events, 2192.3 us)
Sparse Core Ops, SparseCore 0:
  36.4 98.7 all-reduce.11
  138.1 31.6 all-reduce.9
  171.5 51.1 all-gather.18
  224.2 37.0 all-gather.16
  322.2 24.7 reduce-scatter.16
  349.2 23.2 reduce-scatter.18
  382.7 37.0 all-gather.20
  430.7 24.9 reduce-scatter.20
  458.1 23.3 reduce-scatter.22
  493.0 37.0 all-gather.22
  540.6 24.9 reduce-scatter.24
  567.7 23.3 reduce-scatter.26
  603.4 36.9 all-gather.24
  673.4 22.1 reduce-scatter.28
  698.7 23.2 reduce-scatter.30
  726.3 26.0 reduce-scatter.32
  764.4 138.7 all-reduce.13
  905.5 37.1 reduce-scatter.34
  951.9 136.7 all-reduce.15

commit v2 on v1

--- a/solution.py
+++ b/solution.py
@@ -3,6 +3,8 @@
 import jax
 import jax.numpy as jnp
 from jax import lax
+from jax.experimental import pallas as pl
+from jax.experimental.pallas import tpu as pltpu
 from jax.sharding import PartitionSpec as P
 
 BANDS = 16
@@ -74,6 +76,1125 @@
 
 def t_dot(left, right):
     return lax.dot_general(left, right, (((0,), (0,)), ((), ())), preferred_element_type=F32)
+
+
+MESH = pl.DeviceIdType.MESH
+VMEM_LIMIT = 60 * 2**20
+
+
+class Place:
+    def __init__(self):
+        rank = lax.axis_index("sp")
+        self.lanes = lax.axis_size("sp") // SPLIT
+        self.x = lax.axis_index("tp")
+        self.z = rank // self.lanes
+        self.g = rank % self.lanes
+        self.x_peer = (rank, 1 - self.x)
+        self.z_peer = {
+            d: (lax.rem(self.z + d, SPLIT) * self.lanes + self.g, self.x) for d in (1, 2, 3)
+        }
+        self.y, self.c = self.g // 2, self.g % 2
+        self.g_y = (1 - self.y) * 2 + self.c
+        self.g_c = self.y * 2 + 1 - self.c
+        self.g_yc = (1 - self.y) * 2 + 1 - self.c
+        self.y_peer = (self.z * self.lanes + self.g_y, self.x)
+        self.c_peer = (self.z * self.lanes + self.g_c, self.x)
+
+    def z_from(self, d):
+        return lax.rem(self.z + SPLIT - d, SPLIT)
+
+    def z_to(self, d):
+        return lax.rem(self.z + d, SPLIT)
+
+
+def enter(peers):
+    barrier = pltpu.get_barrier_semaphore()
+    for peer in peers:
+        pl.semaphore_signal(barrier, inc=1, device_id=peer, device_id_type=MESH)
+    pl.semaphore_wait(barrier, len(peers))
+
+
+def remote(src, dst, send, recv, peer):
+    return pltpu.make_async_remote_copy(
+        src_ref=src, dst_ref=dst, send_sem=send, recv_sem=recv, device_id=peer, device_id_type=MESH
+    )
+
+
+NEAR = (1, 3, 2)
+
+
+class Gather:
+    def __init__(self, place, buf, send, recv):
+        self.place, self.buf = place, buf
+        own = buf.at[place.z * 2 + place.x]
+        self.own = own
+        self.along_z = [
+            remote(own, own, send.at[i], recv.at[i], place.z_peer[d]) for i, d in enumerate(NEAR)
+        ]
+        self.to_x = remote(own, own, send.at[3], recv.at[3], place.x_peer)
+        self.landed = []
+        self.forward = []
+        for i, d in enumerate(NEAR):
+            block = buf.at[place.z_from(d) * 2 + place.x]
+            self.landed.append(remote(block, block, send.at[i], recv.at[i], place.z_peer[d]))
+            self.forward.append(remote(block, block, send.at[4 + i], recv.at[4 + i], place.x_peer))
+        self.other = [buf.at[place.z * 2 + 1 - place.x]] + [
+            buf.at[place.z_from(d) * 2 + 1 - place.x] for d in NEAR
+        ]
+        self.arrive_x = [
+            remote(block, block, send.at[3 + i], recv.at[3 + i], place.x_peer)
+            for i, block in enumerate(self.other)
+        ]
+
+    def start(self):
+        for copy in self.along_z:
+            copy.start()
+        self.to_x.start()
+
+    def pass_on(self):
+        for landed, forward in zip(self.landed, self.forward):
+            landed.wait_recv()
+            forward.start()
+
+    def finish(self):
+        for copy in self.arrive_x:
+            copy.wait_recv()
+        for copy in self.along_z + [self.to_x] + self.forward:
+            copy.wait_send()
+
+
+class Scatter:
+    def __init__(self, place, part, from_x, to_z, from_z, send, recv):
+        self.place, self.part, self.from_x = place, part, from_x
+        self.to_z, self.from_z = to_z, from_z
+        self.order = [place.z_to(d) for d in NEAR] + [place.z]
+        self.across = [
+            remote(
+                part.at[target, 1 - place.x], from_x.at[i], send.at[i], recv.at[i], place.x_peer
+            )
+            for i, target in enumerate(self.order)
+        ]
+        self.along = [
+            remote(to_z.at[i], from_z.at[i], send.at[4 + i], recv.at[4 + i], place.z_peer[d])
+            for i, d in enumerate(NEAR)
+        ]
+
+    def send_x(self, i):
+        self.across[i].start()
+
+    def pass_on(self):
+        for i in range(3):
+            self.across[i].wait_recv()
+            self.to_z[i] = (
+                self.part[self.order[i], self.place.x].astype(F32) + self.from_x[i].astype(F32)
+            ).astype(BF)
+            self.along[i].start()
+
+    def finish(self):
+        self.across[3].wait_recv()
+        total = self.part[self.place.z, self.place.x].astype(F32) + self.from_x[3].astype(F32)
+        for i in range(3):
+            self.along[i].wait_recv()
+            total = total + self.from_z[i].astype(F32)
+        for copy in self.across + self.along:
+            copy.wait_send()
+        return total
+
+
+def gather_scratch(rows, width):
+    return [
+        pltpu.VMEM((2 * SPLIT, rows, width), BF),
+        pltpu.SemaphoreType.DMA((7,)),
+        pltpu.SemaphoreType.DMA((7,)),
+    ]
+
+
+def scatter_scratch(rows, width):
+    return [
+        pltpu.VMEM((SPLIT, 2, rows, width), BF),
+        pltpu.VMEM((SPLIT, rows, width), BF),
+        pltpu.VMEM((3, rows, width), BF),
+        pltpu.VMEM((3, rows, width), BF),
+        pltpu.SemaphoreType.DMA((7,)),
+        pltpu.SemaphoreType.DMA((7,)),
+    ]
+
+
+def item_rows(mod, items, index, width):
+    first = mod[0:1, index * width : (index + 1) * width]
+    second = mod[1:2, index * width : (index + 1) * width]
+    return jnp.where(items == 0, first, second)
+
+
+def item_sums(value, items):
+    return [
+        jnp.sum(jnp.where(items == item, value, 0.0), axis=0, keepdims=True)
+        for item in range(ITEMS)
+    ]
+
+
+def ffn_kernel(
+    branch, patches, out_grad, mod, items, gain_out, gain_in, gain_ffn, w_gate, w_up, w_down,
+    output, grad_resid, grad_attn, sums, grad_w,
+    n_buf, n_send, n_recv, g_buf, g_send, g_recv,
+    p1, fx1, tz1, fz1, s1, r1, p2, fx2, tz2, fz2, s2, r2,
+    gate_s, up_s, hid_s, gg_s, gu_s, out_send, out_recv,
+):
+    place = Place()
+    rows, width = branch.shape
+    item = items[...]
+    enter([place.x_peer] + [place.z_peer[d] for d in (1, 2, 3)])
+    norms = Gather(place, n_buf, n_send, n_recv)
+    grads = Gather(place, g_buf, g_send, g_recv)
+    down = Scatter(place, p1, fx1, tz1, fz1, s1, r1)
+    back = Scatter(place, p2, fx2, tz2, fz2, s2, r2)
+
+    hat_two, recip_two = normed_pair(branch[...])
+    tanh_one = jnp.tanh(item_rows(mod, item, 1, width))
+    resid = patches[...].astype(F32) + tanh_one * hat_two * gain_out[...]
+    hat_three, recip_three = normed_pair(resid)
+    factor_three = gain_in[...] * (1.0 + item_rows(mod, item, 2, width))
+    norms.own[...] = (hat_three * factor_three).astype(BF)
+    norms.start()
+    norms.pass_on()
+    norms.finish()
+
+    def forward(i, carry):
+        target = lax.rem(place.z + 1 + i, SPLIT)
+        block = n_buf[pl.ds(target * 2, 2)].reshape(2 * rows, width)
+        gate_val = bdot(block, w_gate[...])
+        up_val = bdot(block, w_up[...])
+        gate_s[target] = gate_val
+        up_s[target] = up_val
+        hidden = (gate_val * jax.nn.sigmoid(gate_val) * up_val).astype(BF)
+        hid_s[target] = hidden
+        p1[target] = dot_t(hidden, w_down[...]).astype(BF).reshape(2, rows, width)
+        return carry
+
+    lax.fori_loop(0, SPLIT, forward, 0)
+    for i in range(4):
+        down.send_x(i)
+    down.pass_on()
+    ffn = down.finish()
+
+    hat_four, recip_four = normed_pair(ffn)
+    tanh_two = jnp.tanh(item_rows(mod, item, 3, width))
+    output[place.x] = resid + tanh_two * hat_four * gain_ffn[...]
+    out_copy = remote(output.at[place.x], output.at[place.x], out_send, out_recv, place.x_peer)
+    grad_out = out_grad[...].astype(F32)
+    grad_four = grad_out * tanh_two
+    grads.own[...] = normed_back(grad_four * gain_ffn[...], hat_four, recip_four).astype(BF)
+    grads.start()
+    out_copy.start()
+    gate_sums = item_sums(
+        grad_out * hat_four * gain_ffn[...] * (1.0 - tanh_two * tanh_two), item
+    )
+    sum_ffn_out = jnp.sum(grad_four * hat_four, axis=0, keepdims=True)
+    sums[...] = jnp.zeros_like(sums)
+    sums[2:3] = sum_ffn_out
+    sums[8:9] = gate_sums[0]
+    sums[9:10] = gate_sums[1]
+    grads.pass_on()
+    grads.finish()
+
+    def backward(i, carry):
+        target = lax.rem(place.z + 1 + i, SPLIT)
+        block = g_buf[pl.ds(target * 2, 2)].reshape(2 * rows, width)
+        grad_hidden = bdot(block, w_down[...])
+        gate_val = gate_s[target]
+        gate_sig = jax.nn.sigmoid(gate_val)
+        grad_gate = (
+            grad_hidden * up_s[target] * gate_sig * (1.0 + gate_val * (1.0 - gate_sig))
+        ).astype(BF)
+        grad_up = (grad_hidden * gate_val * gate_sig).astype(BF)
+        gg_s[target] = grad_gate
+        gu_s[target] = grad_up
+        p2[target] = (
+            (dot_t(grad_gate, w_gate[...]) + dot_t(grad_up, w_up[...]))
+            .astype(BF)
+            .reshape(2, rows, width)
+        )
+        return carry
+
+    lax.fori_loop(0, SPLIT, backward, 0)
+    for i in range(4):
+        back.send_x(i)
+    back.pass_on()
+
+    hid = w_gate.shape[1]
+    step = 256
+
+    def weights(i, carry):
+        cols = pl.ds(pl.multiple_of(i * step, step), step)
+        left = n_buf[:, :, cols].reshape(SPLIT * 2 * rows, step)
+        grad_w[cols, 0:hid] = t_dot(left, gg_s[...].reshape(-1, hid)).astype(BF)
+        grad_w[cols, hid : 2 * hid] = t_dot(left, gu_s[...].reshape(-1, hid)).astype(BF)
+        left = g_buf[:, :, cols].reshape(SPLIT * 2 * rows, step)
+        grad_w[cols, 2 * hid : 3 * hid] = t_dot(left, hid_s[...].reshape(-1, hid)).astype(BF)
+        return carry
+
+    lax.fori_loop(0, width // step, weights, 0)
+
+    grad_norm = back.finish()
+    scale_sums = item_sums(grad_norm * hat_three * gain_in[...], item)
+    sums[1:2] = jnp.sum(
+        grad_norm * hat_three * (1.0 + item_rows(mod, item, 2, width)), axis=0, keepdims=True
+    )
+    sums[6:7] = scale_sums[0]
+    sums[7:8] = scale_sums[1]
+    grad_res = grad_out + normed_back(grad_norm * factor_three, hat_three, recip_three)
+    grad_resid[...] = grad_res
+    gate_sums = item_sums(
+        grad_res * hat_two * gain_out[...] * (1.0 - tanh_one * tanh_one), item
+    )
+    grad_two = grad_res * tanh_one
+    sums[0:1] = jnp.sum(grad_two * hat_two, axis=0, keepdims=True)
+    sums[4:5] = gate_sums[0]
+    sums[5:6] = gate_sums[1]
+    grad_attn[...] = normed_back(grad_two * gain_out[...], hat_two, recip_two).astype(BF)
+    out_copy.wait_send()
+    remote(
+        output.at[1 - place.x], output.at[1 - place.x], out_send, out_recv, place.x_peer
+    ).wait_recv()
+
+
+def ffn_call(branch, patches, out_grad, mod, items, gain_out, gain_in, gain_ffn, wg, wu, wd):
+    rows, width = branch.shape
+    hid = wg.shape[1]
+    vmem = pl.BlockSpec(memory_space=pltpu.VMEM)
+    shape = jax.ShapeDtypeStruct
+    return pl.pallas_call(
+        ffn_kernel,
+        out_shape=(
+            shape((2, rows, width), F32),
+            shape((rows, width), F32),
+            shape((rows, width), BF),
+            shape((16, width), F32),
+            shape((width, 3 * hid), BF),
+        ),
+        in_specs=[vmem] * 11,
+        out_specs=[vmem] * 5,
+        scratch_shapes=gather_scratch(rows, width)
+        + gather_scratch(rows, width)
+        + scatter_scratch(rows, width)
+        + scatter_scratch(rows, width)
+        + [
+            pltpu.VMEM((SPLIT, 2 * rows, hid), F32),
+            pltpu.VMEM((SPLIT, 2 * rows, hid), F32),
+            pltpu.VMEM((SPLIT, 2 * rows, hid), BF),
+            pltpu.VMEM((SPLIT, 2 * rows, hid), BF),
+            pltpu.VMEM((SPLIT, 2 * rows, hid), BF),
+            pltpu.SemaphoreType.DMA,
+            pltpu.SemaphoreType.DMA,
+        ],
+        compiler_params=pltpu.CompilerParams(
+            collective_id=2, has_side_effects=True, vmem_limit_bytes=VMEM_LIMIT
+        ),
+        name="feed_forward",
+    )(branch, patches, out_grad, mod, items, gain_out, gain_in, gain_ffn, wg, wu, wd)
+
+
+class LaneGather:
+    def __init__(self, place, buf, send, recv):
+        own = buf.at[place.g]
+        self.own = own
+        self.to_y = remote(own, own, send.at[0], recv.at[0], place.y_peer)
+        self.to_c = remote(own, own, send.at[1], recv.at[1], place.c_peer)
+        across = buf.at[place.g_y]
+        self.from_y = remote(across, across, send.at[2], recv.at[0], place.c_peer)
+        self.on = remote(across, across, send.at[2], recv.at[2], place.c_peer)
+        pair = buf.at[place.g_c]
+        self.from_c = remote(pair, pair, send.at[1], recv.at[1], place.c_peer)
+        diagonal = buf.at[place.g_yc]
+        self.from_diagonal = remote(diagonal, diagonal, send.at[2], recv.at[2], place.c_peer)
+
+    def start(self):
+        self.to_y.start()
+        self.to_c.start()
+
+    def pass_on(self):
+        self.from_y.wait_recv()
+        self.on.start()
+
+    def finish(self):
+        self.from_c.wait_recv()
+        self.from_diagonal.wait_recv()
+        self.to_y.wait_send()
+        self.to_c.wait_send()
+        self.on.wait_send()
+
+
+class WeightGather:
+    def __init__(self, place, shards, buf, send, recv):
+        self.place = place
+        lanes = place.lanes
+        order = [place.z] + [place.z_from(d) for d in NEAR]
+        own = buf.at[place.z * lanes + place.g]
+        self.keep = pltpu.make_async_copy(shards.at[place.z], own, recv.at[3])
+        self.along_z = [
+            remote(shards.at[place.z_to(d)], own, send.at[i], recv.at[i], place.z_peer[d])
+            for i, d in enumerate(NEAR)
+        ]
+        self.blocks, self.to_y, self.to_c, self.from_y, self.on = [], [], [], [], []
+        self.from_c, self.from_diagonal = [], []
+        for i, z in enumerate(order):
+            block = buf.at[z * lanes + place.g]
+            self.blocks.append(block)
+            self.to_y.append(remote(block, block, send.at[4 + i], recv.at[4 + i], place.y_peer))
+            self.to_c.append(remote(block, block, send.at[8 + i], recv.at[8 + i], place.c_peer))
+            across = buf.at[z * lanes + place.g_y]
+            self.from_y.append(
+                remote(across, across, send.at[12 + i], recv.at[4 + i], place.c_peer)
+            )
+            self.on.append(
+                remote(across, across, send.at[12 + i], recv.at[12 + i], place.c_peer)
+            )
+            pair = buf.at[z * lanes + place.g_c]
+            self.from_c.append(remote(pair, pair, send.at[8 + i], recv.at[8 + i], place.c_peer))
+            diagonal = buf.at[z * lanes + place.g_yc]
+            self.from_diagonal.append(
+                remote(diagonal, diagonal, send.at[12 + i], recv.at[12 + i], place.c_peer)
+            )
+        self.landed = [
+            remote(self.blocks[1 + i], self.blocks[1 + i], send.at[i], recv.at[i], place.z_peer[d])
+            for i, d in enumerate(NEAR)
+        ]
+
+    def start(self):
+        for copy in self.along_z:
+            copy.start()
+        self.keep.start()
+
+    def pass_own(self):
+        self.keep.wait()
+        self.to_y[0].start()
+        self.to_c[0].start()
+
+    def pass_z(self, i):
+        self.landed[i].wait_recv()
+        self.to_y[1 + i].start()
+        self.to_c[1 + i].start()
+
+    def pass_y(self, i):
+        self.from_y[i].wait_recv()
+        self.on[i].start()
+
+    def finish(self):
+        for copy in self.from_c + self.from_diagonal:
+            copy.wait_recv()
+        for copy in self.along_z + self.to_y + self.to_c + self.on:
+            copy.wait_send()
+
+
+class AllSum:
+    def __init__(self, place, acc, land, slots, send, recv, over_x):
+        self.place, self.acc, self.land, self.slots = place, acc, land, slots
+        peers = [place.c_peer, place.y_peer] + ([place.x_peer] if over_x else [])
+        self.steps = len(peers)
+        self.pairs = [
+            remote(acc.at[i], land.at[i], send.at[i], recv.at[i], peer)
+            for i, peer in enumerate(peers)
+        ]
+        own = slots.at[place.z]
+        self.own = own
+        self.along_z = [
+            remote(own, own, send.at[3 + i], recv.at[3 + i], place.z_peer[d])
+            for i, d in enumerate(NEAR)
+        ]
+        self.landed = []
+        for i, d in enumerate(NEAR):
+            slot = slots.at[place.z_from(d)]
+            self.landed.append(remote(slot, slot, send.at[3 + i], recv.at[3 + i], place.z_peer[d]))
+
+    def start(self):
+        self.pairs[0].start()
+
+    def step(self, i):
+        self.pairs[i].wait_recv()
+        total = self.acc[i] + self.land[i]
+        if i + 1 < self.steps:
+            self.acc[i + 1] = total
+            self.pairs[i + 1].start()
+        else:
+            self.own[...] = total
+            for copy in self.along_z:
+                copy.start()
+
+    def finish(self):
+        for copy in self.landed:
+            copy.wait_recv()
+        for copy in self.pairs + self.along_z:
+            copy.wait_send()
+        return (self.slots[0] + self.slots[1]) + (self.slots[2] + self.slots[3])
+
+
+class LaneScatter:
+    def __init__(self, place, part, from_c, acc, from_y, send, recv):
+        self.place, self.part, self.from_c = place, part, from_c
+        self.acc, self.from_y = acc, from_y
+        self.to_c = remote(part.at[1 - place.c], from_c, send.at[0], recv.at[0], place.c_peer)
+        self.to_y = remote(acc.at[1 - place.y], from_y, send.at[1], recv.at[1], place.y_peer)
+
+    def start(self):
+        self.to_c.start()
+
+    def step(self):
+        self.to_c.wait_recv()
+        c, y = self.place.c, self.place.y
+        self.acc[1 - y] = (
+            self.part[c, 1 - y].astype(F32) + self.from_c[1 - y].astype(F32)
+        ).astype(BF)
+        self.to_y.start()
+
+    def finish(self):
+        c, y = self.place.c, self.place.y
+        near = self.part[c, y].astype(F32) + self.from_c[y].astype(F32)
+        self.to_y.wait_recv()
+        self.to_c.wait_send()
+        self.to_y.wait_send()
+        return near + self.from_y[...].astype(F32)
+
+
+def segments(lanes):
+    row = lax.broadcasted_iota(jnp.int32, (lanes, lanes), 0) // HEAD
+    col = lax.broadcasted_iota(jnp.int32, (lanes, lanes), 1) // HEAD
+    return jnp.where(row == col, 1.0 / HEAD, 0.0).astype(F32)
+
+
+def head_mean(value, mean):
+    return jnp.dot(value, mean, precision=HIGH, preferred_element_type=F32)
+
+
+def swap_quarters(value):
+    lanes = value.shape[1]
+    lane = lax.broadcasted_iota(jnp.int32, value.shape, 1)
+    even = (lane // (HEAD // 4)) % 2 == 0
+    return jnp.where(
+        even, pltpu.roll(value, lanes - HEAD // 4, 1), pltpu.roll(value, HEAD // 4, 1)
+    )
+
+
+def head_lanes(shape, head):
+    lane = lax.broadcasted_iota(jnp.int32, shape, 1)
+    return (lane >= head * HEAD) & (lane < (head + 1) * HEAD)
+
+
+def of_head(value, head):
+    return jnp.where(head_lanes(value.shape, head), value, jnp.zeros_like(value))
+
+
+def attention_kernel(
+    patches, mod_in, b_ada, pos_in, freqs, cap_in, qkvo_in, ffn_in, grp_items, key_items,
+    gain_in, gain_kq, gain_ckey, gate_row,
+    branch, norm_in, qkvo, ffn, mod, queries, kv, k_all, v_all, kq_hat, kq_recip,
+    cos_t, sin_t, totals, attn_self, attn_cross, mixed, cap_k, cap_v, cap_hat, cap_recip,
+    x_buf, x_send, x_recv, w_send, w_recv, f_send, f_recv,
+    m_acc, m_land, m_slots, m_send, m_recv,
+    pos_buf, pos_send, pos_recv,
+    cap_fc, cap_acc, cap_fy, cap_s, cap_r, cap_out, cap_z, cz_send, cz_recv,
+    cap_kv, ckv_send, ckv_recv, kv_send, kv_recv, p1, fx1, tz1, fz1, s1, r1,
+):
+    place = Place()
+    rows, width = patches.shape
+    wq = queries.shape[1]
+    heads = wq // HEAD
+    both = 2 * rows
+    enter([place.x_peer, place.c_peer, place.y_peer] + [place.z_peer[d] for d in (1, 2, 3)])
+
+    weights = WeightGather(place, qkvo_in, qkvo, w_send, w_recv)
+    weights.start()
+    tokens = Gather(place, x_buf, x_send, x_recv)
+    tokens.own[...] = patches[...]
+    tokens.start()
+    sums = AllSum(place, m_acc, m_land, m_slots, m_send, m_recv, False)
+    m_acc[0] = mod_in[...]
+    sums.start()
+    caption = LaneScatter(place, cap_in, cap_fc, cap_acc, cap_fy, cap_s, cap_r)
+    caption.start()
+    pos_buf[place.z] = pos_in[...]
+    own_pos = pos_buf.at[place.z]
+    pos_out = [
+        remote(own_pos, own_pos, pos_send.at[i], pos_recv.at[i], place.z_peer[d])
+        for i, d in enumerate(NEAR)
+    ]
+    for copy in pos_out:
+        copy.start()
+    weights.pass_own()
+    sums.step(0)
+    sums.step(1)
+    caption.step()
+    mean = segments(2 * wq)
+    lane = lax.broadcasted_iota(jnp.int32, (1, 2 * wq), 1)
+
+    for i, d in enumerate(NEAR):
+        slot = pos_buf.at[place.z_from(d)]
+        remote(slot, slot, pos_send.at[i], pos_recv.at[i], place.z_peer[d]).wait_recv()
+    lane_row = lax.broadcasted_iota(jnp.int32, (1, 2 * HEAD), 1)
+    by_row = (lane_row // (HEAD // 2)) % 2 == 0
+    sign = jnp.where((lane_row // (HEAD // 4)) % 2 == 0, -1.0, 1.0)
+    for i in range(SPLIT):
+        cols = pos_buf[i].T
+        angle = jnp.where(by_row, cols[:, 0:1], cols[:, 1:2]) * freqs[...]
+        cos_t[i] = jnp.cos(angle)
+        sin_t[i] = jnp.sin(angle) * sign
+
+    cap_out[...] = caption.finish().astype(BF)
+    cap_sends = [
+        remote(
+            cap_out.at[place.z_to(d)], cap_z.at[place.z], cz_send.at[i], cz_recv.at[i],
+            place.z_peer[d],
+        )
+        for i, d in enumerate(NEAR)
+    ]
+    for copy in cap_sends:
+        copy.start()
+    cap_z[place.z] = cap_out[place.z]
+    tokens.pass_on()
+    for i in range(3):
+        weights.pass_z(i)
+    for i in range(4):
+        weights.pass_y(i)
+    feed = WeightGather(place, ffn_in, ffn, f_send, f_recv)
+    feed.start()
+    feed.pass_own()
+    mod[...] = sums.finish() + b_ada[...]
+    for i, d in enumerate(NEAR):
+        slot = cap_z.at[place.z_from(d)]
+        remote(slot, slot, cz_send.at[i], cz_recv.at[i], place.z_peer[d]).wait_recv()
+    cap_raw = (cap_z[0].astype(F32) + cap_z[1].astype(F32)) + (
+        cap_z[2].astype(F32) + cap_z[3].astype(F32)
+    )
+    recip = lax.rsqrt(head_mean(cap_raw * cap_raw, mean) + EPS)
+    hat = cap_raw * recip
+    cap_hat[...] = hat
+    cap_recip[...] = recip
+    cap_gather = LaneGather(place, cap_kv, ckv_send, ckv_recv)
+    cap_gather.own[...] = jnp.where(lane < wq, hat * gain_ckey[...], cap_raw).astype(BF)
+    cap_gather.start()
+    tokens.finish()
+    cap_gather.pass_on()
+    weights.finish()
+
+    keep = LaneGather(place, kv, kv_send, kv_recv)
+
+    def project(i, carry):
+        at = pl.ds(pl.multiple_of(i * both, both), both)
+        block = x_buf[pl.ds(i * 2, 2)].reshape(both, width).astype(F32)
+        unit, _ = normed_pair(block)
+        factor = gain_in[...] * (1.0 + item_rows(mod, grp_items[at], 0, width))
+        norm = (unit * factor).astype(BF)
+        norm_in[i] = norm
+        raw = bdot(norm, qkvo[:, :, 0 : 2 * wq].reshape(width, 2 * wq))
+        own_v = bdot(norm, qkvo[:, :, 2 * wq : 4 * wq].reshape(width, 2 * wq))
+        recip = lax.rsqrt(head_mean(raw * raw, mean) + EPS)
+        hat = raw * recip
+        kq_hat[i] = hat
+        kq_recip[i] = recip
+        cos = jnp.concatenate([cos_t[i]] * heads, axis=1)
+        sin = jnp.concatenate([sin_t[i]] * heads, axis=1)
+        gained = hat * gain_kq[...]
+        turned = gained * cos + swap_quarters(gained) * sin
+        kv[place.g, at] = jnp.where(lane < wq, turned, own_v).astype(BF)
+        queries[at] = turned[:, wq:].astype(BF)
+        return carry
+
+    lax.fori_loop(0, SPLIT, project, 0)
+    keep.start()
+    for i in range(3):
+        feed.pass_z(i)
+    cap_gather.finish()
+    kv_text = cap_kv[...].reshape(SPLIT * cap_kv.shape[1], 2 * wq)
+    cap_k[...] = kv_text[:, :wq]
+    cap_v[...] = kv_text[:, wq:]
+    scale = 1.0 / math.sqrt(HEAD)
+    gates = gate_row[...]
+
+    def one_head(block, keys, vals, head, same):
+        scores = dot_t(of_head(block, head), keys)
+        if same is not None:
+            scores = jnp.where(same, scores, NEG)
+        most = jnp.max(scores, axis=1, keepdims=True)
+        weight = jnp.exp(scores - most)
+        total = jnp.sum(weight, axis=1, keepdims=True)
+        out = bdot((weight * (1.0 / total)).astype(BF), vals)
+        return of_head(out, head), most + jnp.log(total)
+
+    slot_lane = lax.broadcasted_iota(jnp.int32, (1, totals.shape[1]), 1)
+
+    def cross(i, carry):
+        at = pl.ds(pl.multiple_of(i * both, both), both)
+        block = (queries[at].astype(F32) * scale).astype(BF)
+        out = jnp.zeros((both, wq), F32)
+        logs = jnp.zeros((both, totals.shape[1]), F32)
+        for head in range(heads):
+            part, log = one_head(block, cap_k[...], cap_v[...], head, None)
+            out = out + part
+            logs = logs + jnp.where(slot_lane == heads + head, log, 0.0)
+        attn_cross[at] = out
+        totals[at] = logs
+        return carry
+
+    lax.fori_loop(0, SPLIT, cross, 0)
+    keep.pass_on()
+    keep.finish()
+    for i in range(SPLIT):
+        lump = kv[i]
+        at = pl.ds(i * lump.shape[0], lump.shape[0])
+        k_all[at] = lump[:, :wq]
+        v_all[at] = lump[:, wq:]
+    for i in range(4):
+        feed.pass_y(i)
+
+    def attend(i, carry):
+        at = pl.ds(pl.multiple_of(i * both, both), both)
+        block = (queries[at].astype(F32) * scale).astype(BF)
+        same = grp_items[at] == key_items[...]
+        out = jnp.zeros((both, wq), F32)
+        logs = totals[at]
+        for head in range(heads):
+            part, log = one_head(block, k_all[...], v_all[...], head, same)
+            out = out + part
+            logs = logs + jnp.where(slot_lane == head, log, 0.0)
+        attn_self[at] = out
+        totals[at] = logs
+        blend = (out + gates * attn_cross[at]).astype(BF)
+        mixed[at] = blend
+        wide = jnp.concatenate([blend, jnp.zeros_like(blend)], axis=1)
+        p1[i] = (
+            dot_t(wide, qkvo[:, :, 2 * wq : 4 * wq].reshape(width, 2 * wq))
+            .astype(BF)
+            .reshape(2, rows, width)
+        )
+        return carry
+
+    lax.fori_loop(0, SPLIT, attend, 0)
+    out = Scatter(place, p1, fx1, tz1, fz1, s1, r1)
+    for i in range(4):
+        out.send_x(i)
+    out.pass_on()
+    feed.finish()
+    branch[...] = out.finish()
+    for copy in pos_out + cap_sends:
+        copy.wait_send()
+
+
+def attention_call(
+    patches, mod_in, b_ada, pos_in, freqs, cap_in, qkvo_in, ffn_in, grp_items, key_items,
+    gain_in, gain_kq, gain_ckey, gate_row,
+):
+    rows, width = patches.shape
+    wq = qkvo_in.shape[2] // 4
+    lanes = cap_in.shape[0] * cap_in.shape[1]
+    text = cap_in.shape[3]
+    both = 2 * rows
+    group = SPLIT * both
+    vmem = pl.BlockSpec(memory_space=pltpu.VMEM)
+    hbm = pl.BlockSpec(memory_space=pl.ANY)
+    shape = jax.ShapeDtypeStruct
+    dma = pltpu.SemaphoreType.DMA
+    outs = {
+        "branch": shape((rows, width), F32),
+        "norm_in": shape((SPLIT, both, width), BF),
+        "qkvo": shape((SPLIT * lanes,) + qkvo_in.shape[1:], BF),
+        "ffn": shape((SPLIT * lanes,) + ffn_in.shape[1:], BF),
+        "mod": shape(mod_in.shape, F32),
+        "queries": shape((group, wq), BF),
+        "kv": shape((lanes, group, 2 * wq), BF),
+        "k_all": shape((lanes * group, wq), BF),
+        "v_all": shape((lanes * group, wq), BF),
+        "kq_hat": shape((SPLIT, both, 2 * wq), F32),
+        "kq_recip": shape((SPLIT, both, 2 * wq), F32),
+        "cos": shape((SPLIT, both, 2 * HEAD), F32),
+        "sin": shape((SPLIT, both, 2 * HEAD), F32),
+        "totals": shape((group, 128), F32),
+        "attn_self": shape((group, wq), F32),
+        "attn_cross": shape((group, wq), F32),
+        "mixed": shape((group, wq), BF),
+        "cap_k": shape((lanes * text, wq), BF),
+        "cap_v": shape((lanes * text, wq), BF),
+        "cap_hat": shape((text, 2 * wq), F32),
+        "cap_recip": shape((text, 2 * wq), F32),
+    }
+    results = pl.pallas_call(
+        attention_kernel,
+        out_shape=tuple(outs.values()),
+        in_specs=[vmem] * 7 + [hbm] + [vmem] * 6,
+        out_specs=[hbm if name == "ffn" else vmem for name in outs],
+        scratch_shapes=gather_scratch(rows, width)
+        + [dma((16,)), dma((16,)), dma((16,)), dma((16,))]
+        + [
+            pltpu.VMEM((2,) + mod_in.shape, F32),
+            pltpu.VMEM((2,) + mod_in.shape, F32),
+            pltpu.VMEM((SPLIT,) + mod_in.shape, F32),
+            dma((6,)),
+            dma((6,)),
+        ]
+        + [pltpu.VMEM((SPLIT,) + pos_in.shape, F32), dma((3,)), dma((3,))]
+        + [
+            pltpu.VMEM(cap_in.shape[1:], BF),
+            pltpu.VMEM(cap_in.shape[1:], BF),
+            pltpu.VMEM(cap_in.shape[2:], BF),
+            dma((2,)),
+            dma((2,)),
+            pltpu.VMEM(cap_in.shape[2:], BF),
+            pltpu.VMEM(cap_in.shape[2:], BF),
+            dma((3,)),
+            dma((3,)),
+            pltpu.VMEM((lanes, text, 2 * wq), BF),
+            dma((3,)),
+            dma((3,)),
+        ]
+        + [dma((3,)), dma((3,))]
+        + scatter_scratch(rows, width),
+        compiler_params=pltpu.CompilerParams(
+            collective_id=1, has_side_effects=True, vmem_limit_bytes=VMEM_LIMIT
+        ),
+        name="attention",
+    )(
+        patches, mod_in, b_ada, pos_in, freqs, cap_in, qkvo_in, ffn_in, grp_items, key_items,
+        gain_in, gain_kq, gain_ckey, gate_row,
+    )
+    return dict(zip(outs, results))
+
+
+def local_any(
+    patches,
+    caption,
+    band_table,
+    block_item,
+    item_band,
+    positions,
+    out_grad,
+    w_query,
+    w_key,
+    w_value,
+    w_out,
+    w_gate,
+    w_up,
+    w_down,
+    w_ckey,
+    w_cvalue,
+    w_ada,
+    b_ada,
+    g_attn_in,
+    g_attn_out,
+    g_ffn_in,
+    g_ffn_out,
+    g_query,
+    g_key,
+    g_ckey,
+    cross_gate,
+):
+    scale = 1.0 / math.sqrt(HEAD)
+    rank = lax.axis_index("sp")
+    half = lax.axis_index("tp")
+    cycle = lax.axis_size("sp")
+    halves = lax.axis_size("tp")
+    lanes = cycle // SPLIT
+    along_z, along_g = groups_of(cycle)
+    my_z, my_g = rank // lanes, rank % lanes
+    tok_rows, width = patches.shape
+    own_rows = tok_rows // halves
+    text_count = caption.shape[0]
+    blocks_dev = tok_rows // BLK
+    wq, wf = w_query.shape[1] // SPLIT, w_gate.shape[1] // SPLIT
+    heads = wq // HEAD
+    sizes = (wq, wq, wq, wq, wf, wf, wf)
+    starts = [sum(sizes[:i]) for i in range(8)]
+
+    def gather_z(block):
+        return lax.all_gather(block, "sp", axis_index_groups=along_z, axis=0, tiled=False)
+
+    def gather_g(block):
+        return lax.all_gather(block, "sp", axis_index_groups=along_g, axis=0, tiled=False)
+
+    def scatter_z(block):
+        return lax.psum_scatter(
+            block, "sp", axis_index_groups=along_z, scatter_dimension=0, tiled=False
+        )
+
+    def scatter_g(block):
+        return lax.psum_scatter(
+            block, "sp", axis_index_groups=along_g, scatter_dimension=0, tiled=False
+        )
+
+    def turn_z(block):
+        return lax.all_to_all(
+            block, "sp", 0, 0, axis_index_groups=along_z, tiled=True
+        )
+
+    def sum_g(block):
+        return lax.psum(block, "sp", axis_index_groups=along_g)
+
+    def gather_tokens(own):
+        both = lax.all_gather(own, "tp", axis=0, tiled=True)
+        return gather_z(both).reshape(SPLIT * tok_rows, -1)
+
+    def scatter_tokens(part):
+        part = part.astype(BF).reshape(SPLIT, halves, own_rows, width)
+        mine = lax.psum_scatter(part, "tp", scatter_dimension=1, tiled=False)
+        return scatter_z(mine.astype(BF)).astype(F32)
+
+    def by_z(block):
+        rows, cols = block.shape
+        return block.reshape(rows, SPLIT, cols // SPLIT).transpose(1, 0, 2)
+
+    shards = jnp.concatenate(
+        [by_z(m) for m in (w_query, w_key, w_value, w_out.T, w_gate, w_up, w_down.T)], axis=2
+    )
+    rows_dev = shards.shape[1]
+    merged = gather_g(turn_z(shards)).transpose(1, 0, 2, 3).reshape(cycle * rows_dev, -1)
+    f_query, f_key, f_value, f_out, f_gate, f_up, f_down = (
+        merged[:, starts[i] : starts[i + 1]] for i in range(7)
+    )
+
+    items_all = block_item.reshape(SPLIT, lanes, blocks_dev)
+    grp_items = jnp.repeat(
+        lax.dynamic_index_in_dim(items_all, my_g, 1, keepdims=False).reshape(-1), BLK
+    )
+    key_items = jnp.repeat(items_all.transpose(1, 0, 2).reshape(-1), BLK)
+    row0 = half * own_rows
+
+    def own_part(block):
+        return lax.dynamic_slice_in_dim(block, row0, own_rows, 0)
+
+    own_items = own_part(
+        jnp.repeat(lax.dynamic_slice_in_dim(block_item, rank * blocks_dev, blocks_dev), BLK)
+    )
+
+    band_hot = (item_band[:, None] == jnp.arange(BANDS, dtype=jnp.int32)[None, :]).astype(F32)
+    cond_pre = jnp.dot(band_hot, band_table, precision=HIGH)
+    cond_sig = jax.nn.sigmoid(cond_pre)
+    cond_low = (cond_pre * cond_sig).astype(BF)
+    text_rows = w_ckey.shape[0]
+    text_local = lax.dynamic_slice_in_dim(caption, rank * text_rows, text_rows, 1)
+    modulation = lax.psum(bdot(cond_low, w_ada), "sp") + b_ada
+    cap_part = jnp.stack([by_z(bdot(text_local, w_ckey)), by_z(bdot(text_local, w_cvalue))], 1)
+    cap_raw = sum_g(scatter_z(cap_part))
+    ckey_hat, ckey_recip = normed_pair(cap_raw[0].reshape(text_count, heads, HEAD))
+
+    def per_head(vector):
+        return lax.dynamic_slice_in_dim(vector, my_z * wq, wq, 0).reshape(heads, HEAD)
+
+    gain_query, gain_key, gain_ckey = per_head(g_query), per_head(g_key), per_head(g_ckey)
+    gate_tanh = jnp.tanh(lax.dynamic_slice_in_dim(cross_gate, my_z * heads, heads, 0))
+    cap_keys = (ckey_hat * gain_ckey).astype(BF)
+    cap_values = cap_raw[1].astype(BF).reshape(text_count, heads, HEAD)
+
+    def of_items(rows, items):
+        return jnp.where(items[:, None] == 0, rows[0], rows[1])
+
+    mod_own = of_items(modulation, own_items)
+    scale_attn, gate_attn, scale_ffn, gate_ffn = (
+        mod_own[:, i * width : (i + 1) * width] for i in range(4)
+    )
+    group_rows = SPLIT * tok_rows
+
+    patch_f = own_part(patches).astype(F32)
+    grad_out = own_part(out_grad).astype(F32)
+    hat_one, recip_one = normed_pair(patch_f)
+    factor_one = g_attn_in * (1.0 + scale_attn)
+    norm_in = gather_tokens((hat_one * factor_one).astype(BF))
+    pos_all = gather_z(positions).transpose(1, 0, 2).reshape(2, group_rows)
+    cos_row, sin_row, cos_col, sin_col = angles(pos_all)
+    split_heads = (group_rows, heads, HEAD)
+    query_raw = bdot(norm_in, f_query).reshape(split_heads)
+    key_raw = bdot(norm_in, f_key).reshape(split_heads)
+    values_low = bdot(norm_in, f_value).astype(BF)
+    query_hat, query_recip = normed_pair(query_raw)
+    queries = rotate(query_hat * gain_query, cos_row, sin_row, cos_col, sin_col).astype(BF)
+    key_hat, key_recip = normed_pair(key_raw)
+    keys_low = rotate(key_hat * gain_key, cos_row, sin_row, cos_col, sin_col).astype(BF)
+    all_keys, all_values = (
+        gather_g(block).reshape(lanes * group_rows, heads, HEAD)
+        for block in (keys_low.reshape(group_rows, wq), values_low)
+    )
+    same = (grp_items[:, None] == key_items[None, :])[None]
+    scores = jnp.einsum("qhd,khd->hqk", queries, all_keys, preferred_element_type=F32) * scale
+    scores = jnp.where(same, scores, NEG)
+    exps = jnp.exp(scores - jnp.max(scores, axis=-1, keepdims=True))
+    probs = exps / jnp.sum(exps, axis=-1, keepdims=True)
+    probs_low = probs.astype(BF)
+    attn_self = jnp.einsum("hqk,khd->qhd", probs_low, all_values, preferred_element_type=F32)
+    cross_scores = (
+        jnp.einsum("qhd,khd->hqk", queries, cap_keys, preferred_element_type=F32) * scale
+    )
+    cross_exp = jnp.exp(cross_scores - jnp.max(cross_scores, axis=-1, keepdims=True))
+    cross_probs = cross_exp / jnp.sum(cross_exp, axis=-1, keepdims=True)
+    cross_low = cross_probs.astype(BF)
+    attn_cross = jnp.einsum("hqk,khd->qhd", cross_low, cap_values, preferred_element_type=F32)
+    mixed = (attn_self + gate_tanh[None, :, None] * attn_cross).astype(BF).reshape(group_rows, wq)
+    attn_branch = scatter_tokens(dot_t(mixed, f_out))
+
+    hat_two, recip_two = normed_pair(attn_branch)
+    tanh_one = jnp.tanh(gate_attn)
+    resid = patch_f + tanh_one * hat_two * g_attn_out
+    hat_three, recip_three = normed_pair(resid)
+    factor_three = g_ffn_in * (1.0 + scale_ffn)
+    norm_ffn = gather_tokens((hat_three * factor_three).astype(BF))
+    gate_val = bdot(norm_ffn, f_gate)
+    up_val = bdot(norm_ffn, f_up)
+    gate_sig = jax.nn.sigmoid(gate_val)
+    hidden = (gate_val * gate_sig * up_val).astype(BF)
+    ffn_branch = scatter_tokens(dot_t(hidden, f_down))
+    hat_four, recip_four = normed_pair(ffn_branch)
+    tanh_two = jnp.tanh(gate_ffn)
+    output = resid + tanh_two * hat_four * g_ffn_out
+
+    grad_gate_ffn = grad_out * hat_four * g_ffn_out * (1.0 - tanh_two * tanh_two)
+    grad_four = grad_out * tanh_two
+    grad_g_ffn_out = jnp.sum(grad_four * hat_four, axis=0)
+    grad_ffn = gather_tokens(
+        normed_back(grad_four * g_ffn_out, hat_four, recip_four).astype(BF)
+    )
+    grad_hidden = bdot(grad_ffn, f_down)
+    grad_gate = (grad_hidden * up_val * gate_sig * (1.0 + gate_val * (1.0 - gate_sig))).astype(BF)
+    grad_up = (grad_hidden * gate_val * gate_sig).astype(BF)
+    grad_norm_ffn = scatter_tokens(dot_t(grad_gate, f_gate) + dot_t(grad_up, f_up))
+    grad_scale_ffn = grad_norm_ffn * hat_three * g_ffn_in
+    grad_g_ffn_in = jnp.sum(grad_norm_ffn * hat_three * (1.0 + scale_ffn), axis=0)
+    grad_resid = grad_out + normed_back(grad_norm_ffn * factor_three, hat_three, recip_three)
+
+    grad_gate_attn = grad_resid * hat_two * g_attn_out * (1.0 - tanh_one * tanh_one)
+    grad_two = grad_resid * tanh_one
+    grad_g_attn_out = jnp.sum(grad_two * hat_two, axis=0)
+    grad_attn = gather_tokens(normed_back(grad_two * g_attn_out, hat_two, recip_two).astype(BF))
+    grad_mixed = bdot(grad_attn, f_out).astype(BF).reshape(split_heads)
+    grad_mixed_f = grad_mixed.astype(F32)
+    grad_cross_gate = jnp.sum(grad_mixed_f * attn_cross, axis=(0, 2)) * (
+        1.0 - gate_tanh * gate_tanh
+    )
+    grad_cross = (gate_tanh[None, :, None] * grad_mixed_f).astype(BF)
+    grad_cprobs = jnp.einsum("qhd,khd->hqk", grad_cross, cap_values, preferred_element_type=F32)
+    grad_cscores = (
+        cross_probs * (grad_cprobs - jnp.sum(cross_probs * grad_cprobs, axis=-1, keepdims=True))
+    ).astype(BF)
+    query_grad = jnp.einsum("hqk,khd->qhd", grad_cscores, cap_keys, preferred_element_type=F32)
+    grad_ckeys_part = (
+        jnp.einsum("hqk,qhd->khd", grad_cscores, queries, preferred_element_type=F32) * scale
+    )
+    grad_cvals_part = jnp.einsum(
+        "hqk,qhd->khd", cross_low, grad_cross, preferred_element_type=F32
+    )
+    row_delta = jnp.sum(grad_mixed_f * attn_self, axis=-1).T
+    grad_probs = jnp.einsum("qhd,khd->hqk", grad_mixed, all_values, preferred_element_type=F32)
+    grad_scores = (probs * (grad_probs - row_delta[..., None])).astype(BF)
+    query_grad = query_grad + jnp.einsum(
+        "hqk,khd->qhd", grad_scores, all_keys, preferred_element_type=F32
+    )
+    key_part = (
+        jnp.einsum("hqk,qhd->khd", grad_scores, queries, preferred_element_type=F32) * scale
+    )
+    value_part = jnp.einsum("hqk,qhd->khd", probs_low, grad_mixed, preferred_element_type=F32)
+    key_grad, value_grad = (
+        scatter_g(block.astype(BF).reshape(lanes, group_rows, wq)) for block in (key_part, value_part)
+    )
+    grad_queries = (query_grad * scale).astype(BF).astype(F32)
+    grad_qnorm = rotate(grad_queries, cos_row, -sin_row, cos_col, -sin_col)
+    grad_g_query = jnp.sum(grad_qnorm * query_hat, axis=0).reshape(-1)
+    grad_query_raw = (
+        normed_back(grad_qnorm * gain_query, query_hat, query_recip).astype(BF).reshape(-1, wq)
+    )
+    grad_keys = key_grad.astype(F32).reshape(split_heads)
+    grad_knorm = rotate(grad_keys, cos_row, -sin_row, cos_col, -sin_col)
+    grad_g_key = jnp.sum(grad_knorm * key_hat, axis=0).reshape(-1)
+    grad_key_raw = (
+        normed_back(grad_knorm * gain_key, key_hat, key_recip).astype(BF).reshape(-1, wq)
+    )
+    grad_values = value_grad.astype(BF)
+    grad_norm_in = scatter_tokens(
+        dot_t(grad_query_raw, f_query) + dot_t(grad_key_raw, f_key) + dot_t(grad_values, f_value)
+    )
+    grad_scale_attn = grad_norm_in * hat_one * g_attn_in
+    grad_g_attn_in = jnp.sum(grad_norm_in * hat_one * (1.0 + scale_attn), axis=0)
+    grad_patches = grad_resid + normed_back(grad_norm_in * factor_one, hat_one, recip_one)
+
+    grad_merged = jnp.concatenate(
+        [
+            t_dot(norm_in, grad_query_raw),
+            t_dot(norm_in, grad_key_raw),
+            t_dot(norm_in, grad_values),
+            t_dot(grad_attn, mixed),
+            t_dot(norm_ffn, grad_gate),
+            t_dot(norm_ffn, grad_up),
+            t_dot(grad_ffn, hidden),
+        ],
+        axis=1,
+    ).astype(BF)
+    grad_merged = grad_merged.reshape(SPLIT, lanes, rows_dev, -1).transpose(1, 0, 2, 3)
+    shard_grads = turn_z(scatter_g(grad_merged)).astype(F32)
+    (shard_query, shard_key, shard_value, shard_out, shard_gate, shard_up, shard_down) = (
+        shard_grads[:, :, starts[i] : starts[i + 1]].transpose(1, 0, 2).reshape(rows_dev, -1)
+        for i in range(7)
+    )
+
+    token_sums = lax.psum(
+        (
+            jnp.stack(
+                [
+                    jnp.concatenate(
+                        [
+                            jnp.sum(
+                                jnp.where((own_items == item)[:, None], block, 0.0), axis=0
+                            )
+                            for block in (
+                                grad_scale_attn,
+                                grad_gate_attn,
+                                grad_scale_ffn,
+                                grad_gate_ffn,
+                            )
+                        ]
+                    )
+                    for item in range(ITEMS)
+                ]
+            ),
+            grad_g_attn_in,
+            grad_g_attn_out,
+            grad_g_ffn_in,
+            grad_g_ffn_out,
+        ),
+        ("sp", "tp"),
+    )
+    head_sums = jnp.concatenate([grad_g_query, grad_g_key, grad_cross_gate])
+    head_sums = gather_z(sum_g(head_sums))
+    grad_ckeys = sum_g(grad_ckeys_part).astype(BF).astype(F32)
+    grad_cvals = sum_g(grad_cvals_part).astype(BF).reshape(text_count, wq)
+    grad_g_ckey = gather_z(jnp.sum(grad_ckeys * ckey_hat, axis=0).reshape(-1)).reshape(-1)
+    grad_ckey_raw = (
+        normed_back(grad_ckeys * gain_ckey, ckey_hat, ckey_recip).astype(BF).reshape(text_count, wq)
+    )
+    cap_grads = gather_z(jnp.stack([grad_ckey_raw, grad_cvals])).transpose(1, 2, 0, 3)
+    cap_grads = cap_grads.reshape(2, text_count, SPLIT * wq)
+    grad_mod = token_sums[0]
+    grad_b_ada = jnp.sum(grad_mod, axis=0)
+    grad_w_ada = jnp.dot(cond_low.astype(F32).T, grad_mod, precision=HIGH)
+    grad_cond_act = jnp.dot(grad_mod, w_ada.astype(F32).T, precision=HIGH)
+    grad_cond_pre = grad_cond_act * cond_sig * (1.0 + cond_pre * (1.0 - cond_sig))
+    grad_band_table = jnp.dot(band_hot.T, grad_cond_pre, precision=HIGH)
+    return (
+        lax.all_gather(output, "tp", axis=0, tiled=True),
+        lax.all_gather(grad_patches, "tp", axis=0, tiled=True),
+        shard_query,
+        shard_key,
+        shard_value,
+        shard_out.T,
+        shard_gate,
+        shard_up,
+        shard_down.T,
+        t_dot(text_local, cap_grads[0]),
+        t_dot(text_local, cap_grads[1]),
+        grad_w_ada,
+        grad_b_ada,
+        token_sums[1],
+        token_sums[2],
+        token_sums[3],
+        token_sums[4],
+        head_sums[:, :wq].reshape(-1),
+        head_sums[:, wq : 2 * wq].reshape(-1),
+        grad_g_ckey,
+        head_sums[:, 2 * wq :].reshape(-1),
+        grad_band_table,
+    )
 
 
 def local(
@@ -158,14 +1279,9 @@
         rows, cols = block.shape
         return block.reshape(rows, SPLIT, cols // SPLIT).transpose(1, 0, 2)
 
-    shards = jnp.concatenate(
-        [by_z(m) for m in (w_query, w_key, w_value, w_out.T, w_gate, w_up, w_down.T)], axis=2
-    )
-    rows_dev = shards.shape[1]
-    merged = gather_g(turn_z(shards)).transpose(1, 0, 2, 3).reshape(cycle * rows_dev, -1)
-    f_query, f_key, f_value, f_out, f_gate, f_up, f_down = (
-        merged[:, starts[i] : starts[i + 1]] for i in range(7)
-    )
+    qkvo_in = jnp.concatenate([by_z(m) for m in (w_key, w_query, w_out.T, w_value)], axis=2)
+    ffn_in = jnp.concatenate([by_z(m) for m in (w_gate, w_up, w_down.T)], axis=2)
+    rows_dev = ffn_in.shape[1]
 
     items_all = block_item.reshape(SPLIT, lanes, blocks_dev)
     grp_items = jnp.repeat(
@@ -187,97 +1303,95 @@
     cond_low = (cond_pre * cond_sig).astype(BF)
     text_rows = w_ckey.shape[0]
     text_local = lax.dynamic_slice_in_dim(caption, rank * text_rows, text_rows, 1)
-    modulation = lax.psum(bdot(cond_low, w_ada), "sp") + b_ada
-    cap_part = jnp.stack([by_z(bdot(text_local, w_ckey)), by_z(bdot(text_local, w_cvalue))], 1)
-    cap_raw = sum_g(scatter_z(cap_part))
-    ckey_hat, ckey_recip = normed_pair(cap_raw[0].reshape(text_count, heads, HEAD))
+    cap_part = jnp.concatenate(
+        [by_z(bdot(text_local, w_ckey)), by_z(bdot(text_local, w_cvalue))], axis=2
+    ).astype(BF)
+    cap_part = cap_part.reshape(SPLIT, 2, 2, text_count // lanes, 2 * wq).transpose(2, 1, 0, 3, 4)
 
     def per_head(vector):
         return lax.dynamic_slice_in_dim(vector, my_z * wq, wq, 0).reshape(heads, HEAD)
 
     gain_query, gain_key, gain_ckey = per_head(g_query), per_head(g_key), per_head(g_ckey)
     gate_tanh = jnp.tanh(lax.dynamic_slice_in_dim(cross_gate, my_z * heads, heads, 0))
-    cap_keys = (ckey_hat * gain_ckey).astype(BF)
-    cap_values = cap_raw[1].astype(BF).reshape(text_count, heads, HEAD)
-
     def of_items(rows, items):
         return jnp.where(items[:, None] == 0, rows[0], rows[1])
 
+    group_rows = SPLIT * tok_rows
+
+    row = lambda vector: vector.reshape(1, -1)
+    lane = jnp.arange(2 * HEAD)
+    freqs = FREQ_BASE ** (-(lane % (HEAD // 4)).astype(F32) / (HEAD // 4))
+    att = attention_call(
+        own_part(patches),
+        bdot(cond_low, w_ada),
+        row(b_ada),
+        jnp.pad(positions.astype(F32), ((0, 6), (0, 0))),
+        row(freqs),
+        cap_part,
+        qkvo_in,
+        ffn_in,
+        grp_items[:, None],
+        row(key_items),
+        row(g_attn_in),
+        jnp.concatenate([row(gain_key), row(gain_query)], axis=1),
+        jnp.concatenate([row(gain_ckey), jnp.ones((1, wq), F32)], axis=1),
+        row(jnp.repeat(gate_tanh, HEAD)),
+    )
+    attn_branch = att["branch"]
+    modulation = att["mod"]
+    ffn_w = att["ffn"].reshape(width, -1)
+    f_gate, f_up, f_down = (ffn_w[:, i * wf : (i + 1) * wf] for i in range(3))
+    qkvo = att["qkvo"].reshape(width, -1)
+    f_key, f_query, f_out, f_value = (qkvo[:, i * wq : (i + 1) * wq] for i in range(4))
+    norm_in = att["norm_in"].reshape(group_rows, width)
+    split_heads = (group_rows, heads, HEAD)
+    queries = att["queries"].reshape(split_heads)
+    all_keys, all_values = (att[n].reshape(-1, heads, HEAD) for n in ("k_all", "v_all"))
+    kq_hat = att["kq_hat"].reshape(group_rows, 2, heads, HEAD)
+    kq_recip = att["kq_recip"].reshape(group_rows, 2, heads, HEAD)
+    key_hat, query_hat = kq_hat[:, 0], kq_hat[:, 1]
+    key_recip, query_recip = kq_recip[:, 0], kq_recip[:, 1]
+    attn_self, attn_cross = (att[n].reshape(split_heads) for n in ("attn_self", "attn_cross"))
+    mixed = att["mixed"]
+    cap_keys, cap_values = (att[n].reshape(text_count, heads, HEAD) for n in ("cap_k", "cap_v"))
+    ckey_hat, ckey_recip = (
+        gather_g(att[n][:, :wq]).reshape(text_count, heads, HEAD) for n in ("cap_hat", "cap_recip")
+    )
+    log_total = att["totals"][:, :heads].T
+    cross_log = att["totals"][:, heads : 2 * heads].T
+    cos64, sin64 = (att[n].reshape(group_rows, 2 * HEAD)[:, None, :HEAD] for n in ("cos", "sin"))
+    quarter = HEAD // 4
+    cos_row, cos_col = cos64[..., :quarter], cos64[..., 2 * quarter : 3 * quarter]
+    sin_row, sin_col = sin64[..., quarter : 2 * quarter], sin64[..., 3 * quarter :]
     mod_own = of_items(modulation, own_items)
-    scale_attn, gate_attn, scale_ffn, gate_ffn = (
-        mod_own[:, i * width : (i + 1) * width] for i in range(4)
-    )
-    group_rows = SPLIT * tok_rows
-
-    patch_f = own_part(patches).astype(F32)
-    grad_out = own_part(out_grad).astype(F32)
-    hat_one, recip_one = normed_pair(patch_f)
+    scale_attn = mod_own[:, :width]
+    hat_one, recip_one = normed_pair(own_part(patches).astype(F32))
     factor_one = g_attn_in * (1.0 + scale_attn)
-    norm_in = gather_tokens((hat_one * factor_one).astype(BF))
-    pos_all = gather_z(positions).transpose(1, 0, 2).reshape(2, group_rows)
-    cos_row, sin_row, cos_col, sin_col = angles(pos_all)
-    split_heads = (group_rows, heads, HEAD)
-    query_raw = bdot(norm_in, f_query).reshape(split_heads)
-    key_raw = bdot(norm_in, f_key).reshape(split_heads)
-    values_low = bdot(norm_in, f_value).astype(BF)
-    query_hat, query_recip = normed_pair(query_raw)
-    queries = rotate(query_hat * gain_query, cos_row, sin_row, cos_col, sin_col).astype(BF)
-    key_hat, key_recip = normed_pair(key_raw)
-    keys_low = rotate(key_hat * gain_key, cos_row, sin_row, cos_col, sin_col).astype(BF)
-    all_keys, all_values = (
-        gather_g(block).reshape(lanes * group_rows, heads, HEAD)
-        for block in (keys_low.reshape(group_rows, wq), values_low)
-    )
     same = (grp_items[:, None] == key_items[None, :])[None]
     scores = jnp.einsum("qhd,khd->hqk", queries, all_keys, preferred_element_type=F32) * scale
-    scores = jnp.where(same, scores, NEG)
-    exps = jnp.exp(scores - jnp.max(scores, axis=-1, keepdims=True))
-    probs = exps / jnp.sum(exps, axis=-1, keepdims=True)
+    probs = jnp.where(same, jnp.exp(scores - log_total[..., None]), 0.0)
     probs_low = probs.astype(BF)
-    attn_self = jnp.einsum("hqk,khd->qhd", probs_low, all_values, preferred_element_type=F32)
     cross_scores = (
         jnp.einsum("qhd,khd->hqk", queries, cap_keys, preferred_element_type=F32) * scale
     )
-    cross_exp = jnp.exp(cross_scores - jnp.max(cross_scores, axis=-1, keepdims=True))
-    cross_probs = cross_exp / jnp.sum(cross_exp, axis=-1, keepdims=True)
+    cross_probs = jnp.exp(cross_scores - cross_log[..., None])
     cross_low = cross_probs.astype(BF)
-    attn_cross = jnp.einsum("hqk,khd->qhd", cross_low, cap_values, preferred_element_type=F32)
-    mixed = (attn_self + gate_tanh[None, :, None] * attn_cross).astype(BF).reshape(group_rows, wq)
-    attn_branch = scatter_tokens(dot_t(mixed, f_out))
-
-    hat_two, recip_two = normed_pair(attn_branch)
-    tanh_one = jnp.tanh(gate_attn)
-    resid = patch_f + tanh_one * hat_two * g_attn_out
-    hat_three, recip_three = normed_pair(resid)
-    factor_three = g_ffn_in * (1.0 + scale_ffn)
-    norm_ffn = gather_tokens((hat_three * factor_three).astype(BF))
-    gate_val = bdot(norm_ffn, f_gate)
-    up_val = bdot(norm_ffn, f_up)
-    gate_sig = jax.nn.sigmoid(gate_val)
-    hidden = (gate_val * gate_sig * up_val).astype(BF)
-    ffn_branch = scatter_tokens(dot_t(hidden, f_down))
-    hat_four, recip_four = normed_pair(ffn_branch)
-    tanh_two = jnp.tanh(gate_ffn)
-    output = resid + tanh_two * hat_four * g_ffn_out
-
-    grad_gate_ffn = grad_out * hat_four * g_ffn_out * (1.0 - tanh_two * tanh_two)
-    grad_four = grad_out * tanh_two
-    grad_g_ffn_out = jnp.sum(grad_four * hat_four, axis=0)
-    grad_ffn = gather_tokens(
-        normed_back(grad_four * g_ffn_out, hat_four, recip_four).astype(BF)
-    )
-    grad_hidden = bdot(grad_ffn, f_down)
-    grad_gate = (grad_hidden * up_val * gate_sig * (1.0 + gate_val * (1.0 - gate_sig))).astype(BF)
-    grad_up = (grad_hidden * gate_val * gate_sig).astype(BF)
-    grad_norm_ffn = scatter_tokens(dot_t(grad_gate, f_gate) + dot_t(grad_up, f_up))
-    grad_scale_ffn = grad_norm_ffn * hat_three * g_ffn_in
-    grad_g_ffn_in = jnp.sum(grad_norm_ffn * hat_three * (1.0 + scale_ffn), axis=0)
-    grad_resid = grad_out + normed_back(grad_norm_ffn * factor_three, hat_three, recip_three)
-
-    grad_gate_attn = grad_resid * hat_two * g_attn_out * (1.0 - tanh_one * tanh_one)
-    grad_two = grad_resid * tanh_one
-    grad_g_attn_out = jnp.sum(grad_two * hat_two, axis=0)
-    grad_attn = gather_tokens(normed_back(grad_two * g_attn_out, hat_two, recip_two).astype(BF))
+
+    output, grad_resid, grad_attn, ffn_sums, ffn_grads = ffn_call(
+        attn_branch,
+        own_part(patches),
+        own_part(out_grad),
+        modulation,
+        own_items[:, None],
+        row(g_attn_out),
+        row(g_ffn_in),
+        row(g_ffn_out),
+        f_gate,
+        f_up,
+        f_down,
+    )
+
+    grad_attn = gather_tokens(grad_attn)
     grad_mixed = bdot(grad_attn, f_out).astype(BF).reshape(split_heads)
     grad_mixed_f = grad_mixed.astype(F32)
     grad_cross_gate = jnp.sum(grad_mixed_f * attn_cross, axis=(0, 2)) * (
@@ -334,12 +1448,10 @@
             t_dot(norm_in, grad_key_raw),
             t_dot(norm_in, grad_values),
             t_dot(grad_attn, mixed),
-            t_dot(norm_ffn, grad_gate),
-            t_dot(norm_ffn, grad_up),
-            t_dot(grad_ffn, hidden),
         ],
         axis=1,
     ).astype(BF)
+    grad_merged = jnp.concatenate([grad_merged, ffn_grads], axis=1)
     grad_merged = grad_merged.reshape(SPLIT, lanes, rows_dev, -1).transpose(1, 0, 2, 3)
     shard_grads = turn_z(scatter_g(grad_merged)).astype(F32)
     (shard_query, shard_key, shard_value, shard_out, shard_gate, shard_up, shard_down) = (
@@ -347,32 +1459,12 @@
         for i in range(7)
     )
 
+    scale_sums = jnp.stack(item_sums(grad_scale_attn, own_items[:, None])).reshape(ITEMS, width)
+    mod_sums = jnp.concatenate(
+        [scale_sums, ffn_sums[4:6], ffn_sums[6:8], ffn_sums[8:10]], axis=1
+    )
     token_sums = lax.psum(
-        (
-            jnp.stack(
-                [
-                    jnp.concatenate(
-                        [
-                            jnp.sum(
-                                jnp.where((own_items == item)[:, None], block, 0.0), axis=0
-                            )
-                            for block in (
-                                grad_scale_attn,
-                                grad_gate_attn,
-                                grad_scale_ffn,
-                                grad_gate_ffn,
-                            )
-                        ]
-                    )
-                    for item in range(ITEMS)
-                ]
-            ),
-            grad_g_attn_in,
-            grad_g_attn_out,
-            grad_g_ffn_in,
-            grad_g_ffn_out,
-        ),
-        ("sp", "tp"),
+        (mod_sums, grad_g_attn_in, ffn_sums[0], ffn_sums[1], ffn_sums[2]), ("sp", "tp")
     )
     head_sums = jnp.concatenate([grad_g_query, grad_g_key, grad_cross_gate])
     head_sums = gather_z(sum_g(head_sums))
@@ -391,7 +1483,7 @@
     grad_cond_pre = grad_cond_act * cond_sig * (1.0 + cond_pre * (1.0 - cond_sig))
     grad_band_table = jnp.dot(band_hot.T, grad_cond_pre, precision=HIGH)
     return (
-        lax.all_gather(output, "tp", axis=0, tiled=True),
+        output.reshape(tok_rows, width),
         lax.all_gather(grad_patches, "tp", axis=0, tiled=True),
         shard_query,
         shard_key,
@@ -417,6 +1509,8 @@
 
 
 def solution(mesh):
+    lanes = mesh.shape["sp"] // SPLIT
+    body = local if lanes == 4 and mesh.shape["tp"] == 2 else local_any
     in_specs = (
         P("sp", None),
         P(),
@@ -469,4 +1563,4 @@
         P("tp"),
         P(None, "sp"),
     )
-    return jax.shard_map(local, mesh=mesh, in_specs=in_specs, out_specs=out_specs, check_vma=False)
+    return jax.shard_map(body, mesh=mesh, in_specs=in_specs, out_specs=out_specs, check_vma=False)

time: 1140 us -> 843 us (0.74)
  waiting for transfers between devices: 638 us -> 239 us
  Pallas kernels: 0 us -> 254 us
  blocking collectives: 195 us -> 93.8 us
  matrix products: 106 us -> 64.9 us
  local copies, waits for them, and re-layouts: 115 us -> 135 us
  other arithmetic: 42.8 us -> 28.9 us
    pallas_call x0 -> x2, Pallas kernels: none -> 254 us  [the longest x1 139 us: attention_call(): pl.pallas_call(attention_kernel, out_shape=tuple(outs.values()), in_specs...]
    all_gather x4 -> x1, waiting for transfers between devices: 139 us -> 7.04 us  [gather_z(): lax.all_gather(block, 'sp', axis_index_groups=along_z, axis=0, tiled=False)]
    unnamed x21 -> x8, waiting for transfers between devices: 157 us -> 44 us
    reduce_scatter x4 -> x1, waiting for transfers between devices: 108 us -> 31.2 us  [scatter_z(): lax.psum_scatter(block, 'sp', axis_index_groups=along_z, scatter_dimensio...]
    reduce_scatter x4 -> x1, waiting for transfers between devices: 75 us -> 0.02 us  [scatter_tokens(): mine = lax.psum_scatter(part, 'tp', scatter_dimension=1, tiled=False)]
    psum x1 -> x0, blocking collectives: 60.1 us -> none  [local(): modulation = lax.psum(bdot(cond_low, w_ada), 'sp') + b_ada]
    all_gather x4 -> x1, blocking collectives: 25.8 us -> 6.79 us  [gather_tokens(): both = lax.all_gather(own, 'tp', axis=0, tiled=True)]
    dot_general x7 -> x0, local copies, waits for them, and re-layouts: 14.4 us -> none  [the longest x4 10.7 us: t_dot(): lax.dot_general(left, right, (((0,), (0,)), ((), ())), preferred_element_...]
  transfers between devices with their start and end apart: 21 -> 8, of which waited for: 16 -> 6; matrix products, arithmetic and copies ran while one was open for 9% -> 13% of each run, Pallas kernels for 0% -> 0%
where the time goes in v2:
time: 843 us; the launch traced here: 835 us
  Pallas kernels  254 us (30%)
  waiting for transfers between devices  239 us (28%)
  local copies, waits for them, and re-layouts  135 us (16%)
  blocking collectives  93.8 us (11%)
  matrix products  64.9 us (8%)
  other arithmetic  28.9 us (3%)
  between operations  15.1 us (2%)
    pallas_call x1, Pallas kernels, attention_call(): pl.pallas_call(attention_kernel, out_shape=tuple(outs.values()), in_specs...  139 us
    psum x1, waiting for transfers between devices, local(): lax.psum((mod_sums, grad_g_attn_in, ffn_sums[0], ffn_sums[1], ffn_sums[2]...  130 us
    pallas_call x1, Pallas kernels, ffn_call(): pl.pallas_call(ffn_kernel, out_shape=(shape((2, rows, width), F32), shape...  115 us
    unnamed x8, waiting for transfers between devices  44 us
    all_gather x3, blocking collectives, gather_z(): lax.all_gather(block, 'sp', axis_index_groups=along_z, axis=0, tiled=False)  37.6 us
    reduce_scatter x1, waiting for transfers between devices, scatter_z(): lax.psum_scatter(block, 'sp', axis_index_groups=along_z, scatter_dimensio...  31.2 us
    reduce_scatter x2, waiting for transfers between devices, scatter_g(): lax.psum_scatter(block, 'sp', axis_index_groups=along_g, scatter_dimensio...  27.1 us
    psum x1, blocking collectives, sum_g(): return lax.psum(block, 'sp', axis_index_groups=along_g)  23.3 us
  transfers between devices with their start and end apart: 8, of which 6 were waited for; matrix products, arithmetic and copies ran while one was open for 13% of the time, Pallas kernels for 0%

profile of v2, /device:TPU:0, one launch (start us, length us, event | category | flops | bytes accessed | tf_op | source)
XLA Modules:
  0.0 835.4 jit_solution(15167240985703860224)
XLA Ops:
  49.2 139.2 %attention.1 = (f32[64,1536]{1,0:T(8,128)}, bf16[4,128,1536]{2,1,0:T(8,128)(2,1)}, bf16[16,96,768]{2,1,0:T(8,128)(2,1)}, bf16[16,96,1536]{2,1,0:T(8,128)(2,1)}, ...) custom-call(bf16[64,1536]{1,0:T(8,128)(2,1)} %get-tuple-element.94.p, ...), custom_call_target="tpu_custom_call" | custom-call | tf_op jit(solution)/shard_map/attention/pallas_call | solution.py:818
  188.4 4.7 fusion.85
  193.1 114.7 %feed_forward.1 = (f32[2,64,1536]{2,1,0:T(8,128)}, f32[64,1536]{1,0:T(8,128)}, bf16[64,1536]{1,0:T(8,128)(2,1)}, f32[16,1536]{1,0:T(8,128)}, bf16[1536,1536]{1,0:T(8,128)(2,1)}) custom-call(f32[64,1536]{1,0:T(8,128)} %get-tuple-element.47.branch, bf16[64,1536]{1,0:T(8,128)(2,1)} %get-tuple-element.94.patches, ...), custom_call_target="tpu_custom_call" | custom-call | tf_op jit(solution)/shard_map/feed_forward/pallas_call | solution.py:366
  307.8 6.8 all_gather.39
  335.8 6.3 fusion.91
  342.2 7.0 all-gather.8.cloned.1.call-done
  349.2 3.6 multiply_reduce_fusion.1
  355.0 7.5 fusion.10
  364.2 4.6 multiply_convert_fusion
  388.4 5.8 fusion.16
  396.1 10.1 %reduce-scatter.8.cloned.1.call-done = bf16[1,512,192]{1,2,0:T(8,128)(2,1)} async-done(((bf16[4,512,192]{1,2,0:T(8,128)(2,1)}), bf16[1,512,192]{1,2,0:T(8,128)(2,1)}) %reduce-scatter.8.cloned.1.call-update) | async-done | bytes 196624 | tf_op jit(solution)/shard_map/reduce_scatter | solution.py:1257
  415.8 17.0 %reduce-scatter.10.cloned.1.call-done = bf16[1,512,192]{1,2,0:T(8,128)(2,1)} async-done(((bf16[4,512,192]{1,2,0:T(8,128)(2,1)}), bf16[1,512,192]{1,2,0:T(8,128)(2,1)}) %reduce-scatter.10.cloned.1.call-update) | async-done | bytes 196624 | tf_op jit(solution)/shard_map/reduce_scatter | solution.py:1257
  457.4 11.7 %concatenate.94 = bf16[1536,2304]{1,0:T(8,128)(2,1)} concatenate(bf16[1536,192]{1,0:T(8,128)(2,1)} %copy.327, bf16[1536,192]{1,0:T(8,128)(2,1)} %copy.328, bf16[1536,192]{1,0:T(8,128)(2,1)} %copy.329, bf16[1536,192]{1,0:T(8,128)(2,1)S(1)} %copy.330, bf16[1536,1536]{1,0:T(8,128)(2,1)} %get-tuple-element.67), dimensions={1} | concatenate | bytes 14155776 | tf_op jit(solution)/shard_map/concatenate | solution.py:1454
  470.8 6.2 all-gather.2
  478.1 8.1 all-gather.1
  498.1 23.3 %all-reduce.12 = (bf16[256,3,64]{0,2,1:T(8,128)(2,1)S(1)}, bf16[256,3,64]{0,2,1:T(8,128)(2,1)S(1)}, f32[1,387]{1,0:T(1,128)S(1)}) all-reduce(f32[256,3,64]{0,2,1:T(8,128)} %convolution_bitcast_fusion, f32[256,3,64]{0,2,1:T(8,128)S(1)} %fusion.17, ...), channel_id=1, replica_groups={{0,2,4,6},{8,10,12,14},{16,18,20,22},{24,26,28,30},{1,3,5,7},{9,11,13,1..., use_global_device_ids=true, to_apply=%region_13.14 | all-reduce | flops 98691 | bytes 592920 | tf_op jit(solution)/shard_map/psum | solution.py:1267
  521.4 11.9 %all-gather.4 = f32[4,1,387]{2,1,0:T(1,128)S(1)} all-gather(f32[1,1,387]{2,1,0:T(1,128)S(1)} %bitcast.326), channel_id=1, replica_groups={{0,8,16,24},{2,10,18,26},{4,12,20,28},{6,14,22,30},{1,9,17,25},{3,11,19..., dimensions={0}, use_global_device_ids=true | all-gather | bytes 7740 | tf_op jit(solution)/shard_map/all_gather | solution.py:1246
  536.6 9.4 %all-gather.5 = f32[4,1,192]{2,1,0:T(1,128)S(1)} all-gather(f32[1,1,192]{2,1,0:T(1,128)S(1)} %reshape.508), channel_id=1, replica_groups={{0,8,16,24},{2,10,18,26},{4,12,20,28},{6,14,22,30},{1,9,17,25},{3,11,19..., dimensions={0}, use_global_device_ids=true | all-gather | bytes 3840 | tf_op jit(solution)/shard_map/all_gather | solution.py:1246
  546.7 16.4 %all-gather.3 = bf16[8,256,192]{1,2,0:T(8,128)(2,1)S(1)} all-gather(bf16[2,256,192]{1,2,0:T(8,128)(2,1)S(1)} %pad_maximum_fusion.5), channel_id=5, replica_groups={{0,8,16,24},{2,10,18,26},{4,12,20,28},{6,14,22,30},{1,9,17,25},{3,11,19..., dimensions={0}, use_global_device_ids=true | all-gather | bytes 983040 | tf_op jit(solution)/shard_map/all_gather | solution.py:1246
  565.5 43.8 %all-reduce.9.cloned.1.call-done = bf16[4,4,96,2304]{3,2,0,1:T(8,128)(2,1)} async-done(((bf16[4,4,96,2304]{3,2,0,1:T(8,128)(2,1)}), bf16[4,4,96,2304]{3,2,0,1:T(8,128)(2,1)}) %all-reduce.9.cloned.1.call-update) | async-done | bytes 7077904
  612.9 4.7 all-to-all-start
  617.6 31.2 %reduce-scatter.14.cloned.1.call-done = bf16[1,64,1536]{2,1,0:T(8,128)(2,1)} async-done(((bf16[4,64,1536]{2,1,0:T(8,128)(2,1)}), bf16[1,64,1536]{2,1,0:T(8,128)(2,1)}) %reduce-scatter.14.cloned.1.call-update) | async-done | bytes 196624 | tf_op jit(solution)/shard_map/reduce_scatter | solution.py:1252
  653.4 11.9 %all_gather.42 = f32[128,1536]{1,0:T(8,128)} all-gather(f32[64,1536]{1,0:T(8,128)S(1)} %fusion.30), channel_id=1, replica_groups=mesh['sp'=16,'tp'=2] {'tp'}, dimensions={0}, use_global_device_ids=true | all-gather | bytes 1179648 | tf_op jit(solution)/shard_map/all_gather | solution.py:1487
  665.2 129.7 %all-reduce.11.cloned.1.call-done = (f32[2,6144]{1,0:T(2,128)}, f32[1536]{0:T(1024)}, f32[1536]{0:T(1024)}, f32[1536]{0:T(1024)}, f32[1536]{0:T(1024)}) async-done(((f32[2,6144]{1,0:T(2,128)}, f32[1536]{0:T(1024)}, f32[1536]{0:T(1024)}, f32[1536]{0:T(1024)}, f32[1536]{0:T(1024)}), (f32[2,6144]{1,0:T(2,128)}, f32[1536]{0:T(1024)}, f32[1536]{0:T(1024)}, f32[1536]{0:T(1024)}, ...) | async-done | bytes 73744 | tf_op jit(solution)/shard_map/psum | solution.py:1466
  (306 shorter events, 184.8 us)
Async XLA Ops:
  7.2 26.3 %copy-start = (bf16[256,4096]{1,0:T(8,128)(2,1)S(1)}, bf16[256,4096]{1,0:T(8,128)(2,1)}, u32[]{:S(2)}) copy-start(bf16[256,4096]{1,0:T(8,128)(2,1)} %param.27) | copy-start | bytes 6291460
  7.2 26.2 %copy-start.22 = (bf16[256,768]{1,0:T(8,128)(2,1)S(1)}, bf16[256,768]{1,0:T(8,128)(2,1)}, u32[]{:S(2)}) copy-start(bf16[256,768]{1,0:T(8,128)(2,1)} %param.40) | copy-start | bytes 1179652
  7.2 342.0 %all-gather.8.cloned.1.call-start = ((), (), s32[]{:S(2)}) async-start(), calls=%async_computation.9 | async-start | bytes 1966080 | tf_op jit(solution)/shard_map/all_gather | solution.py:1246
  10.4 29.3 %copy-start.39 = (f32[192]{0:T(256)}, f32[192]{0:T(256)S(1)}, u32[]{:S(2)}) copy-start(f32[192]{0:T(256)S(1)} %dynamic_slice.37) | copy-start | bytes 2308
  11.2 303.5 %copy-start.37 = (f32[192]{0:T(256)}, f32[192]{0:T(256)S(1)}, u32[]{:S(2)}) copy-start(f32[192]{0:T(256)S(1)} %dynamic_slice.36) | copy-start | bytes 2308
  193.1 121.7 %copy-start.40 = (f32[192]{0:T(256)S(1)}, f32[192]{0:T(256)}, u32[]{:S(2)}) copy-start(f32[192]{0:T(256)} %copy-done.39) | copy-start | bytes 2308
  193.1 121.8 %copy-start.26 = (s32[64,32]{1,0:T(8,128)S(1)}, s32[64,32]{1,0:T(8,128)}, u32[]{:S(2)}) copy-start(s32[64,32]{1,0:T(8,128)} %copy-done.25) | copy-start | bytes 24580
  193.1 121.9 %copy-start.32 = (bf16[256,192]{1,0:T(8,128)(2,1)S(1)}, bf16[256,192]{1,0:T(8,128)(2,1)}, u32[]{:S(2)}) copy-start(bf16[256,192]{1,0:T(8,128)(2,1)} %get-tuple-element.53) | copy-start | bytes 294916
  193.1 122.0 %copy-start.31 = (bf16[256,192]{1,0:T(8,128)(2,1)S(1)}, bf16[256,192]{1,0:T(8,128)(2,1)}, u32[]{:S(2)}) copy-start(bf16[256,192]{1,0:T(8,128)(2,1)} %get-tuple-element.58) | copy-start | bytes 294916
  193.1 122.1 %copy-start.28 = (bf16[512,192]{1,0:T(8,128)(2,1)S(1)}, bf16[512,192]{1,0:T(8,128)(2,1)}, u32[]{:S(2)}) copy-start(bf16[512,192]{1,0:T(8,128)(2,1)} %get-tuple-element.54) | copy-start | bytes 589828
  314.6 91.6 %reduce-scatter.8.cloned.1.call-start = ((), (), s32[]{:S(2)}) async-start(), calls=%async_computation.5 | async-start | bytes 983040 | tf_op jit(solution)/shard_map/reduce_scatter | solution.py:1257
  383.9 48.9 %reduce-scatter.10.cloned.1.call-start = ((), (), s32[]{:S(2)}) async-start(), calls=%async_computation.6 | async-start | bytes 983040 | tf_op jit(solution)/shard_map/reduce_scatter | solution.py:1257
  394.2 140.2 %reduce-scatter.12.cloned.1.call-start = ((), (), s32[]{:S(2)}) async-start(), calls=%async_computation.7 | async-start | bytes 2359296 | tf_op jit(solution)/shard_map/reduce_scatter | solution.py:1275
  437.2 172.1 %all-reduce.9.cloned.1.call-start = ((), (), s32[]{:S(2)}) async-start(), calls=%async_computation.10 | async-start | bytes 14155776
  469.1 28.3 %copy-start.5 = (bf16[3,512,256]{1,2,0:T(8,128)(2,1)S(1)}, bf16[3,512,256]{1,2,0:T(8,128)(2,1)}, u32[]{:S(2)}) copy-start(bf16[3,512,256]{1,2,0:T(8,128)(2,1)} %copy-done.4) | copy-start | bytes 2359300
  469.1 179.7 %reduce-scatter.14.cloned.1.call-start = ((), (), s32[]{:S(2)}) async-start(), calls=%async_computation.8 | async-start | bytes 983040 | tf_op jit(solution)/shard_map/reduce_scatter | solution.py:1252
  486.2 47.0 %copy-start.36 = (f32[3,64]{1,0:T(4,128)S(1)}, f32[3,64]{1,0:T(4,128)}, u32[]{:S(2)}) copy-start(f32[3,64]{1,0:T(4,128)} %mul.482) | copy-start | bytes 2308
  490.4 158.4 %copy-start.50 = (pred[64]{0:T(512)(128)(4,1)}, pred[64]{0:T(512)(128)(4,1)S(1)}, u32[]{:S(2)}) copy-start(pred[64]{0:T(512)(128)(4,1)S(1)} %get-tuple-element.141) | copy-start | bytes 196
  612.9 35.9 %copy-start.7 = (bf16[64,1536]{1,0:T(8,128)(2,1)S(1)}, bf16[64,1536]{1,0:T(8,128)(2,1)}, u32[]{:S(2)}) copy-start(bf16[64,1536]{1,0:T(8,128)(2,1)} %get-tuple-element.94.patches) | copy-start | bytes 589828
  612.9 35.9 %copy-start.34 = (f32[1536]{0:T(1024)S(1)}, f32[1536]{0:T(1024)}, u32[]{:S(2)}) copy-start(f32[1536]{0:T(1024)} %param.44) | copy-start | bytes 18436
  612.9 39.3 %copy-start.20 = (f32[64,1536]{1,0:T(8,128)S(1)}, f32[64,1536]{1,0:T(8,128)}, u32[]{:S(2)}) copy-start(f32[64,1536]{1,0:T(8,128)} %get-tuple-element.51) | copy-start | bytes 1179652
  612.9 189.3 %all-to-all-start = ((bf16[4,96,2304]{2,1,0:T(8,128)(2,1)}), bf16[4,96,2304]{2,1,0:T(8,128)(2,1)}, u32[]{:S(2)}, u32[]{:S(2)}) async-start(bf16[4,96,2304]{2,1,0:T(8,128)(2,1)} %dynamic-slice_bitcast_fusion), calls=%async_computation.4 | async-start | bytes 3538944 | tf_op jit(solution)/shard_map/all_to_all | solution.py:1262
  617.6 178.8 %copy-start.18 = (bf16[64,6144]{1,0:T(8,128)(2,1)S(1)}, bf16[64,6144]{1,0:T(8,128)(2,1)}, u32[]{:S(2)}) copy-start(bf16[64,6144]{1,0:T(8,128)(2,1)} %param.42) | copy-start | bytes 2359300
  617.6 177.3 %all-reduce.11.cloned.1.call-start = ((), (), s32[]{:S(2)}) async-start(), calls=%async_computation.11 | async-start | bytes 163840 | tf_op jit(solution)/shard_map/psum | solution.py:1466
  (40 other events, 245.7 us)
Sparse Core Ops, SparseCore 0:
  314.7 34.4 all-gather.7
  384.0 22.1 reduce-scatter.7
  409.5 23.2 reduce-scatter.9
  437.3 26.0 reduce-scatter.11
  469.2 140.0 all-reduce.8
  611.6 37.1 reduce-scatter.13
  658.0 136.8 all-reduce.10

commit v3 on v2

--- a/solution.py
+++ b/solution.py
@@ -322,18 +322,21 @@
     back.pass_on()
 
     hid = w_gate.shape[1]
-    step = 256
+    block_rows = grad_w.shape[3]
+    step = 4 * block_rows
 
     def weights(i, carry):
         cols = pl.ds(pl.multiple_of(i * step, step), step)
-        left = n_buf[:, :, cols].reshape(SPLIT * 2 * rows, step)
-        grad_w[cols, 0:hid] = t_dot(left, gg_s[...].reshape(-1, hid)).astype(BF)
-        grad_w[cols, hid : 2 * hid] = t_dot(left, gu_s[...].reshape(-1, hid)).astype(BF)
-        left = g_buf[:, :, cols].reshape(SPLIT * 2 * rows, step)
-        grad_w[cols, 2 * hid : 3 * hid] = t_dot(left, hid_s[...].reshape(-1, hid)).astype(BF)
+        norm = n_buf[:, :, cols].reshape(SPLIT * 2 * rows, step)
+        grad = g_buf[:, :, cols].reshape(SPLIT * 2 * rows, step)
+        for j, (left, right) in enumerate(((norm, gg_s), (norm, gu_s), (grad, hid_s))):
+            block = t_dot(left, right[...].reshape(-1, hid)).astype(BF)
+            block = block.reshape(4, block_rows, hid)
+            for g in range(4):
+                grad_w[g % 2, g // 2, i, :, j * hid : (j + 1) * hid] = block[g]
         return carry
 
-    lax.fori_loop(0, width // step, weights, 0)
+    lax.fori_loop(0, SPLIT, weights, 0)
 
     grad_norm = back.finish()
     scale_sums = item_sums(grad_norm * hat_three * gain_in[...], item)
@@ -370,7 +373,7 @@
             shape((rows, width), F32),
             shape((rows, width), BF),
             shape((16, width), F32),
-            shape((width, 3 * hid), BF),
+            shape((2, 2, SPLIT, width // (4 * SPLIT), 3 * hid), BF),
         ),
         in_specs=[vmem] * 11,
         out_specs=[vmem] * 5,
@@ -857,6 +860,378 @@
     return dict(zip(outs, results))
 
 
+class TurnZ:
+    def __init__(self, place, out, land, send, recv):
+        self.place, self.out, self.land = place, out, land
+        self.sends = [
+            remote(
+                out.at[place.z_to(d)], land.at[place.z], send.at[i], recv.at[i], place.z_peer[d]
+            )
+            for i, d in enumerate(NEAR)
+        ]
+        self.landed = []
+        for i, d in enumerate(NEAR):
+            slot = land.at[place.z_from(d)]
+            self.landed.append(remote(slot, slot, send.at[i], recv.at[i], place.z_peer[d]))
+
+    def start(self):
+        for copy in self.sends:
+            copy.start()
+        self.land[self.place.z] = self.out[self.place.z]
+
+    def finish(self):
+        for copy in self.landed:
+            copy.wait_recv()
+        for copy in self.sends:
+            copy.wait_send()
+
+
+class SpreadZ:
+    def __init__(self, place, buf, send, recv):
+        own = buf.at[place.z]
+        self.own = own
+        self.sends = [
+            remote(own, own, send.at[i], recv.at[i], place.z_peer[d]) for i, d in enumerate(NEAR)
+        ]
+        self.landed = []
+        for i, d in enumerate(NEAR):
+            slot = buf.at[place.z_from(d)]
+            self.landed.append(remote(slot, slot, send.at[i], recv.at[i], place.z_peer[d]))
+
+    def start(self):
+        for copy in self.sends:
+            copy.start()
+
+    def finish(self):
+        for copy in self.landed:
+            copy.wait_recv()
+        for copy in self.sends:
+            copy.wait_send()
+
+
+def backward_kernel(
+    patches, grad_resid, grad_attn, ffn_sums, ffn_part,
+    norm_in, qkvo, mod, queries, k_all, v_all, kq_hat, kq_recip, cos_t, sin_t, totals,
+    attn_self, attn_cross, mixed, cap_k, cap_v, cap_hat, cap_recip, text,
+    items, grp_items, key_items, gain_in, gain_kq, gain_ckey, gate_row,
+    d_patches, d_query, d_key, d_value, d_out, d_gate, d_up, d_down, d_ckey, d_cvalue,
+    early_out, late_out, head_out,
+    g_buf, g_send, g_recv,
+    e_acc, e_land, e_slots, e_send, e_recv, l_acc, l_land, l_slots, l_send, l_recv,
+    h_acc, h_land, h_slots, h_send, h_recv,
+    f_fc, f_acc, f_fy, f_s, f_r, f_out, f_land, fz_s, fz_r,
+    w_part, w_fc, w_acc, w_fy, w_s, w_r, w_out, w_land, wz_s, wz_r,
+    t_part, t_fc, t_acc, t_fy, t_s, t_r, t_z, tz_s, tz_r, t_all, ta_s, ta_r,
+    kv_part, kv_fc, kv_acc, kv_fy, kv_s, kv_r, kv_sum,
+    dk_acc, dv_acc, dq_s, dkq_s, ov_s, mix_s, dck_acc, dcv_acc,
+    p1, fx1, tz1, fz1, s1, r1, out_send, out_recv,
+):
+    place = Place()
+    rows, width = patches.shape
+    wq = queries.shape[1]
+    heads = wq // HEAD
+    both = 2 * rows
+    scale = 1.0 / math.sqrt(HEAD)
+    enter([place.x_peer, place.c_peer, place.y_peer] + [place.z_peer[d] for d in (1, 2, 3)])
+    ffn = LaneScatter(place, ffn_part, f_fc, f_acc, f_fy, f_s, f_r)
+    grads = Gather(place, g_buf, g_send, g_recv)
+    grads.own[...] = grad_attn[...]
+    grads.start()
+    early = AllSum(place, e_acc, e_land, e_slots, e_send, e_recv, True)
+    e_acc[0] = ffn_sums[...]
+    early.start()
+    ffn.start()
+    mean = segments(2 * wq)
+    mean_q = segments(wq)
+    lane = lax.broadcasted_iota(jnp.int32, (1, 2 * wq), 1)
+    dk_acc[...] = jnp.zeros_like(dk_acc)
+    dv_acc[...] = jnp.zeros_like(dv_acc)
+    dck_acc[...] = jnp.zeros_like(dck_acc)
+    dcv_acc[...] = jnp.zeros_like(dcv_acc)
+    early.step(0)
+    early.step(1)
+    grads.pass_on()
+    early.step(2)
+    ffn.step()
+    grads.finish()
+    gates = gate_row[...]
+
+    def attend(i, gate_sum):
+        at = pl.ds(pl.multiple_of(i * both, both), both)
+        block = g_buf[pl.ds(i * 2, 2)].reshape(both, width)
+        d_mix = bdot(block, qkvo[:, :, 2 * wq : 4 * wq].reshape(width, 2 * wq))[:, :wq].astype(BF)
+        mix_f = d_mix.astype(F32)
+        d_cross = (gates * mix_f).astype(BF)
+        delta = head_mean(mix_f * attn_self[at], mean_q) * HEAD
+        gate_sum = gate_sum + jnp.sum(mix_f * attn_cross[at], axis=0, keepdims=True)
+        query = (queries[at].astype(F32) * scale).astype(BF)
+        logs = totals[at]
+        same = grp_items[at] == key_items[...]
+        dq = jnp.zeros((both, wq), F32)
+        for head in range(heads):
+            query_h = of_head(query, head)
+            cross_h = of_head(d_cross, head)
+            probs = jnp.exp(dot_t(query_h, cap_k[...]) - logs[:, heads + head : heads + head + 1])
+            d_probs = dot_t(cross_h, cap_v[...])
+            inner = jnp.sum(probs * d_probs, axis=1, keepdims=True)
+            d_scores = (probs * (d_probs - inner)).astype(BF)
+            part = bdot(d_scores, cap_k[...])
+            dck_acc[...] += t_dot(d_scores, query_h)
+            dcv_acc[...] += t_dot(probs.astype(BF), cross_h)
+            mix_h = of_head(d_mix, head)
+            scores = jnp.where(same, dot_t(query_h, k_all[...]), NEG)
+            probs = jnp.exp(scores - logs[:, head : head + 1])
+            d_probs = dot_t(mix_h, v_all[...])
+            d_scores = (probs * (d_probs - delta[:, head * HEAD : head * HEAD + 1])).astype(BF)
+            part = part + bdot(d_scores, k_all[...])
+            dq = dq + of_head(part, head)
+            dk_acc[...] += t_dot(d_scores, query_h)
+            dv_acc[...] += t_dot(probs.astype(BF), mix_h)
+        dq = (dq * scale).astype(BF).astype(F32)
+        dq_s[at] = jnp.concatenate([jnp.zeros_like(dq), dq], axis=1)
+        mix_s[at] = jnp.concatenate([mixed[at], jnp.zeros_like(mixed[at])], axis=1)
+        return gate_sum
+
+    gate_sum = lax.fori_loop(0, SPLIT, attend, jnp.zeros((1, wq), F32))
+
+    keys = LaneScatter(place, kv_part, kv_fc, kv_acc, kv_fy, kv_s, kv_r)
+    owned = SPLIT * both
+    for g in range(4):
+        at = slice(g * owned, (g + 1) * owned)
+        kv_part[g % 2, g // 2] = jnp.concatenate([dk_acc[at], dv_acc[at]], axis=1).astype(BF)
+    keys.start()
+    words = cap_hat.shape[0]
+    caption = LaneScatter(place, t_part, t_fc, t_acc, t_fy, t_s, t_r)
+    for g in range(4):
+        at = slice(g * words, (g + 1) * words)
+        t_part[g % 2, g // 2] = jnp.concatenate([dck_acc[at], dcv_acc[at]], axis=1).astype(BF)
+    caption.start()
+    f_out[...] = ffn.finish().astype(BF)
+    turn_f = TurnZ(place, f_out, f_land, fz_s, fz_r)
+    turn_f.start()
+    keys.step()
+    caption.step()
+    d_cap = caption.finish()
+    d_cap_low = d_cap.astype(BF).astype(F32)
+    cap_gain = jnp.where(lane < wq, gain_ckey[...], 0.0)
+    gck_sum = jnp.sum(jnp.where(lane < wq, d_cap_low * cap_hat[...], 0.0), axis=0, keepdims=True)
+    hat = cap_hat[...]
+    d_hat = d_cap_low * cap_gain
+    d_raw = cap_recip[...] * (d_hat - hat * head_mean(d_hat * hat, mean))
+    cap_spread = SpreadZ(place, t_z, tz_s, tz_r)
+    cap_spread.own[...] = jnp.where(lane < wq, d_raw, d_cap).astype(BF)
+    cap_spread.start()
+    kv_sum[...] = keys.finish().astype(BF).reshape(kv_sum.shape)
+
+    def raw(i, head_sum):
+        at = pl.ds(pl.multiple_of(i * both, both), both)
+        total = kv_sum[at].astype(F32)
+        d_kq = jnp.where(lane < wq, total, dq_s[at])
+        cos = jnp.concatenate([cos_t[i]] * heads, axis=1)
+        sin = jnp.concatenate([sin_t[i]] * heads, axis=1)
+        d_norm = d_kq * cos - swap_quarters(d_kq) * sin
+        hat = kq_hat[i]
+        head_sum = head_sum + jnp.sum(d_norm * hat, axis=0, keepdims=True)
+        d_hat = d_norm * gain_kq[...]
+        d_kq = (kq_recip[i] * (d_hat - hat * head_mean(d_hat * hat, mean))).astype(BF)
+        dkq_s[at] = d_kq
+        d_ov = jnp.where(lane < wq, 0.0, total).astype(BF)
+        ov_s[at] = d_ov
+        p1[i] = (
+            (
+                dot_t(d_kq, qkvo[:, :, 0 : 2 * wq].reshape(width, 2 * wq))
+                + dot_t(d_ov, qkvo[:, :, 2 * wq : 4 * wq].reshape(width, 2 * wq))
+            )
+            .astype(BF)
+            .reshape(2, rows, width)
+        )
+        return head_sum
+
+    head_sum = lax.fori_loop(0, SPLIT, raw, jnp.zeros((1, 2 * wq), F32))
+    back = Scatter(place, p1, fx1, tz1, fz1, s1, r1)
+    for i in range(4):
+        back.send_x(i)
+    heads_sum = AllSum(place, h_acc, h_land, h_slots, h_send, h_recv, False)
+    h_acc[0] = jnp.zeros(h_acc.shape[1:], F32)
+    h_acc[0, 0:1] = head_sum
+    h_acc[0, 1:2] = gck_sum
+    h_acc[0, 2:3] = jnp.concatenate([gate_sum, jnp.zeros_like(gate_sum)], axis=1)
+    heads_sum.start()
+
+    block_rows = qkvo.shape[1]
+    step = 4 * block_rows
+
+    def matrices(i, carry):
+        cols = pl.ds(pl.multiple_of(i * step, step), step)
+        left = norm_in[:, :, cols].reshape(SPLIT * both, step)
+        above = g_buf[:, :, cols].reshape(SPLIT * both, step)
+        d_kq = t_dot(left, dkq_s[...]).astype(BF).reshape(4, block_rows, 2 * wq)
+        d_ov = t_dot(left, ov_s[...]) + t_dot(above, mix_s[...])
+        d_ov = d_ov.astype(BF).reshape(4, block_rows, 2 * wq)
+        for g in range(4):
+            w_part[g % 2, g // 2, i, :, 0 : 2 * wq] = d_kq[g]
+            w_part[g % 2, g // 2, i, :, 2 * wq : 4 * wq] = d_ov[g]
+        return carry
+
+    back.pass_on()
+    lax.fori_loop(0, SPLIT, matrices, 0)
+    attn = LaneScatter(place, w_part, w_fc, w_acc, w_fy, w_s, w_r)
+    attn.start()
+    cap_spread.finish()
+    cap_all = LaneGather(place, t_all, ta_s, ta_r)
+    cap_all.own[...] = t_z[...]
+    cap_all.start()
+    heads_sum.step(0)
+    heads_sum.step(1)
+    attn.step()
+    cap_all.pass_on()
+
+    item = items[...]
+    d_norm = back.finish()
+    hat, recip = normed_pair(patches[...].astype(F32))
+    factor = 1.0 + item_rows(mod, item, 0, width)
+    scale_sums = item_sums(d_norm * hat * gain_in[...], item)
+    late = AllSum(place, l_acc, l_land, l_slots, l_send, l_recv, True)
+    l_acc[0] = jnp.zeros(l_acc.shape[1:], F32)
+    l_acc[0, 0:1] = jnp.sum(d_norm * hat * factor, axis=0, keepdims=True)
+    l_acc[0, 1:2] = scale_sums[0]
+    l_acc[0, 2:3] = scale_sums[1]
+    late.start()
+    d_patches[place.x] = grad_resid[...] + normed_back(d_norm * gain_in[...] * factor, hat, recip)
+    own_d = d_patches.at[place.x]
+    out_copy = remote(own_d, own_d, out_send, out_recv, place.x_peer)
+    out_copy.start()
+    late.step(0)
+    w_out[...] = attn.finish().astype(BF)
+    turn_w = TurnZ(place, w_out, w_land, wz_s, wz_r)
+    turn_w.start()
+    late.step(1)
+    late.step(2)
+    turn_f.finish()
+    wf = f_land.shape[2] // 3
+    for z in range(SPLIT):
+        at = slice(z * wf, (z + 1) * wf)
+        d_gate[:, at] = f_land[z, :, 0:wf].astype(F32)
+        d_up[:, at] = f_land[z, :, wf : 2 * wf].astype(F32)
+        d_down[at] = f_land[z, :, 2 * wf : 3 * wf].astype(F32).T
+    cap_all.finish()
+    for z in range(SPLIT):
+        at = slice(z * wq, (z + 1) * wq)
+        d_cap = t_dot(text[...], t_all[:, z].reshape(4 * words, 2 * wq))
+        d_ckey[:, at] = d_cap[:, :wq]
+        d_cvalue[:, at] = d_cap[:, wq:]
+    early_out[...] = early.finish()
+    heads_sum.finish()
+    head_out[...] = h_slots[...]
+    late_out[...] = late.finish()
+    turn_w.finish()
+    for z in range(SPLIT):
+        at = slice(z * wq, (z + 1) * wq)
+        d_key[:, at] = w_land[z, :, 0:wq].astype(F32)
+        d_query[:, at] = w_land[z, :, wq : 2 * wq].astype(F32)
+        d_out[at] = w_land[z, :, 2 * wq : 3 * wq].astype(F32).T
+        d_value[:, at] = w_land[z, :, 3 * wq : 4 * wq].astype(F32)
+    other = d_patches.at[1 - place.x]
+    remote(other, other, out_send, out_recv, place.x_peer).wait_recv()
+    out_copy.wait_send()
+
+
+def backward_call(
+    patches, grad_resid, grad_attn, ffn_sums, ffn_part, att, text,
+    items, grp_items, key_items, gain_in, gain_kq, gain_ckey, gate_row,
+):
+    rows, width = patches.shape
+    names = (
+        "norm_in", "qkvo", "mod", "queries", "k_all", "v_all", "kq_hat", "kq_recip", "cos", "sin",
+        "totals", "attn_self", "attn_cross", "mixed", "cap_k", "cap_v", "cap_hat", "cap_recip",
+    )
+    group, wq = att["queries"].shape
+    lanes = group // rows // 2
+    lanes = att["qkvo"].shape[0] // SPLIT
+    row_dev = att["qkvo"].shape[1]
+    words = att["cap_hat"].shape[0]
+    wf = ffn_part.shape[4] // 3
+    vmem = pl.BlockSpec(memory_space=pltpu.VMEM)
+    shape = jax.ShapeDtypeStruct
+    dma = pltpu.SemaphoreType.DMA
+    tile = pltpu.VMEM
+
+    def all_sum(size, steps):
+        return [
+            tile((steps,) + size, F32), tile((steps,) + size, F32), tile((SPLIT,) + size, F32),
+            dma((6,)), dma((6,)),
+        ]
+
+    def lane_scatter(size):
+        return [tile((2,) + size, BF), tile((2,) + size, BF), tile(size, BF), dma((2,)), dma((2,))]
+
+    def turn_z(size):
+        return [tile(size, BF), tile(size, BF), dma((3,)), dma((3,))]
+
+    ffn_size = ffn_part.shape[2:]
+    attn_size = (SPLIT, row_dev, 4 * wq)
+    cap_size = (words, 2 * wq)
+    kv_size = (group, 2 * wq)
+    outs = (
+        shape((2, rows, width), F32),
+        shape((row_dev, SPLIT * wq), F32),
+        shape((row_dev, SPLIT * wq), F32),
+        shape((row_dev, SPLIT * wq), F32),
+        shape((SPLIT * wq, row_dev), F32),
+        shape((row_dev, SPLIT * wf), F32),
+        shape((row_dev, SPLIT * wf), F32),
+        shape((SPLIT * wf, row_dev), F32),
+        shape((text.shape[1], SPLIT * wq), F32),
+        shape((text.shape[1], SPLIT * wq), F32),
+        shape(ffn_sums.shape, F32),
+        shape((8, width), F32),
+        shape((SPLIT, 8, 2 * wq), F32),
+    )
+    args = (
+        [patches, grad_resid, grad_attn, ffn_sums, ffn_part]
+        + [att[name] for name in names]
+        + [text, items, grp_items, key_items, gain_in, gain_kq, gain_ckey, gate_row]
+    )
+    return pl.pallas_call(
+        backward_kernel,
+        out_shape=outs,
+        in_specs=[vmem] * len(args),
+        out_specs=[vmem] * len(outs),
+        scratch_shapes=gather_scratch(rows, width)
+        + all_sum(ffn_sums.shape, 3)
+        + all_sum((8, width), 3)
+        + all_sum((8, 2 * wq), 2)
+        + lane_scatter(ffn_size)
+        + turn_z(ffn_size)
+        + [tile((2, 2) + attn_size, BF)]
+        + lane_scatter(attn_size)
+        + turn_z(attn_size)
+        + [tile((2, 2) + cap_size, BF)]
+        + lane_scatter(cap_size)
+        + [tile((SPLIT,) + cap_size, BF), dma((3,)), dma((3,))]
+        + [tile((lanes, SPLIT) + cap_size, BF), dma((3,)), dma((3,))]
+        + [tile((2, 2) + kv_size, BF)]
+        + lane_scatter(kv_size)
+        + [tile(kv_size, BF)]
+        + [
+            tile((lanes * group, wq), F32),
+            tile((lanes * group, wq), F32),
+            tile((group, 2 * wq), F32),
+            tile((group, 2 * wq), BF),
+            tile((group, 2 * wq), BF),
+            tile((group, 2 * wq), BF),
+            tile((lanes * words, wq), F32),
+            tile((lanes * words, wq), F32),
+        ]
+        + scatter_scratch(rows, width)
+        + [dma, dma],
+        compiler_params=pltpu.CompilerParams(
+            collective_id=3, has_side_effects=True, vmem_limit_bytes=VMEM_LIMIT
+        ),
+        name="attention_backward",
+    )(*args)
+
+
 def local_any(
     patches,
     caption,
@@ -1242,39 +1617,6 @@
     sizes = (wq, wq, wq, wq, wf, wf, wf)
     starts = [sum(sizes[:i]) for i in range(8)]
 
-    def gather_z(block):
-        return lax.all_gather(block, "sp", axis_index_groups=along_z, axis=0, tiled=False)
-
-    def gather_g(block):
-        return lax.all_gather(block, "sp", axis_index_groups=along_g, axis=0, tiled=False)
-
-    def scatter_z(block):
-        return lax.psum_scatter(
-            block, "sp", axis_index_groups=along_z, scatter_dimension=0, tiled=False
-        )
-
-    def scatter_g(block):
-        return lax.psum_scatter(
-            block, "sp", axis_index_groups=along_g, scatter_dimension=0, tiled=False
-        )
-
-    def turn_z(block):
-        return lax.all_to_all(
-            block, "sp", 0, 0, axis_index_groups=along_z, tiled=True
-        )
-
-    def sum_g(block):
-        return lax.psum(block, "sp", axis_index_groups=along_g)
-
-    def gather_tokens(own):
-        both = lax.all_gather(own, "tp", axis=0, tiled=True)
-        return gather_z(both).reshape(SPLIT * tok_rows, -1)
-
-    def scatter_tokens(part):
-        part = part.astype(BF).reshape(SPLIT, halves, own_rows, width)
-        mine = lax.psum_scatter(part, "tp", scatter_dimension=1, tiled=False)
-        return scatter_z(mine.astype(BF)).astype(F32)
-
     def by_z(block):
         rows, cols = block.shape
         return block.reshape(rows, SPLIT, cols // SPLIT).transpose(1, 0, 2)
@@ -1321,6 +1663,9 @@
     row = lambda vector: vector.reshape(1, -1)
     lane = jnp.arange(2 * HEAD)
     freqs = FREQ_BASE ** (-(lane % (HEAD // 4)).astype(F32) / (HEAD // 4))
+    gain_kq_row = jnp.concatenate([row(gain_key), row(gain_query)], axis=1)
+    gain_ckey_row = jnp.concatenate([row(gain_ckey), jnp.ones((1, wq), F32)], axis=1)
+    gate_tanh_row = row(jnp.repeat(gate_tanh, HEAD))
     att = attention_call(
         own_part(patches),
         bdot(cond_low, w_ada),
@@ -1333,51 +1678,16 @@
         grp_items[:, None],
         row(key_items),
         row(g_attn_in),
-        jnp.concatenate([row(gain_key), row(gain_query)], axis=1),
-        jnp.concatenate([row(gain_ckey), jnp.ones((1, wq), F32)], axis=1),
-        row(jnp.repeat(gate_tanh, HEAD)),
+        gain_kq_row,
+        gain_ckey_row,
+        gate_tanh_row,
     )
     attn_branch = att["branch"]
     modulation = att["mod"]
     ffn_w = att["ffn"].reshape(width, -1)
     f_gate, f_up, f_down = (ffn_w[:, i * wf : (i + 1) * wf] for i in range(3))
-    qkvo = att["qkvo"].reshape(width, -1)
-    f_key, f_query, f_out, f_value = (qkvo[:, i * wq : (i + 1) * wq] for i in range(4))
-    norm_in = att["norm_in"].reshape(group_rows, width)
-    split_heads = (group_rows, heads, HEAD)
-    queries = att["queries"].reshape(split_heads)
-    all_keys, all_values = (att[n].reshape(-1, heads, HEAD) for n in ("k_all", "v_all"))
-    kq_hat = att["kq_hat"].reshape(group_rows, 2, heads, HEAD)
-    kq_recip = att["kq_recip"].reshape(group_rows, 2, heads, HEAD)
-    key_hat, query_hat = kq_hat[:, 0], kq_hat[:, 1]
-    key_recip, query_recip = kq_recip[:, 0], kq_recip[:, 1]
-    attn_self, attn_cross = (att[n].reshape(split_heads) for n in ("attn_self", "attn_cross"))
-    mixed = att["mixed"]
-    cap_keys, cap_values = (att[n].reshape(text_count, heads, HEAD) for n in ("cap_k", "cap_v"))
-    ckey_hat, ckey_recip = (
-        gather_g(att[n][:, :wq]).reshape(text_count, heads, HEAD) for n in ("cap_hat", "cap_recip")
-    )
-    log_total = att["totals"][:, :heads].T
-    cross_log = att["totals"][:, heads : 2 * heads].T
-    cos64, sin64 = (att[n].reshape(group_rows, 2 * HEAD)[:, None, :HEAD] for n in ("cos", "sin"))
-    quarter = HEAD // 4
-    cos_row, cos_col = cos64[..., :quarter], cos64[..., 2 * quarter : 3 * quarter]
-    sin_row, sin_col = sin64[..., quarter : 2 * quarter], sin64[..., 3 * quarter :]
-    mod_own = of_items(modulation, own_items)
-    scale_attn = mod_own[:, :width]
-    hat_one, recip_one = normed_pair(own_part(patches).astype(F32))
-    factor_one = g_attn_in * (1.0 + scale_attn)
-    same = (grp_items[:, None] == key_items[None, :])[None]
-    scores = jnp.einsum("qhd,khd->hqk", queries, all_keys, preferred_element_type=F32) * scale
-    probs = jnp.where(same, jnp.exp(scores - log_total[..., None]), 0.0)
-    probs_low = probs.astype(BF)
-    cross_scores = (
-        jnp.einsum("qhd,khd->hqk", queries, cap_keys, preferred_element_type=F32) * scale
-    )
-    cross_probs = jnp.exp(cross_scores - cross_log[..., None])
-    cross_low = cross_probs.astype(BF)
-
-    output, grad_resid, grad_attn, ffn_sums, ffn_grads = ffn_call(
+
+    output, grad_resid, grad_attn, ffn_sums, ffn_part = ffn_call(
         attn_branch,
         own_part(patches),
         own_part(out_grad),
@@ -1391,92 +1701,32 @@
         f_down,
     )
 
-    grad_attn = gather_tokens(grad_attn)
-    grad_mixed = bdot(grad_attn, f_out).astype(BF).reshape(split_heads)
-    grad_mixed_f = grad_mixed.astype(F32)
-    grad_cross_gate = jnp.sum(grad_mixed_f * attn_cross, axis=(0, 2)) * (
-        1.0 - gate_tanh * gate_tanh
-    )
-    grad_cross = (gate_tanh[None, :, None] * grad_mixed_f).astype(BF)
-    grad_cprobs = jnp.einsum("qhd,khd->hqk", grad_cross, cap_values, preferred_element_type=F32)
-    grad_cscores = (
-        cross_probs * (grad_cprobs - jnp.sum(cross_probs * grad_cprobs, axis=-1, keepdims=True))
-    ).astype(BF)
-    query_grad = jnp.einsum("hqk,khd->qhd", grad_cscores, cap_keys, preferred_element_type=F32)
-    grad_ckeys_part = (
-        jnp.einsum("hqk,qhd->khd", grad_cscores, queries, preferred_element_type=F32) * scale
-    )
-    grad_cvals_part = jnp.einsum(
-        "hqk,qhd->khd", cross_low, grad_cross, preferred_element_type=F32
-    )
-    row_delta = jnp.sum(grad_mixed_f * attn_self, axis=-1).T
-    grad_probs = jnp.einsum("qhd,khd->hqk", grad_mixed, all_values, preferred_element_type=F32)
-    grad_scores = (probs * (grad_probs - row_delta[..., None])).astype(BF)
-    query_grad = query_grad + jnp.einsum(
-        "hqk,khd->qhd", grad_scores, all_keys, preferred_element_type=F32
-    )
-    key_part = (
-        jnp.einsum("hqk,qhd->khd", grad_scores, queries, preferred_element_type=F32) * scale
-    )
-    value_part = jnp.einsum("hqk,qhd->khd", probs_low, grad_mixed, preferred_element_type=F32)
-    key_grad, value_grad = (
-        scatter_g(block.astype(BF).reshape(lanes, group_rows, wq)) for block in (key_part, value_part)
-    )
-    grad_queries = (query_grad * scale).astype(BF).astype(F32)
-    grad_qnorm = rotate(grad_queries, cos_row, -sin_row, cos_col, -sin_col)
-    grad_g_query = jnp.sum(grad_qnorm * query_hat, axis=0).reshape(-1)
-    grad_query_raw = (
-        normed_back(grad_qnorm * gain_query, query_hat, query_recip).astype(BF).reshape(-1, wq)
-    )
-    grad_keys = key_grad.astype(F32).reshape(split_heads)
-    grad_knorm = rotate(grad_keys, cos_row, -sin_row, cos_col, -sin_col)
-    grad_g_key = jnp.sum(grad_knorm * key_hat, axis=0).reshape(-1)
-    grad_key_raw = (
-        normed_back(grad_knorm * gain_key, key_hat, key_recip).astype(BF).reshape(-1, wq)
-    )
-    grad_values = value_grad.astype(BF)
-    grad_norm_in = scatter_tokens(
-        dot_t(grad_query_raw, f_query) + dot_t(grad_key_raw, f_key) + dot_t(grad_values, f_value)
-    )
-    grad_scale_attn = grad_norm_in * hat_one * g_attn_in
-    grad_g_attn_in = jnp.sum(grad_norm_in * hat_one * (1.0 + scale_attn), axis=0)
-    grad_patches = grad_resid + normed_back(grad_norm_in * factor_one, hat_one, recip_one)
-
-    grad_merged = jnp.concatenate(
-        [
-            t_dot(norm_in, grad_query_raw),
-            t_dot(norm_in, grad_key_raw),
-            t_dot(norm_in, grad_values),
-            t_dot(grad_attn, mixed),
-        ],
-        axis=1,
-    ).astype(BF)
-    grad_merged = jnp.concatenate([grad_merged, ffn_grads], axis=1)
-    grad_merged = grad_merged.reshape(SPLIT, lanes, rows_dev, -1).transpose(1, 0, 2, 3)
-    shard_grads = turn_z(scatter_g(grad_merged)).astype(F32)
-    (shard_query, shard_key, shard_value, shard_out, shard_gate, shard_up, shard_down) = (
-        shard_grads[:, :, starts[i] : starts[i + 1]].transpose(1, 0, 2).reshape(rows_dev, -1)
-        for i in range(7)
-    )
-
-    scale_sums = jnp.stack(item_sums(grad_scale_attn, own_items[:, None])).reshape(ITEMS, width)
-    mod_sums = jnp.concatenate(
-        [scale_sums, ffn_sums[4:6], ffn_sums[6:8], ffn_sums[8:10]], axis=1
-    )
-    token_sums = lax.psum(
-        (mod_sums, grad_g_attn_in, ffn_sums[0], ffn_sums[1], ffn_sums[2]), ("sp", "tp")
-    )
-    head_sums = jnp.concatenate([grad_g_query, grad_g_key, grad_cross_gate])
-    head_sums = gather_z(sum_g(head_sums))
-    grad_ckeys = sum_g(grad_ckeys_part).astype(BF).astype(F32)
-    grad_cvals = sum_g(grad_cvals_part).astype(BF).reshape(text_count, wq)
-    grad_g_ckey = gather_z(jnp.sum(grad_ckeys * ckey_hat, axis=0).reshape(-1)).reshape(-1)
-    grad_ckey_raw = (
-        normed_back(grad_ckeys * gain_ckey, ckey_hat, ckey_recip).astype(BF).reshape(text_count, wq)
-    )
-    cap_grads = gather_z(jnp.stack([grad_ckey_raw, grad_cvals])).transpose(1, 2, 0, 3)
-    cap_grads = cap_grads.reshape(2, text_count, SPLIT * wq)
-    grad_mod = token_sums[0]
+    (
+        grad_patches, shard_query, shard_key, shard_value, shard_out, shard_gate, shard_up,
+        shard_down, grad_w_ckey, grad_w_cvalue, early, late, head_rows,
+    ) = backward_call(
+        own_part(patches),
+        grad_resid,
+        grad_attn,
+        ffn_sums,
+        ffn_part,
+        att,
+        text_local,
+        own_items[:, None],
+        grp_items[:, None],
+        row(key_items),
+        row(g_attn_in),
+        gain_kq_row,
+        gain_ckey_row,
+        gate_tanh_row,
+    )
+    grad_mod = jnp.concatenate([late[1:3], early[4:6], early[6:8], early[8:10]], axis=1)
+    grad_g_query = head_rows[:, 0, wq:].reshape(-1)
+    grad_g_key = head_rows[:, 0, :wq].reshape(-1)
+    grad_g_ckey = head_rows[:, 1, :wq].reshape(-1)
+    grad_cross_gate = jnp.sum(head_rows[:, 2, :wq].reshape(-1, HEAD), axis=1)
+    all_tanh = jnp.tanh(cross_gate)
+    grad_cross_gate = grad_cross_gate * (1.0 - all_tanh * all_tanh)
     grad_b_ada = jnp.sum(grad_mod, axis=0)
     grad_w_ada = jnp.dot(cond_low.astype(F32).T, grad_mod, precision=HIGH)
     grad_cond_act = jnp.dot(grad_mod, w_ada.astype(F32).T, precision=HIGH)
@@ -1484,26 +1734,26 @@
     grad_band_table = jnp.dot(band_hot.T, grad_cond_pre, precision=HIGH)
     return (
         output.reshape(tok_rows, width),
-        lax.all_gather(grad_patches, "tp", axis=0, tiled=True),
+        grad_patches.reshape(tok_rows, width),
         shard_query,
         shard_key,
         shard_value,
-        shard_out.T,
+        shard_out,
         shard_gate,
         shard_up,
-        shard_down.T,
-        t_dot(text_local, cap_grads[0]),
-        t_dot(text_local, cap_grads[1]),
+        shard_down,
+        grad_w_ckey,
+        grad_w_cvalue,
         grad_w_ada,
         grad_b_ada,
-        token_sums[1],
-        token_sums[2],
-        token_sums[3],
-        token_sums[4],
-        head_sums[:, :wq].reshape(-1),
-        head_sums[:, wq : 2 * wq].reshape(-1),
+        late[0],
+        early[0],
+        early[1],
+        early[2],
+        grad_g_query,
+        grad_g_key,
         grad_g_ckey,
-        head_sums[:, 2 * wq :].reshape(-1),
+        grad_cross_gate,
         grad_band_table,
     )
 

time: 843 us -> 438 us (0.52)
  waiting for transfers between devices: 239 us -> 0 us
  Pallas kernels: 254 us -> 384 us
  local copies, waits for them, and re-layouts: 135 us -> 39.1 us
  blocking collectives: 93.8 us -> 0 us
  matrix products: 64.9 us -> 7 us
  other arithmetic: 28.9 us -> 5.87 us
  between operations: 15.1 us -> 1 us
    pallas_call x0 -> x1, Pallas kernels: none -> 130 us  [backward_call(): pl.pallas_call(backward_kernel, out_shape=outs, in_specs=[vmem] * len(arg...]
    psum x1 -> x0, waiting for transfers between devices: 130 us -> none  [local(): lax.psum((mod_sums, grad_g_attn_in, ffn_sums[0], ffn_sums[1], ffn_sums[2]...]
    all_gather x7 -> x0, blocking collectives: 70.6 us -> none  [the longest x3 37.6 us: gather_z(): lax.all_gather(block, 'sp', axis_index_groups=along_z, axis=0, tiled=False)]
    reduce_scatter x4 -> x0, waiting for transfers between devices: 58.3 us -> none  [the longest x1 31.2 us: scatter_z(): lax.psum_scatter(block, 'sp', axis_index_groups=along_z, scatter_dimensio...]
    dot_general x19 -> x0, matrix products: 51 us -> none  [the longest x6 13.8 us: t_dot(): lax.dot_general(left, right, (((0,), (0,)), ((), ())), preferred_element_...]
    unnamed x8 -> x0, waiting for transfers between devices: 44 us -> none
    reshape x20 -> x0, local copies, waits for them, and re-layouts: 30 us -> none  [the longest x7 11.9 us: local(): shard_grads[:, :, starts[i]:starts[i + 1]].transpose(1, 0, 2)]
    psum x1 -> x0, blocking collectives: 23.3 us -> none  [sum_g(): return lax.psum(block, 'sp', axis_index_groups=along_g)]
  transfers between devices with their start and end apart: 8 -> 0, of which waited for: 6 -> 0; matrix products, arithmetic and copies ran while one was open for 13% -> 0% of each run, Pallas kernels for 0% -> 0%
where the time goes in v3:
time: 438 us; the launch traced here: 437 us
  Pallas kernels  384 us (88%)
  local copies, waits for them, and re-layouts  39.1 us (9%)
  matrix products  7 us (2%)
  other arithmetic  5.87 us (1%)
    pallas_call x1, Pallas kernels, attention_call(): pl.pallas_call(attention_kernel, out_shape=tuple(outs.values()), in_specs...  139 us
    pallas_call x1, Pallas kernels, backward_call(): pl.pallas_call(backward_kernel, out_shape=outs, in_specs=[vmem] * len(arg...  130 us
    pallas_call x1, Pallas kernels, ffn_call(): pl.pallas_call(ffn_kernel, out_shape=(shape((2, rows, width), F32), shape...  115 us
    unnamed x65, local copies, waits for them, and re-layouts  13.2 us

profile of v3, /device:TPU:0, one launch (start us, length us, event | category | flops | bytes accessed | tf_op | source)
XLA Modules:
  0.0 437.3 jit_solution(5055435680971852204)
XLA Ops:
  0.7 1.9 constant_dynamic-slice_fusion
  2.6 0.9 fusion.2
  3.5 2.0 fusion.10.mod_in
  8.1 1.2 copy_bitcast_fusion.cap_in
  9.8 1.2 reshape.156
  10.9 1.1 reshape.155
  12.1 1.1 pad_maximum_fusion.2.qkvo_in
  13.3 1.1 pad_maximum_fusion.ffn_in
  14.7 1.0 broadcast_in_dim_reshape.5.grp_items
  21.5 139.1 %attention.1 = (f32[64,1536]{1,0:T(8,128)}, bf16[4,128,1536]{2,1,0:T(8,128)(2,1)}, bf16[16,96,768]{2,1,0:T(8,128)(2,1)}, bf16[16,96,1536]{2,1,0:T(8,128)(2,1)}, ...) custom-call(bf16[64,1536]{1,0:T(8,128)(2,1)} %get-tuple-element.156., ...), custom_call_target="tpu_custom_call" | custom-call | tf_op jit(solution)/shard_map/attention/pallas_call | solution.py:821
  163.4 4.7 %fusion.12 = (bf16[1536,512]{1,0:T(8,128)(2,1)}, bf16[1536,512]{1,0:T(8,128)(2,1)}, bf16[1536,512]{1,0:T(8,128)(2,1)}) fusion(bf16[1536,1536]{1,0:T(8,128)(2,1)} %bitcast.55), kind=kLoop, calls=%fused_computation.47 | loop fusion | bytes 9437184 | tf_op jit(solution)/shard_map/slice | solution.py:1688
  168.1 114.7 %feed_forward.1 = (f32[2,64,1536]{2,1,0:T(8,128)}, f32[64,1536]{1,0:T(8,128)}, bf16[64,1536]{1,0:T(8,128)(2,1)}, f32[16,1536]{1,0:T(8,128)}, bf16[2,2,4,96,1536]{4,3,2,1,0:T(8,128)(2,1)}) custom-call(f32[64,1536]{1,0:T(8,128)} %get-tuple-element.60.branch, bf16[64,1536]{1,0:T(8,128)(2,1)} %get-tuple-element.156.patches, ...), custom_call_target="tpu_custom_call" | custom-call | tf_op jit(solution)/shard_map/feed_forward/pallas_call | solution.py:369
  282.8 130.5 %attention_backward.1 = (f32[2,64,1536]{2,1,0:T(8,128)}, f32[96,768]{1,0:T(8,128)}, f32[96,768]{1,0:T(8,128)}, f32[96,768]{1,0:T(8,128)}, f32[768,96]{1,0:T(8,12...) custom-call(bf16[64,1536]{1,0:T(8,128)(2,1)} %get-tuple-element.156., ...), custom_call_target="tpu_custom_call" | custom-call | tf_op jit(solution)/shard_map/attention_backward/pallas_call | solution.py:1195
  413.3 1.9 copy.71
  415.2 2.5 copy.72
  418.5 2.0 fusion.9
  421.2 1.4 slice_reduce_fusion.3
  423.2 1.0 slice_reduce_fusion.4
  428.5 2.1 copy.95
  430.7 0.9 copy.96
  433.7 0.9 copy.100
  434.6 0.9 copy.101
  435.5 0.9 copy.102
  436.4 0.9 copy.103
  (110 shorter events, 20.6 us)
Async XLA Ops:
  0.7 6.0 %copy-start = (bf16[256,4096]{1,0:T(8,128)(2,1)S(1)}, bf16[256,4096]{1,0:T(8,128)(2,1)}, u32[]{:S(2)}) copy-start(bf16[256,4096]{1,0:T(8,128)(2,1)} %param.27) | copy-start | bytes 6291460
  0.7 4.9 %copy-start.23 = (s32[2,128]{1,0:T(2,128)S(1)}, s32[2,128]{1,0:T(2,128)}, u32[]{:S(2)}) copy-start(s32[2,128]{1,0:T(2,128)} %param.31) | copy-start | bytes 3076
  0.7 6.0 %copy-start.8 = (bf16[256,768]{1,0:T(8,128)(2,1)S(1)}, bf16[256,768]{1,0:T(8,128)(2,1)}, u32[]{:S(2)}) copy-start(bf16[256,768]{1,0:T(8,128)(2,1)} %param.41) | copy-start | bytes 1179652
  5.5 1.8 copy-start.9
  8.0 1.3 copy-start.16
  8.1 1.4 copy-start.17
  9.8 3.4 copy-start.11
  13.3 1.2 copy-start.24
  13.3 3.3 copy-start.19
  13.3 7.3 %copy-start.25 = (f32[12]{0:T(128)S(1)}, f32[12]{0:T(128)}, u32[]{:S(2)}) copy-start(f32[12]{0:T(128)} %param.51) | copy-start | bytes 148
  21.5 140.2 %copy-start.20 = (f32[1536]{0:T(1024)S(1)}, f32[1536]{0:T(1024)}, u32[]{:S(2)}) copy-start(f32[1536]{0:T(1024)} %param.45) | copy-start | bytes 18436
  21.5 140.8 %copy-start.21 = (f32[1536]{0:T(1024)S(1)}, f32[1536]{0:T(1024)}, u32[]{:S(2)}) copy-start(f32[1536]{0:T(1024)} %param.46) | copy-start | bytes 18436
  21.5 141.4 %copy-start.22 = (f32[1536]{0:T(1024)S(1)}, f32[1536]{0:T(1024)}, u32[]{:S(2)}) copy-start(f32[1536]{0:T(1024)} %param.47) | copy-start | bytes 18436
  413.2 4.4 %copy-start.18 = (f32[16,1536]{1,0:T(8,128)S(1)}, f32[16,1536]{1,0:T(8,128)}, u32[]{:S(2)}) copy-start(f32[16,1536]{1,0:T(8,128)} %get-tuple-element.96) | copy-start | bytes 294916
  415.2 11.8 %copy-start.1 = (bf16[64,6144]{1,0:T(8,128)(2,1)S(1)}, bf16[64,6144]{1,0:T(8,128)(2,1)}, u32[]{:S(2)}) copy-start(bf16[64,6144]{1,0:T(8,128)(2,1)} %param.42) | copy-start | bytes 2359300
  417.7 10.0 %copy-start.26 = (s32[2]{0:T(128)S(1)}, s32[2]{0:T(128)}, u32[]{:S(2)}) copy-start(s32[2]{0:T(128)} %param.30) | copy-start | bytes 28
  426.4 4.3 copy-start.7
  428.5 3.0 copy-start.15
  428.5 3.7 copy-start.14
  430.7 2.3 copy-start.13
  430.7 3.0 copy-start.6
  431.6 3.0 copy-start.5
  433.7 1.8 copy-start.4
  434.6 1.8 copy-start.3
  (3 other events, 3.3 us)

commit v4 on v1

--- a/solution.py
+++ b/solution.py
@@ -1,8 +1,12 @@
+import functools
 import math
+from types import SimpleNamespace
 
 import jax
 import jax.numpy as jnp
 from jax import lax
+from jax.experimental import pallas as pl
+from jax.experimental.pallas import tpu as pltpu
 from jax.sharding import PartitionSpec as P
 
 BANDS = 16
@@ -76,7 +80,1356 @@
     return lax.dot_general(left, right, (((0,), (0,)), ((), ())), preferred_element_type=F32)
 
 
-def local(
+MESH = pl.DeviceIdType.MESH
+VMEM_LIMIT = 63 * 2**20
+NEAR = (1, 3, 2)
+
+
+class Place:
+    def __init__(self):
+        rank = lax.axis_index("sp")
+        self.lanes = lax.axis_size("sp") // SPLIT
+        self.x = lax.axis_index("tp")
+        self.z = rank // self.lanes
+        self.g = rank % self.lanes
+        self.x_peer = (rank, 1 - self.x)
+        self.z_peer = {
+            d: (lax.rem(self.z + d, SPLIT) * self.lanes + self.g, self.x) for d in (1, 2, 3)
+        }
+        self.z_pair = self.at_z(self.z + 1 - 2 * lax.rem(self.z, 2))
+        self.z_far = self.z_peer[2]
+        self.y, self.c = self.g // 2, self.g % 2
+        self.g_y = (1 - self.y) * 2 + self.c
+        self.g_c = self.y * 2 + 1 - self.c
+        self.g_yc = (1 - self.y) * 2 + 1 - self.c
+        self.y_peer = (self.z * self.lanes + self.g_y, self.x)
+        self.c_peer = (self.z * self.lanes + self.g_c, self.x)
+
+    def z_from(self, d):
+        return lax.rem(self.z + SPLIT - d, SPLIT)
+
+    def z_to(self, d):
+        return lax.rem(self.z + d, SPLIT)
+
+
+    def block(self, i):
+        middle = lax.div(self.z * (3 - self.z), 2)
+        near = i + middle * (1 - 2 * i) * (1 - lax.div(i, 2))
+        return near + lax.div(self.z, 2) * (3 - 2 * near)
+
+    def at_z(self, z):
+        return (z * self.lanes + self.g, self.x)
+
+
+def remote(src, dst, send, recv, peer):
+    return pltpu.make_async_remote_copy(
+        src_ref=src, dst_ref=dst, send_sem=send, recv_sem=recv, device_id=peer, device_id_type=MESH
+    )
+
+
+def as_index(i):
+    return jnp.int32(i) if isinstance(i, int) else i
+
+
+class Gather:
+    def __init__(self, place, buf, send, recv):
+        self.place, self.buf, self.send, self.recv = place, buf, send, recv
+        self.own = buf.at[place.z * 2 + place.x]
+
+    def to_right(self, z):
+        place = self.place
+        block = self.buf.at[z * 2 + place.x]
+        steps = place.z - z
+        return remote(
+            block, block, self.send.at[steps], self.recv.at[3 + steps], place.at_z(place.z + 1)
+        )
+
+    def to_left(self, z):
+        place = self.place
+        block = self.buf.at[z * 2 + place.x]
+        steps = z - place.z
+        return remote(
+            block, block, self.send.at[3 + steps], self.recv.at[steps], place.at_z(place.z - 1)
+        )
+
+    def to_x(self, z):
+        block = self.buf.at[z * 2 + self.place.x]
+        return remote(
+            block, block, self.send.at[6 + z], self.recv.at[6 + z], self.place.x_peer
+        )
+
+    def landed(self, z, index):
+        block = self.buf.at[z * 2 + self.place.x]
+        return remote(block, block, self.send.at[index], self.recv.at[index], self.place.x_peer)
+
+    def start(self):
+        place = self.place
+
+        @pl.when(place.z < 3)
+        def _():
+            self.to_right(place.z).start()
+
+        @pl.when(place.z > 0)
+        def _():
+            self.to_left(place.z).start()
+
+        self.to_x(place.z).start()
+
+    def pass_on(self, i):
+        place = self.place
+        z = place.block(as_index(i))
+
+        @pl.when(z < place.z)
+        def _():
+            self.landed(z, 2 + place.z - z).wait_recv()
+
+            @pl.when(place.z < 3)
+            def _():
+                self.to_right(z).start()
+
+        @pl.when(z > place.z)
+        def _():
+            self.landed(z, z - place.z - 1).wait_recv()
+
+            @pl.when(place.z > 0)
+            def _():
+                self.to_left(z).start()
+
+        self.to_x(z).start()
+
+    def arrive(self, i):
+        z = self.place.block(as_index(i))
+        block = self.buf.at[z * 2 + 1 - self.place.x]
+        remote(
+            block, block, self.send.at[6 + z], self.recv.at[6 + z], self.place.x_peer
+        ).wait_recv()
+
+    def finish(self):
+        place = self.place
+        for z in range(SPLIT):
+
+            @pl.when((z <= place.z) & (place.z < 3))
+            def _():
+                self.to_right(z).wait_send()
+
+            @pl.when((z >= place.z) & (place.z > 0))
+            def _():
+                self.to_left(z).wait_send()
+
+            self.to_x(z).wait_send()
+
+
+class Scatter:
+    def __init__(self, place, part, from_x, from_z, send, recv):
+        self.place, self.part, self.from_x = place, part, from_x
+        self.from_z, self.send, self.recv = from_z, send, recv
+
+    def across(self, z):
+        return remote(
+            self.part.at[z, 1 - self.place.x],
+            self.from_x.at[z],
+            self.send.at[z],
+            self.recv.at[z],
+            self.place.x_peer,
+        )
+
+    def along(self, z):
+        return remote(
+            self.part.at[z, self.place.x],
+            self.from_z.at[self.place.z],
+            self.send.at[4 + z],
+            self.recv.at[4 + self.place.z],
+            self.place.at_z(z),
+        )
+
+    def pass_on(self, z):
+        self.across(z).wait_recv()
+        own = self.part[z, self.place.x].astype(F32)
+        self.part[z, self.place.x] = (own + self.from_x[z].astype(F32)).astype(BF)
+        self.along(z).start()
+
+    def finish(self):
+        place = self.place
+        self.across(place.z).wait_recv()
+        total = self.part[place.z, place.x].astype(F32) + self.from_x[place.z].astype(F32)
+        for d in (1, 2, 3):
+            z = place.z_to(d)
+            block = self.from_z.at[z]
+            remote(
+                block, block, self.send.at[4 + z], self.recv.at[4 + z], place.at_z(z)
+            ).wait_recv()
+            total = total + self.from_z[z].astype(F32)
+        for z in range(SPLIT):
+            self.across(z).wait_send()
+        for d in (1, 2, 3):
+            self.along(place.z_to(d)).wait_send()
+        return total
+
+
+def flow(place, gather, scatter, work, carry, between=None):
+    def order(i):
+        return place.block(i if gather is not None else 3 - i)
+
+    def step(i, carry):
+        if gather is not None:
+
+            @pl.when((i >= 1) & (i < 3))
+            def _():
+                gather.pass_on(i + 1)
+
+            gather.arrive(i)
+        if between is not None:
+            pl.when(i == 2)(between)
+        z = order(i)
+        carry = work(z, carry)
+        if scatter is not None:
+            scatter.across(z).start()
+        if gather is not None:
+
+            @pl.when(i == 0)
+            def _():
+                gather.pass_on(1)
+
+        if scatter is not None:
+            first = 2 if gather is not None else 1
+
+            @pl.when(i >= first)
+            def _():
+                scatter.pass_on(order(i - 1))
+
+        return carry
+
+    carry = lax.fori_loop(0, SPLIT, step, carry)
+    if scatter is not None and gather is not None:
+        scatter.pass_on(order(jnp.int32(3)))
+    return carry
+
+
+class LaneGather:
+    def __init__(self, place, buf, send, recv):
+        own = buf.at[place.g]
+        self.own = own
+        self.to_y = remote(own, own, send.at[0], recv.at[0], place.y_peer)
+        self.to_c = remote(own, own, send.at[1], recv.at[1], place.c_peer)
+        across = buf.at[place.g_y]
+        self.from_y = remote(across, across, send.at[2], recv.at[0], place.c_peer)
+        self.on = remote(across, across, send.at[2], recv.at[2], place.c_peer)
+        pair = buf.at[place.g_c]
+        self.from_c = remote(pair, pair, send.at[1], recv.at[1], place.c_peer)
+        diagonal = buf.at[place.g_yc]
+        self.from_diagonal = remote(diagonal, diagonal, send.at[2], recv.at[2], place.c_peer)
+
+    def start(self):
+        self.to_y.start()
+        self.to_c.start()
+
+    def pass_on(self):
+        self.from_y.wait_recv()
+        self.on.start()
+
+    def finish(self):
+        self.from_c.wait_recv()
+        self.from_diagonal.wait_recv()
+        self.sent()
+
+    def sent(self):
+        self.to_y.wait_send()
+        self.to_c.wait_send()
+        self.on.wait_send()
+
+
+class WeightGather:
+    def __init__(self, place, shards, buf, send, recv):
+        self.place, self.shards, self.buf = place, shards, buf
+        self.send, self.recv = send, recv
+        self.keep = pltpu.make_async_copy(
+            shards.at[place.z], buf.at[place.z * place.lanes + place.g], recv.at[place.z]
+        )
+
+    def copy(self, z, g, sent, landed, peer):
+        block = self.buf.at[z * self.place.lanes + g]
+        return remote(block, block, self.send.at[sent + z], self.recv.at[landed + z], peer)
+
+    def along(self, z):
+        place = self.place
+        return remote(
+            self.shards.at[z],
+            self.buf.at[place.z * place.lanes + place.g],
+            self.send.at[z],
+            self.recv.at[place.z],
+            place.at_z(z),
+        )
+
+    def to_y(self, z):
+        return self.copy(z, self.place.g, 4, 4, self.place.y_peer)
+
+    def to_c(self, z):
+        return self.copy(z, self.place.g, 8, 8, self.place.c_peer)
+
+    def on(self, z):
+        return self.copy(z, self.place.g_y, 12, 12, self.place.c_peer)
+
+    def start(self, i):
+        self.along(self.place.block(as_index(i))).start()
+
+    def pass_own(self):
+        self.keep.start()
+        self.keep.wait()
+        self.to_y(self.place.z).start()
+        self.to_c(self.place.z).start()
+
+    def pass_z(self, i):
+        z = self.place.block(as_index(i))
+        self.copy(z, self.place.g, 0, 0, self.place.x_peer).wait_recv()
+        self.to_y(z).start()
+        self.to_c(z).start()
+
+    def pass_y(self, i):
+        z = self.place.block(as_index(i))
+        self.copy(z, self.place.g_y, 12, 4, self.place.c_peer).wait_recv()
+        self.on(z).start()
+
+    def finish(self):
+        place = self.place
+        for z in range(SPLIT):
+            self.copy(z, place.g_c, 8, 8, place.c_peer).wait_recv()
+            self.copy(z, place.g_yc, 12, 12, place.c_peer).wait_recv()
+        for d in (1, 2, 3):
+            self.along(place.z_to(d)).wait_send()
+        for z in range(SPLIT):
+            self.to_y(z).wait_send()
+            self.to_c(z).wait_send()
+            self.on(z).wait_send()
+
+
+class AllSum:
+    def __init__(self, peers, acc, land, send, recv):
+        self.acc, self.land = acc, land
+        self.pairs = [
+            remote(acc.at[i], land.at[i], send.at[i], recv.at[i], peer)
+            for i, peer in enumerate(peers)
+        ]
+
+    def start(self):
+        self.pairs[0].start()
+
+    def step(self):
+        pair, *rest = self.pairs
+        pair.wait_recv()
+        pair.wait_send()
+        i = self.acc.shape[0] - len(self.pairs)
+        total = self.acc[i] + self.land[i]
+        self.pairs = rest
+        if rest:
+            self.acc[i + 1] = total
+            rest[0].start()
+        return total
+
+
+class LaneScatter:
+    def __init__(self, place, part, from_c, from_y, send, recv):
+        self.part, self.from_c, self.from_y = part, from_c, from_y
+        self.count = count = from_y.shape[0]
+        self.base = (place.c * 2 + place.y) * count
+        self.away = (place.c * 2 + 1 - place.y) * count
+        self.base_c, self.away_c = place.y * count, (1 - place.y) * count
+        self.to_c = remote(
+            part.at[pl.ds((1 - place.c) * 2 * count, 2 * count)],
+            from_c,
+            send.at[0],
+            recv.at[0],
+            place.c_peer,
+        )
+        self.to_y = remote(
+            part.at[pl.ds(self.away, count)], from_y, send.at[1], recv.at[1], place.y_peer
+        )
+        self.own = part.at[pl.ds(self.base, count)]
+
+    def start(self):
+        self.to_c.start()
+
+    def step(self):
+        self.to_c.wait_recv()
+
+        def add(i, carry):
+            at = self.away + i
+            near = self.part[at].astype(F32) + self.from_c[self.away_c + i].astype(F32)
+            self.part[at] = near.astype(BF)
+            return carry
+
+        lax.fori_loop(0, self.count, add, 0)
+        self.to_y.start()
+
+    def finish(self):
+        self.to_y.wait_recv()
+        self.to_c.wait_send()
+
+        def add(i, carry):
+            at = self.base + i
+            near = self.part[at].astype(F32) + self.from_c[self.base_c + i].astype(F32)
+            self.part[at] = (near + self.from_y[i].astype(F32)).astype(BF)
+            return carry
+
+        lax.fori_loop(0, self.count, add, 0)
+        self.to_y.wait_send()
+
+
+class TurnZ:
+    def __init__(self, place, out, base, land, send, recv):
+        self.keep = pltpu.make_async_copy(
+            out.at[base + place.z], land.at[place.z], send.at[3]
+        )
+        self.sends = [
+            remote(
+                out.at[base + place.z_to(d)],
+                land.at[place.z],
+                send.at[i],
+                recv.at[i],
+                place.z_peer[d],
+            )
+            for i, d in enumerate(NEAR)
+        ]
+        self.landed = []
+        for i, d in enumerate(NEAR):
+            slot = land.at[place.z_from(d)]
+            self.landed.append(remote(slot, slot, send.at[i], recv.at[i], place.z_peer[d]))
+
+    def start(self):
+        for copy in self.sends:
+            copy.start()
+        self.keep.start()
+
+    def finish(self):
+        for copy in self.landed:
+            copy.wait_recv()
+        for copy in self.sends:
+            copy.wait_send()
+        self.keep.wait()
+
+
+class SpreadZ:
+    def __init__(self, place, buf, send, recv):
+        own = buf.at[place.z]
+        self.own = own
+        self.sends = [
+            remote(own, own, send.at[i], recv.at[i], place.z_peer[d]) for i, d in enumerate(NEAR)
+        ]
+        self.landed = []
+        for i, d in enumerate(NEAR):
+            slot = buf.at[place.z_from(d)]
+            self.landed.append(remote(slot, slot, send.at[i], recv.at[i], place.z_peer[d]))
+
+    def start(self):
+        for copy in self.sends:
+            copy.start()
+
+    def finish(self):
+        for copy in self.landed:
+            copy.wait_recv()
+        for copy in self.sends:
+            copy.wait_send()
+
+
+def item_rows(mod, items, index, width):
+    first = mod[0:1, index * width : (index + 1) * width]
+    second = mod[1:2, index * width : (index + 1) * width]
+    return jnp.where(items == 0, first, second)
+
+
+def item_sums(value, items):
+    return [
+        jnp.sum(jnp.where(items == item, value, 0.0), axis=0, keepdims=True)
+        for item in range(ITEMS)
+    ]
+
+
+def segments(lanes):
+    row = lax.broadcasted_iota(jnp.int32, (lanes, lanes), 0) // HEAD
+    col = lax.broadcasted_iota(jnp.int32, (lanes, lanes), 1) // HEAD
+    return jnp.where(row == col, 1.0 / HEAD, 0.0).astype(F32)
+
+
+def head_mean(value, mean):
+    return jnp.dot(value, mean, precision=HIGH, preferred_element_type=F32)
+
+
+def swap_quarters(value):
+    lanes = value.shape[1]
+    lane = lax.broadcasted_iota(jnp.int32, value.shape, 1)
+    even = (lane // (HEAD // 4)) % 2 == 0
+    return jnp.where(
+        even, pltpu.roll(value, lanes - HEAD // 4, 1), pltpu.roll(value, HEAD // 4, 1)
+    )
+
+
+def head_lanes(shape, head):
+    lane = lax.broadcasted_iota(jnp.int32, shape, 1)
+    return (lane >= head * HEAD) & (lane < (head + 1) * HEAD)
+
+
+def of_head(value, head):
+    return jnp.where(head_lanes(value.shape, head), value, jnp.zeros_like(value))
+
+
+def lane_order(g):
+    return (g % 2) * 2 + g // 2
+
+
+def layer_kernel(names, *refs):
+    r = SimpleNamespace(**dict(zip(names, refs)))
+    place = Place()
+    z, g, x = place.z, place.g, place.x
+    tok_rows, width = r.patches.shape
+    rows = tok_rows // 2
+    wq, wf = r.w_query.shape[1] // SPLIT, r.w_gate.shape[1] // SPLIT
+    two = 2 * wq
+    heads = wq // HEAD
+    group = SPLIT * tok_rows
+    scale = 1.0 / math.sqrt(HEAD)
+    peers = [place.x_peer, place.c_peer, place.y_peer] + [place.z_peer[d] for d in (1, 2, 3)]
+    barrier = pltpu.get_barrier_semaphore()
+    for peer in peers:
+        pl.semaphore_signal(barrier, inc=1, device_id=peer, device_id_type=MESH)
+
+    text_cols = pl.ds(pl.multiple_of((z * place.lanes + g) * r.text.shape[1], 128), r.text.shape[1])
+    text_copy = pltpu.make_async_copy(r.caption.at[:, text_cols], r.text, r.text_sem)
+    text_copy.start()
+    for i in range(SPLIT):
+        at = slice(i * wq, (i + 1) * wq)
+        r.qkvo_in[i, :, 0:wq] = r.w_key[:, at]
+        r.qkvo_in[i, :, wq:two] = r.w_query[:, at]
+        r.qkvo_in[i, :, two : two + wq] = r.w_out[at, :].T
+        r.qkvo_in[i, :, two + wq : 2 * two] = r.w_value[:, at]
+    pl.semaphore_wait(barrier, len(peers))
+
+    weights = WeightGather(place, r.qkvo_in, r.qkvo, r.w_send, r.w_recv)
+    weights.start(1)
+    mine = pl.ds(pl.multiple_of(x * rows, rows), rows)
+    tokens = Gather(place, r.x_buf, r.x_send, r.x_recv)
+    tokens.own[...] = r.patches[mine]
+    tokens.start()
+    along = [place.c_peer, place.y_peer, place.z_pair, place.z_far]
+    sums = AllSum(along, r.m_acc, r.m_land, r.m_send, r.m_recv)
+    pre, sig = conditioning(r.band_table, r.item_band)
+    act = jnp.concatenate([pre * sig, jnp.zeros((6, pre.shape[1]), F32)], axis=0).astype(BF)
+    r.m_acc[0] = bdot(act, r.w_ada[...])[:ITEMS]
+    sums.start()
+    spots = SpreadZ(place, r.pos_buf, r.pos_send, r.pos_recv)
+    spots.own[...] = jnp.concatenate(
+        [r.positions[...].astype(F32), jnp.zeros((6, tok_rows), F32)], axis=0
+    )
+    spots.start()
+    weights.pass_own()
+    weights.start(2)
+    text_copy.wait()
+    words = r.cap_part.shape[1]
+    caption = LaneScatter(place, r.cap_part, r.cap_fc, r.cap_fy, r.cap_s, r.cap_r)
+    for kind, matrix in enumerate((r.w_ckey, r.w_cvalue)):
+        full = bdot(r.text[...], matrix[...]).astype(BF)
+        for i in range(SPLIT):
+            for lane_g in range(4):
+                block = lane_order(lane_g) * SPLIT + i
+                r.cap_part[block, :, kind * wq : (kind + 1) * wq] = full[
+                    lane_g * words : (lane_g + 1) * words, i * wq : (i + 1) * wq
+                ]
+    caption.start()
+    for i in range(SPLIT):
+        at = slice(i * wf, (i + 1) * wf)
+        r.ffn_in[i, :, 0:wf] = r.w_gate[:, at]
+        r.ffn_in[i, :, wf : 2 * wf] = r.w_up[:, at]
+        r.ffn_in[i, :, 2 * wf : 3 * wf] = r.w_down[at, :].T
+    sums.step()
+    sums.step()
+    caption.step()
+    weights.start(3)
+    tokens.pass_on(1)
+    weights.pass_z(1)
+    sums.step()
+
+    blocks = tok_rows // BLK
+    token = lax.broadcasted_iota(jnp.int32, (group, 1), 0) // BLK
+    key = lax.broadcasted_iota(jnp.int32, (1, 4 * group), 1) // BLK
+    token_item = jnp.zeros((group, 1), jnp.int32)
+    key_item = jnp.zeros((1, 4 * group), jnp.int32)
+    for i in range(SPLIT):
+        for j in range(blocks):
+            own = r.block_item[(i * place.lanes + g) * blocks + j]
+            token_item = jnp.where(token == i * blocks + j, own, token_item)
+            for other in range(4):
+                value = r.block_item[(i * place.lanes + other) * blocks + j]
+                key_item = jnp.where(key == (other * SPLIT + i) * blocks + j, value, key_item)
+    r.items[...] = token_item
+    for i in range(4):
+        r.key_items[i] = key_item[:, i * group : (i + 1) * group]
+    own_at = pl.ds(pl.multiple_of(z * tok_rows + x * rows, rows), rows)
+
+    mean = segments(two)
+    mean_q = segments(wq)
+    lane = lax.broadcasted_iota(jnp.int32, (1, two), 1)
+    gain_kq = r.head_rows[z, 0:1]
+    gain_ckey = r.head_rows[z, 1:2]
+    gates = jnp.tanh(r.head_rows[z, 2:3])[:, :wq]
+    freqs = r.head_rows[z, 3:4][:, : 2 * HEAD]
+    gain_in, gain_attn = r.rows_in[0:1], r.rows_in[1:2]
+    gain_ffn, gain_out = r.rows_in[2:3], r.rows_in[3:4]
+
+    spots.finish()
+    lane_row = lax.broadcasted_iota(jnp.int32, (1, 2 * HEAD), 1)
+    by_row = (lane_row // (HEAD // 2)) % 2 == 0
+    sign = jnp.where((lane_row // (HEAD // 4)) % 2 == 0, -1.0, 1.0)
+    for i in range(SPLIT):
+        cols = r.pos_buf[i].T
+        angle = jnp.where(by_row, cols[:, 0:1], cols[:, 1:2]) * freqs
+        r.cos_t[i] = jnp.cos(angle)
+        r.sin_t[i] = jnp.sin(angle) * sign
+
+    caption.finish()
+    cap_turn = TurnZ(place, r.cap_part, caption.base, r.cap_z, r.cz_send, r.cz_recv)
+    cap_turn.start()
+    for i in (2, 3):
+        tokens.pass_on(i)
+        weights.pass_z(i)
+    for i in range(4):
+        weights.pass_y(i)
+    feed = WeightGather(place, r.ffn_in, r.ffn, r.f_send, r.f_recv)
+    for i in (1, 2, 3):
+        feed.start(i)
+    feed.pass_own()
+    r.mod[...] = sums.step() + jnp.concatenate(
+        [r.rows_in[4 + i : 5 + i] for i in range(4)], axis=1
+    )
+    cap_turn.finish()
+    cap_raw = (r.cap_z[0].astype(F32) + r.cap_z[1].astype(F32)) + (
+        r.cap_z[2].astype(F32) + r.cap_z[3].astype(F32)
+    )
+    cap_recip = lax.rsqrt(head_mean(cap_raw * cap_raw, mean) + EPS)
+    cap_hat = cap_raw * cap_recip
+    r.cap_hat[...] = cap_hat
+    r.cap_recip[...] = cap_recip
+    cap_gather = LaneGather(place, r.cap_kv, r.ckv_send, r.ckv_recv)
+    cap_gather.own[...] = jnp.where(lane < wq, cap_hat * gain_ckey, cap_raw).astype(BF)
+    cap_gather.start()
+    for i in range(4):
+        tokens.arrive(i)
+    cap_gather.pass_on()
+    weights.finish()
+
+    keep = LaneGather(place, r.kv, r.kv_send, r.kv_recv)
+
+    def span(i):
+        return pl.ds(pl.multiple_of(i * tok_rows, tok_rows), tok_rows)
+
+    def w_kq():
+        return r.qkvo[:, :, 0:two].reshape(width, two)
+
+    def w_ov():
+        return r.qkvo[:, :, two : 2 * two].reshape(width, two)
+
+    def project(i, carry):
+        block = r.x_buf[pl.ds(i * 2, 2)].reshape(tok_rows, width).astype(F32)
+        unit, _ = normed_pair(block)
+        factor = gain_in * (1.0 + item_rows(r.mod, r.items[span(i)], 0, width))
+        norm = (unit * factor).astype(BF)
+        r.norm_in[i] = norm
+        raw = bdot(norm, w_kq())
+        own_v = bdot(norm, w_ov())
+        recip = lax.rsqrt(head_mean(raw * raw, mean) + EPS)
+        hat = raw * recip
+        r.kq_hat[i] = hat
+        r.kq_recip[i] = recip
+        cos = jnp.concatenate([r.cos_t[i]] * heads, axis=1)
+        sin = jnp.concatenate([r.sin_t[i]] * heads, axis=1)
+        gained = hat * gain_kq
+        turned = gained * cos + swap_quarters(gained) * sin
+        r.kv[g, span(i)] = jnp.where(lane < wq, turned, own_v).astype(BF)
+        r.queries[span(i)] = (turned[:, wq:].astype(BF).astype(F32) * scale).astype(BF)
+        return carry
+
+    lax.fori_loop(0, SPLIT, project, 0)
+    keep.start()
+    slot_lane = lax.broadcasted_iota(jnp.int32, (1, r.totals.shape[1]), 1)
+    ones = jnp.where(lax.broadcasted_iota(jnp.int32, (1, HEAD), 1) == 0, 1.0, 0.0).astype(BF)
+
+    def with_ones(values):
+        return jnp.concatenate([values, jnp.broadcast_to(ones, (values.shape[0], HEAD))], axis=1)
+
+    def split_lump(index):
+        lump = r.kv[index]
+        r.k_all[index] = lump[:, :wq]
+        r.v_all[index] = with_ones(lump[:, wq:])
+
+    def attend(head, keys, values, same):
+        scores = dot_t(of_head(r.queries[...], head), keys)
+        if same is not None:
+            scores = jnp.where(same, scores, NEG)
+        out = bdot(jnp.exp(scores).astype(BF), values)
+        return of_head(out[:, :wq], head), jnp.where(slot_lane == head, out[:, wq : wq + 1], 0.0)
+
+    def cross(head, carry):
+        out, total = attend(head, r.cap_k[...], r.cap_v[...], None)
+        r.attn_cross[...] += out
+        r.cross_logs[...] += total
+        return carry
+
+    def attend_into(index):
+        def step(head, carry):
+            same = r.items[...] == r.key_items[index]
+            out, total = attend(head, r.k_all[index], r.v_all[index], same)
+            r.attn_self[...] += out
+            r.totals[...] += total
+            return carry
+
+        lax.fori_loop(0, heads, step, 0)
+
+    for ref in (r.attn_self, r.attn_cross, r.totals, r.cross_logs):
+        ref[...] = jnp.zeros_like(ref)
+    split_lump(g)
+    attend_into(g)
+    cap_gather.finish()
+    kv_text = r.cap_kv[...].reshape(4 * words, two)
+    r.cap_k[...] = kv_text[:, :wq]
+    r.cap_v[...] = with_ones(kv_text[:, wq:])
+    feed.pass_z(1)
+    keep.from_c.wait_recv()
+    split_lump(place.g_c)
+    attend_into(place.g_c)
+    feed.pass_z(2)
+    keep.pass_on()
+    split_lump(place.g_y)
+    attend_into(place.g_y)
+    feed.pass_z(3)
+    lax.fori_loop(0, heads, cross, 0)
+    keep.from_diagonal.wait_recv()
+    split_lump(place.g_yc)
+    attend_into(place.g_yc)
+
+    def by_total(out, totals):
+        shares = jnp.zeros_like(out)
+        for head in range(heads):
+            share = 1.0 / totals[:, head : head + 1]
+            shares = shares + of_head(jnp.broadcast_to(share, out.shape), head)
+        return out * shares
+
+    def blend(i, carry):
+        at = span(i)
+        self_part = by_total(r.attn_self[at], r.totals[at])
+        cross_part = by_total(r.attn_cross[at], r.cross_logs[at])
+        r.attn_self[at] = self_part
+        r.attn_cross[at] = cross_part
+        r.totals[at] = jnp.log(r.totals[at])
+        r.cross_logs[at] = jnp.log(r.cross_logs[at])
+        mixed = (self_part + gates * cross_part).astype(BF)
+        wide = jnp.concatenate([mixed, jnp.zeros_like(mixed)], axis=1)
+        r.mix_s[at] = wide
+        r.part[i] = dot_t(wide, w_ov()).astype(BF).reshape(2, rows, width)
+        return carry
+
+    def scatter_of(send, recv):
+        return Scatter(place, r.part, r.from_x, r.from_z, send, recv)
+
+    out_sum = scatter_of(r.s1, r.r1)
+    flow(place, None, out_sum, blend, 0)
+    for i in range(4):
+        feed.pass_y(i)
+    branch = out_sum.finish()
+
+    item = r.items[own_at]
+    hat_two, recip_two = normed_pair(branch)
+    tanh_one = jnp.tanh(item_rows(r.mod, item, 1, width))
+    resid = r.patches[mine].astype(F32) + tanh_one * hat_two * gain_attn
+    hat_three, recip_three = normed_pair(resid)
+    factor_three = gain_ffn * (1.0 + item_rows(r.mod, item, 2, width))
+    norms = Gather(place, r.n_buf, r.n_send, r.n_recv)
+    norms.own[...] = (hat_three * factor_three).astype(BF)
+    norms.start()
+    tokens.finish()
+    keep.sent()
+    feed.finish()
+
+    def f_weights(index):
+        return r.ffn[:, :, index * wf : (index + 1) * wf].reshape(width, wf)
+
+    def forward(i, carry):
+        block = r.n_buf[pl.ds(i * 2, 2)].reshape(tok_rows, width)
+        gate_val = bdot(block, f_weights(0))
+        up_val = bdot(block, f_weights(1))
+        r.gate_s[i] = gate_val
+        r.up_s[i] = up_val
+        hidden = (gate_val * jax.nn.sigmoid(gate_val) * up_val).astype(BF)
+        r.hid_s[i] = hidden
+        r.part[i] = dot_t(hidden, f_weights(2)).astype(BF).reshape(2, rows, width)
+        return carry
+
+    down = scatter_of(r.s2, r.r2)
+    flow(place, norms, down, forward, 0)
+    ffn = down.finish()
+    norms.finish()
+
+    hat_four, recip_four = normed_pair(ffn)
+    tanh_two = jnp.tanh(item_rows(r.mod, item, 3, width))
+    grad_out = r.out_grad[mine].astype(F32)
+    grad_four = grad_out * tanh_two
+    grads = Gather(place, r.g_buf, r.g_send, r.g_recv)
+    grads.own[...] = normed_back(grad_four * gain_out, hat_four, recip_four).astype(BF)
+    grads.start()
+    output = resid + tanh_two * hat_four * gain_out
+    r.out_own[...] = output
+    r.out_half[0] = output.astype(BF)
+    out_copy = remote(r.out_half.at[0], r.out_half.at[1], r.o_send, r.o_recv, place.x_peer)
+    out_copy.start()
+    everywhere = along[:2] + [place.x_peer] + along[2:]
+    early = AllSum(everywhere, r.e_acc, r.e_land, r.e_send, r.e_recv)
+    r.e_acc[0] = jnp.zeros(r.e_acc.shape[1:], F32)
+    gate_sums = item_sums(grad_out * hat_four * gain_out * (1.0 - tanh_two * tanh_two), item)
+    r.e_acc[0, 2:3] = jnp.sum(grad_four * hat_four, axis=0, keepdims=True)
+    r.e_acc[0, 8:9] = gate_sums[0]
+    r.e_acc[0, 9:10] = gate_sums[1]
+
+    def backward(i, carry):
+        block = r.g_buf[pl.ds(i * 2, 2)].reshape(tok_rows, width)
+        grad_hidden = bdot(block, f_weights(2))
+        gate_val = r.gate_s[i]
+        gate_sig = jax.nn.sigmoid(gate_val)
+        grad_gate = (
+            grad_hidden * r.up_s[i] * gate_sig * (1.0 + gate_val * (1.0 - gate_sig))
+        ).astype(BF)
+        grad_up = (grad_hidden * gate_val * gate_sig).astype(BF)
+        r.gg_s[i] = grad_gate
+        r.gu_s[i] = grad_up
+        r.part[i] = (
+            (dot_t(grad_gate, f_weights(0)) + dot_t(grad_up, f_weights(1)))
+            .astype(BF)
+            .reshape(2, rows, width)
+        )
+        return carry
+
+    back = scatter_of(r.s3, r.r3)
+    flow(place, grads, back, backward, 0)
+
+    block_rows = r.ffn.shape[1]
+    step_cols = 4 * block_rows
+
+    def ffn_matrices(i, carry):
+        cols = pl.ds(pl.multiple_of(i * step_cols, step_cols), step_cols)
+        norm = r.n_buf[:, :, cols].reshape(group, step_cols)
+        grad = r.g_buf[:, :, cols].reshape(group, step_cols)
+        for j, (left, right) in enumerate(((norm, r.gg_s), (norm, r.gu_s), (grad, r.hid_s))):
+            block = t_dot(left, right[...].reshape(group, wf)).astype(BF)
+            block = block.reshape(4, block_rows, wf)
+            for other in range(4):
+                r.ffn[lane_order(other) * SPLIT + i, :, j * wf : (j + 1) * wf] = block[other]
+        return carry
+
+    lax.fori_loop(0, SPLIT, ffn_matrices, 0)
+    f_home = LaneScatter(place, r.ffn, r.f_fc, r.f_fy, r.fh_s, r.fh_r)
+    f_home.start()
+    grad_norm = back.finish()
+    grads.finish()
+    d_resid = grad_out + normed_back(grad_norm * factor_three, hat_three, recip_three)
+    grad_two = d_resid * tanh_one
+    attn_grads = Gather(place, r.x_buf, r.a_send, r.a_recv)
+    attn_grads.own[...] = normed_back(grad_two * gain_attn, hat_two, recip_two).astype(BF)
+    attn_grads.start()
+    r.dp_own[...] = d_resid
+    scale_sums = item_sums(grad_norm * hat_three * gain_ffn, item)
+    gate_sums = item_sums(d_resid * hat_two * gain_attn * (1.0 - tanh_one * tanh_one), item)
+    r.e_acc[0, 0:1] = jnp.sum(grad_two * hat_two, axis=0, keepdims=True)
+    r.e_acc[0, 1:2] = jnp.sum(
+        grad_norm * hat_three * (1.0 + item_rows(r.mod, item, 2, width)), axis=0, keepdims=True
+    )
+    r.e_acc[0, 4:5] = gate_sums[0]
+    r.e_acc[0, 5:6] = gate_sums[1]
+    r.e_acc[0, 6:7] = scale_sums[0]
+    r.e_acc[0, 7:8] = scale_sums[1]
+
+    r.dk_acc[...] = jnp.zeros_like(r.dk_acc)
+    r.dv_acc[...] = jnp.zeros_like(r.dv_acc)
+    r.dck_acc[...] = jnp.zeros_like(r.dck_acc)
+    r.dcv_acc[...] = jnp.zeros_like(r.dcv_acc)
+    f_home.step()
+
+    def attend_back(i, gate_sum):
+        at = span(i)
+        block = r.x_buf[pl.ds(i * 2, 2)].reshape(tok_rows, width)
+        d_mix = bdot(block, w_ov())[:, :wq].astype(BF)
+        mix_f = d_mix.astype(F32)
+        d_cross = (gates * mix_f).astype(BF)
+        delta = head_mean(mix_f * r.attn_self[at], mean_q) * HEAD
+        gate_sum = gate_sum + jnp.sum(mix_f * r.attn_cross[at], axis=0, keepdims=True)
+        query = r.queries[at]
+        logs = r.totals[at]
+        cross_logs = r.cross_logs[at]
+        dq = jnp.zeros((tok_rows, wq), F32)
+        for head in range(heads):
+            stack = slice(head * tok_rows, (head + 1) * tok_rows)
+            query_h = of_head(query, head)
+            cross_h = of_head(d_cross, head)
+            r.q_stack[stack] = query_h
+            r.c_stack[stack] = cross_h
+            r.m_stack[stack] = of_head(d_mix, head)
+            probs = jnp.exp(dot_t(query_h, r.cap_k[...]) - cross_logs[:, head : head + 1])
+            d_probs = dot_t(cross_h, r.cap_v[:, :wq])
+            inner = jnp.sum(probs * d_probs, axis=1, keepdims=True)
+            d_scores = (probs * (d_probs - inner)).astype(BF)
+            r.cp_stack[stack] = probs.astype(BF)
+            r.cs_stack[stack] = d_scores
+            dq = dq + of_head(bdot(d_scores, r.cap_k[...]), head)
+        r.dck_acc[...] += t_dot(r.cs_stack[...], r.q_stack[...])
+        r.dcv_acc[...] += t_dot(r.cp_stack[...], r.c_stack[...])
+        for j in range(4):
+            same = r.items[at] == r.key_items[j]
+            for head in range(heads):
+                stack = slice(head * tok_rows, (head + 1) * tok_rows)
+                scores = jnp.where(same, dot_t(r.q_stack[stack], r.k_all[j]), NEG)
+                probs = jnp.exp(scores - logs[:, head : head + 1])
+                d_probs = dot_t(r.m_stack[stack], r.v_all[j, :, :wq])
+                d_scores = (probs * (d_probs - delta[:, head * HEAD : head * HEAD + 1])).astype(BF)
+                r.p_stack[stack] = probs.astype(BF)
+                r.s_stack[stack] = d_scores
+                dq = dq + of_head(bdot(d_scores, r.k_all[j]), head)
+            r.dk_acc[j] += t_dot(r.s_stack[...], r.q_stack[...])
+            r.dv_acc[j] += t_dot(r.p_stack[...], r.m_stack[...])
+        r.dq_s[at] = (dq * scale).astype(BF)
+        return gate_sum
+
+    f_turn = TurnZ(place, r.ffn, f_home.base, r.f_land, r.fz_s, r.fz_r)
+
+    def turn_ffn():
+        f_home.finish()
+        f_turn.start()
+
+    gate_sum = flow(place, attn_grads, None, attend_back, jnp.zeros((1, wq), F32), turn_ffn)
+    early.start()
+
+    keys_home = LaneScatter(place, r.kv, r.kv_fc, r.kv_fy, r.kvh_s, r.kvh_r)
+    for i in range(4):
+        r.kv[lane_order(i)] = jnp.concatenate([r.dk_acc[i], r.dv_acc[i]], axis=1).astype(BF)
+    keys_home.start()
+    cap_home = LaneScatter(place, r.t_part, r.t_fc, r.t_fy, r.t_s, r.t_r)
+    for i in range(4):
+        at = slice(i * words, (i + 1) * words)
+        d_cap = jnp.concatenate([r.dck_acc[at], r.dcv_acc[at]], axis=1)
+        r.t_part[lane_order(i)] = d_cap.astype(BF)
+    cap_home.start()
+
+    def turn_back(i, grad):
+        cos = jnp.concatenate([r.cos_t[i]] * heads, axis=1)
+        sin = jnp.concatenate([r.sin_t[i]] * heads, axis=1)
+        d_norm = grad * cos - swap_quarters(grad) * sin
+        hat = r.kq_hat[i]
+        gain_sum = jnp.sum(d_norm * hat, axis=0, keepdims=True)
+        d_hat = d_norm * gain_kq
+        grad = (r.kq_recip[i] * (d_hat - hat * head_mean(d_hat * hat, mean))).astype(BF)
+        return grad, gain_sum
+
+    def raw_queries(i, query_sum):
+        d_query = r.dq_s[span(i)].astype(F32)
+        d_query = jnp.concatenate([jnp.zeros_like(d_query), d_query], axis=1)
+        grad, gain_sum = turn_back(i, d_query)
+        r.dq_raw[span(i)] = grad
+        return query_sum + gain_sum
+
+    keys_home.step()
+    early.step()
+    cap_home.step()
+    query_sum = lax.fori_loop(0, SPLIT, raw_queries, jnp.zeros((1, two), F32))
+
+    def store_part(part, i, block):
+        block = block.astype(BF).reshape(4, block_rows, two)
+        for other in range(4):
+            part[lane_order(other) * SPLIT + i] = block[other]
+
+    def matrices_oq(i, carry):
+        cols = pl.ds(pl.multiple_of(i * step_cols, step_cols), step_cols)
+        above = r.x_buf[:, :, cols].reshape(group, step_cols)
+        left = r.norm_in[:, :, cols].reshape(group, step_cols)
+        store_part(r.a_part, i, t_dot(above, r.mix_s[...]) + t_dot(left, r.dq_raw[...]))
+        return carry
+
+    lax.fori_loop(0, SPLIT, matrices_oq, 0)
+    a_home = LaneScatter(place, r.a_part, r.a_fc, r.a_fy, r.ah_s, r.ah_r)
+    a_home.start()
+    early.step()
+    a_home.step()
+
+    cap_home.finish()
+    d_cap = r.t_part[cap_home.base].astype(F32)
+    hat = r.cap_hat[...]
+    key_lanes = lane < wq
+    cap_sum = jnp.sum(jnp.where(key_lanes, d_cap * hat, 0.0), axis=0, keepdims=True)
+    d_hat = d_cap * jnp.where(key_lanes, gain_ckey, 0.0)
+    d_raw = r.cap_recip[...] * (d_hat - hat * head_mean(d_hat * hat, mean))
+    cap_spread = SpreadZ(place, r.t_z, r.tz_s, r.tz_r)
+    cap_spread.own[...] = jnp.where(key_lanes, d_raw, d_cap).astype(BF)
+    cap_spread.start()
+    keys_home.finish()
+
+    def raw_keys(i, key_sum):
+        total = r.kv[keys_home.base, span(i)].astype(F32)
+        grad, gain_sum = turn_back(i, jnp.where(key_lanes, total, 0.0))
+        r.dkv_raw[span(i)] = jnp.where(key_lanes, grad.astype(F32), total).astype(BF)
+        d_kq = jnp.where(key_lanes, grad.astype(F32), r.dq_raw[span(i)].astype(F32)).astype(BF)
+        d_ov = jnp.where(key_lanes, 0.0, total).astype(BF)
+        r.part[i] = (
+            (dot_t(d_kq, w_kq()) + dot_t(d_ov, w_ov())).astype(BF).reshape(2, rows, width)
+        )
+        return key_sum + gain_sum
+
+    in_sum = scatter_of(r.s4, r.r4)
+    key_sum = flow(place, None, in_sum, raw_keys, jnp.zeros((1, two), F32))
+
+    def matrices_kv(i, carry):
+        cols = pl.ds(pl.multiple_of(i * step_cols, step_cols), step_cols)
+        left = r.norm_in[:, :, cols].reshape(group, step_cols)
+        store_part(r.b_part, i, t_dot(left, r.dkv_raw[...]))
+        return carry
+
+    lax.fori_loop(0, SPLIT, matrices_kv, 0)
+    b_home = LaneScatter(place, r.b_part, r.b_fc, r.b_fy, r.bh_s, r.bh_r)
+    b_home.start()
+    heads_sum = AllSum(along[:2], r.h_acc, r.h_land, r.h_send, r.h_recv)
+    r.h_acc[0] = jnp.zeros(r.h_acc.shape[1:], F32)
+    r.h_acc[0, 0:1] = jnp.where(key_lanes, key_sum, query_sum)
+    r.h_acc[0, 1:2] = cap_sum
+    r.h_acc[0, 2:3] = jnp.concatenate([gate_sum, jnp.zeros_like(gate_sum)], axis=1)
+    heads_sum.start()
+    a_home.finish()
+    a_turn = TurnZ(place, r.a_part, a_home.base, r.a_land, r.az_s, r.az_r)
+    a_turn.start()
+    cap_spread.finish()
+    cap_all = LaneGather(place, r.t_all, r.ta_s, r.ta_r)
+    cap_all.own[...] = r.t_z[...]
+    cap_all.start()
+    b_home.step()
+    heads_sum.step()
+    heads_spread = SpreadZ(place, r.h_slots, r.hz_send, r.hz_recv)
+    heads_spread.own[...] = heads_sum.step()
+    heads_spread.start()
+    early.step()
+    early.step()
+    cap_all.pass_on()
+
+    d_norm = in_sum.finish()
+    hat, recip = normed_pair(r.patches[mine].astype(F32))
+    factor = 1.0 + item_rows(r.mod, item, 0, width)
+    d_patches = r.dp_own[...] + normed_back(d_norm * gain_in * factor, hat, recip)
+    r.dp_own[...] = d_patches
+    r.dp_half[0] = d_patches.astype(BF)
+    dp_copy = remote(r.dp_half.at[0], r.dp_half.at[1], r.dp_send, r.dp_recv, place.x_peer)
+    dp_copy.start()
+    scale_sums = item_sums(d_norm * hat * gain_in, item)
+    late = AllSum(everywhere, r.l_acc, r.l_land, r.l_send, r.l_recv)
+    r.l_acc[0] = jnp.zeros(r.l_acc.shape[1:], F32)
+    r.l_acc[0, 0:1] = jnp.sum(d_norm * hat * factor, axis=0, keepdims=True)
+    r.l_acc[0, 1:2] = scale_sums[0]
+    r.l_acc[0, 2:3] = scale_sums[1]
+    late.start()
+    b_home.finish()
+    b_turn = TurnZ(place, r.b_part, b_home.base, r.b_land, r.bz_s, r.bz_r)
+    b_turn.start()
+    for _ in range(4):
+        late.step()
+    out_copy.wait()
+    attn_grads.finish()
+    r.early[...] = early.step()
+    heads_spread.finish()
+    f_turn.finish()
+    a_turn.finish()
+    cap_all.finish()
+    dp_copy.wait()
+    r.late[...] = late.step()
+    b_turn.finish()
+
+
+def finish_kernel(
+    out_own, out_half, dp_own, dp_half, f_land, a_land, b_land, t_all, early, late, heads_in, text,
+    head_rows, band_table, item_band, w_ada,
+    output, d_patches, d_query, d_key, d_value, d_out, d_gate, d_up, d_down, d_ckey, d_cvalue,
+    d_ada, d_b_ada, d_attn_in, d_attn_out, d_ffn_in, d_ffn_out, d_g_query, d_g_key, d_g_ckey,
+    d_cross, d_band,
+):
+    x = lax.axis_index("tp")
+    rows, width = out_own.shape
+    wf = f_land.shape[2] // 3
+    wq = a_land.shape[2] // 2
+    words = t_all.shape[2]
+    mine = pl.ds(pl.multiple_of(x * rows, rows), rows)
+    other = pl.ds(pl.multiple_of((1 - x) * rows, rows), rows)
+    output[mine] = out_own[...]
+    output[other] = out_half[1].astype(F32)
+    d_patches[mine] = dp_own[...]
+    d_patches[other] = dp_half[1].astype(F32)
+    for z in range(SPLIT):
+        at = slice(z * wf, (z + 1) * wf)
+        d_gate[:, at] = f_land[z, :, 0:wf].astype(F32)
+        d_up[:, at] = f_land[z, :, wf : 2 * wf].astype(F32)
+        d_down[at] = f_land[z, :, 2 * wf : 3 * wf].astype(F32).T
+        at = slice(z * wq, (z + 1) * wq)
+        d_out[at] = a_land[z, :, 0:wq].astype(F32).T
+        d_query[:, at] = a_land[z, :, wq : 2 * wq].astype(F32)
+        d_key[:, at] = b_land[z, :, 0:wq].astype(F32)
+        d_value[:, at] = b_land[z, :, wq : 2 * wq].astype(F32)
+        d_cap = t_dot(text[...], t_all[:, z].reshape(4 * words, 2 * wq))
+        d_ckey[:, at] = d_cap[:, :wq]
+        d_cvalue[:, at] = d_cap[:, wq:]
+    grad_mod = jnp.concatenate([late[1:3], early[4:6], early[6:8], early[8:10]], axis=1)
+    pre, sig = conditioning(band_table, item_band)
+    low = (pre * sig).astype(BF).astype(F32)
+    cols = jnp.concatenate([low, jnp.zeros((6, low.shape[1]), F32)], axis=0).T
+    d_ada[...] = cols[:, 0:1] * grad_mod[0:1] + cols[:, 1:2] * grad_mod[1:2]
+    d_act = lax.dot_general(
+        grad_mod,
+        w_ada[...].astype(F32),
+        (((1,), (1,)), ((), ())),
+        precision=HIGH,
+        preferred_element_type=F32,
+    )
+    d_pre = d_act * sig * (1.0 + pre * (1.0 - sig))
+    band = lax.broadcasted_iota(jnp.int32, (BANDS, 1), 0)
+    d_band[...] = sum(
+        jnp.where(band == item_band[i], d_pre[i : i + 1], 0.0) for i in range(ITEMS)
+    )
+    d_b_ada[...] = (grad_mod[0:1] + grad_mod[1:2]).reshape(d_b_ada.shape)
+    d_attn_in[...] = late[0:1].reshape(d_attn_in.shape)
+    d_attn_out[...] = early[0:1].reshape(d_attn_out.shape)
+    d_ffn_in[...] = early[1:2].reshape(d_ffn_in.shape)
+    d_ffn_out[...] = early[2:3].reshape(d_ffn_out.shape)
+
+    def joined(row, part):
+        return jnp.concatenate(
+            [heads_in[z, row : row + 1, part * wq : (part + 1) * wq] for z in range(SPLIT)], axis=1
+        ).reshape(d_g_key.shape)
+
+    d_g_key[...] = joined(0, 0)
+    d_g_query[...] = joined(0, 1)
+    d_g_ckey[...] = joined(1, 0)
+    heads = wq // HEAD
+    lane = lax.broadcasted_iota(jnp.int32, (wq, 128), 0) // HEAD
+    col = lax.broadcasted_iota(jnp.int32, (wq, 128), 1)
+    total = jnp.zeros((8, 128), F32)
+    for z in range(SPLIT):
+        gate = jnp.tanh(head_rows[z, 2:3, :wq])
+        terms = heads_in[z, 2:3, :wq] * (1.0 - gate * gate)
+        terms = jnp.concatenate([terms, jnp.zeros((7, wq), F32)], axis=0)
+        pick = jnp.where(col == lane + z * heads, 1.0, 0.0)
+        total = total + jnp.dot(terms, pick, precision=HIGH, preferred_element_type=F32)
+    d_cross[...] = total[0:1]
+
+
+def conditioning(band_table, item_band):
+    band = lax.broadcasted_iota(jnp.int32, (BANDS, 1), 0)
+    table = band_table[...]
+    pre = jnp.concatenate(
+        [
+            jnp.sum(jnp.where(band == item_band[i], table, 0.0), axis=0, keepdims=True)
+            for i in range(ITEMS)
+        ],
+        axis=0,
+    )
+    return pre, jax.nn.sigmoid(pre)
+
+
+def layer_call(ins):
+    tok_rows, width = ins["patches"].shape
+    rows = tok_rows // 2
+    row_dev, q_cols = ins["w_query"].shape
+    wq, wf = q_cols // SPLIT, ins["w_gate"].shape[1] // SPLIT
+    two = 2 * wq
+    heads = wq // HEAD
+    lanes = 4
+    group = SPLIT * tok_rows
+    text, features = ins["caption"].shape
+    words = text // lanes
+    feat_dev = ins["w_ckey"].shape[0]
+    mod = (ITEMS, 4 * width)
+    tile, sem = pltpu.VMEM, lambda count: pltpu.SemaphoreType.DMA((count,))
+    cap = (words, two)
+    shard = (SPLIT, row_dev)
+    both, half = (SPLIT, tok_rows), (rows, width)
+
+    def sum_tile(size, steps):
+        return tile((steps,) + size, F32)
+
+    scratch = dict(
+        text_sem=pltpu.SemaphoreType.DMA,
+        qkvo_in=tile(shard + (2 * two,), BF),
+        ffn_in=tile(shard + (3 * wf,), BF),
+        qkvo=tile((SPLIT * lanes, row_dev, 2 * two), BF),
+        ffn=tile((SPLIT * lanes, row_dev, 3 * wf), BF),
+        w_send=sem(16),
+        w_recv=sem(16),
+        f_send=sem(16),
+        f_recv=sem(16),
+        x_buf=tile((2 * SPLIT,) + half, BF),
+        n_buf=tile((2 * SPLIT,) + half, BF),
+        g_buf=tile((2 * SPLIT,) + half, BF),
+        x_send=sem(10),
+        x_recv=sem(10),
+        n_send=sem(10),
+        n_recv=sem(10),
+        g_send=sem(10),
+        g_recv=sem(10),
+        a_send=sem(10),
+        a_recv=sem(10),
+        part=tile((SPLIT, 2) + half, BF),
+        from_x=tile((SPLIT,) + half, BF),
+        from_z=tile((SPLIT,) + half, BF),
+        s1=sem(8),
+        r1=sem(8),
+        s2=sem(8),
+        r2=sem(8),
+        s3=sem(8),
+        r3=sem(8),
+        s4=sem(8),
+        r4=sem(8),
+        m_acc=sum_tile((ITEMS, 4 * width), 4),
+        m_land=sum_tile((ITEMS, 4 * width), 4),
+        m_send=sem(6),
+        m_recv=sem(6),
+        e_acc=sum_tile((16, width), 5),
+        e_land=sum_tile((16, width), 5),
+        e_send=sem(6),
+        e_recv=sem(6),
+        l_acc=sum_tile((8, width), 5),
+        l_land=sum_tile((8, width), 5),
+        l_send=sem(6),
+        l_recv=sem(6),
+        h_acc=sum_tile((8, two), 2),
+        h_land=sum_tile((8, two), 2),
+        hz_send=sem(3),
+        hz_recv=sem(3),
+        h_send=sem(6),
+        h_recv=sem(6),
+        mod=tile((ITEMS, 4 * width), F32),
+        pos_buf=tile((SPLIT, 8, tok_rows), F32),
+        pos_send=sem(3),
+        pos_recv=sem(3),
+        cap_part=tile((4 * SPLIT,) + cap, BF),
+        cap_fc=tile((2 * SPLIT,) + cap, BF),
+        cap_fy=tile((SPLIT,) + cap, BF),
+        cap_s=sem(2),
+        cap_r=sem(2),
+        cap_z=tile((SPLIT,) + cap, BF),
+        cz_send=sem(4),
+        cz_recv=sem(4),
+        cap_kv=tile((lanes,) + cap, BF),
+        ckv_send=sem(3),
+        ckv_recv=sem(3),
+        cap_hat=tile(cap, F32),
+        cap_recip=tile(cap, F32),
+        cap_k=tile((text, wq), BF),
+        cap_v=tile((text, wq + HEAD), BF),
+        items=tile((group, 1), jnp.int32),
+        key_items=tile((lanes, 1, group), jnp.int32),
+        cos_t=tile(both + (2 * HEAD,), F32),
+        sin_t=tile(both + (2 * HEAD,), F32),
+        norm_in=tile(both + (width,), BF),
+        kq_hat=tile(both + (two,), F32),
+        kq_recip=tile(both + (two,), F32),
+        kv=tile((lanes, group, two), BF),
+        kv_send=sem(3),
+        kv_recv=sem(3),
+        k_all=tile((lanes, group, wq), BF),
+        v_all=tile((lanes, group, wq + HEAD), BF),
+        queries=tile((group, wq), BF),
+        totals=tile((group, 128), F32),
+        cross_logs=tile((group, 128), F32),
+        attn_self=tile((group, wq), F32),
+        attn_cross=tile((group, wq), F32),
+        mix_s=tile((group, two), BF),
+        gate_s=tile(both + (wf,), F32),
+        up_s=tile(both + (wf,), F32),
+        hid_s=tile(both + (wf,), BF),
+        gg_s=tile(both + (wf,), BF),
+        gu_s=tile(both + (wf,), BF),
+        o_send=pltpu.SemaphoreType.DMA,
+        o_recv=pltpu.SemaphoreType.DMA,
+        dp_send=pltpu.SemaphoreType.DMA,
+        dp_recv=pltpu.SemaphoreType.DMA,
+        f_fc=tile((2 * SPLIT, row_dev, 3 * wf), BF),
+        f_fy=tile((SPLIT, row_dev, 3 * wf), BF),
+        fh_s=sem(2),
+        fh_r=sem(2),
+        fz_s=sem(4),
+        fz_r=sem(4),
+        a_part=tile((4 * SPLIT, row_dev, two), BF),
+        a_fc=tile((2 * SPLIT, row_dev, two), BF),
+        a_fy=tile((SPLIT, row_dev, two), BF),
+        ah_s=sem(2),
+        ah_r=sem(2),
+        az_s=sem(4),
+        az_r=sem(4),
+        b_part=tile((4 * SPLIT, row_dev, two), BF),
+        b_fc=tile((2 * SPLIT, row_dev, two), BF),
+        b_fy=tile((SPLIT, row_dev, two), BF),
+        bh_s=sem(2),
+        bh_r=sem(2),
+        bz_s=sem(4),
+        bz_r=sem(4),
+        kv_fc=tile((2, group, two), BF),
+        kv_fy=tile((1, group, two), BF),
+        kvh_s=sem(2),
+        kvh_r=sem(2),
+        t_part=tile((4,) + cap, BF),
+        t_fc=tile((2,) + cap, BF),
+        t_fy=tile((1,) + cap, BF),
+        t_s=sem(2),
+        t_r=sem(2),
+        t_z=tile((SPLIT,) + cap, BF),
+        tz_s=sem(3),
+        tz_r=sem(3),
+        ta_s=sem(3),
+        ta_r=sem(3),
+        dk_acc=tile((lanes, group, wq), F32),
+        dv_acc=tile((lanes, group, wq), F32),
+        dck_acc=tile((text, wq), F32),
+        dcv_acc=tile((text, wq), F32),
+        q_stack=tile((heads * tok_rows, wq), BF),
+        c_stack=tile((heads * tok_rows, wq), BF),
+        m_stack=tile((heads * tok_rows, wq), BF),
+        cp_stack=tile((heads * tok_rows, text), BF),
+        cs_stack=tile((heads * tok_rows, text), BF),
+        p_stack=tile((heads * tok_rows, group), BF),
+        s_stack=tile((heads * tok_rows, group), BF),
+        dq_s=tile((group, wq), BF),
+        dq_raw=tile((group, two), BF),
+        dkv_raw=tile((group, two), BF),
+    )
+    shape = jax.ShapeDtypeStruct
+    outs = dict(
+        out_own=shape((rows, width), F32),
+        out_half=shape((2, rows, width), BF),
+        dp_own=shape((rows, width), F32),
+        dp_half=shape((2, rows, width), BF),
+        f_land=shape((SPLIT, row_dev, 3 * wf), BF),
+        a_land=shape((SPLIT, row_dev, two), BF),
+        b_land=shape((SPLIT, row_dev, two), BF),
+        t_all=shape((lanes, SPLIT) + cap, BF),
+        early=shape((16, width), F32),
+        late=shape((8, width), F32),
+        h_slots=shape((SPLIT, 8, two), F32),
+        text=shape((text, feat_dev), BF),
+    )
+    vmem = pl.BlockSpec(memory_space=pltpu.VMEM)
+    hbm = pl.BlockSpec(memory_space=pl.ANY)
+    smem = pl.BlockSpec(memory_space=pltpu.SMEM)
+    places = dict(caption=hbm, block_item=smem, item_band=smem)
+    names = list(ins) + list(outs) + list(scratch)
+    results = pl.pallas_call(
+        functools.partial(layer_kernel, names),
+        out_shape=tuple(outs.values()),
+        in_specs=[places.get(name, vmem) for name in ins],
+        out_specs=[hbm if name.endswith("_land") else vmem for name in outs],
+        scratch_shapes=list(scratch.values()),
+        compiler_params=pltpu.CompilerParams(
+            collective_id=1, has_side_effects=True, vmem_limit_bytes=VMEM_LIMIT
+        ),
+        name="layer",
+    )(*ins.values())
+    return dict(zip(outs, results))
+
+
+def local_any(
     patches,
     caption,
     band_table,
@@ -416,7 +1769,100 @@
     )
 
 
+def local(
+    patches,
+    caption,
+    band_table,
+    block_item,
+    item_band,
+    positions,
+    out_grad,
+    w_query,
+    w_key,
+    w_value,
+    w_out,
+    w_gate,
+    w_up,
+    w_down,
+    w_ckey,
+    w_cvalue,
+    w_ada,
+    b_ada,
+    g_attn_in,
+    g_attn_out,
+    g_ffn_in,
+    g_ffn_out,
+    g_query,
+    g_key,
+    g_ckey,
+    cross_gate,
+):
+    width = patches.shape[1]
+    wq = w_query.shape[1] // SPLIT
+    rows_in = jnp.concatenate(
+        [jnp.stack([g_attn_in, g_attn_out, g_ffn_in, g_ffn_out]), b_ada.reshape(4, width)]
+    )
+    gains = [vector.reshape(SPLIT, wq) for vector in (g_key, g_query, g_ckey)]
+    pad = jnp.zeros((SPLIT, wq), F32)
+    freqs = FREQ_BASE ** (-(jnp.arange(2 * wq) % (HEAD // 4)).astype(F32) / (HEAD // 4))
+    head_rows = jnp.stack(
+        [
+            jnp.concatenate([gains[0], gains[1]], axis=1),
+            jnp.concatenate([gains[2], pad], axis=1),
+            jnp.concatenate([jnp.repeat(cross_gate, HEAD).reshape(SPLIT, wq), pad], axis=1),
+            jnp.broadcast_to(freqs, (SPLIT, 2 * wq)),
+        ]
+        + [jnp.zeros((SPLIT, 2 * wq), F32)] * 4,
+        axis=1,
+    )
+    done = layer_call(
+        dict(
+            patches=patches,
+            caption=caption,
+            band_table=band_table,
+            block_item=block_item,
+            item_band=item_band,
+            positions=positions,
+            out_grad=out_grad,
+            w_query=w_query,
+            w_key=w_key,
+            w_value=w_value,
+            w_out=w_out,
+            w_gate=w_gate,
+            w_up=w_up,
+            w_down=w_down,
+            w_ckey=w_ckey,
+            w_cvalue=w_cvalue,
+            w_ada=w_ada,
+            rows_in=rows_in,
+            head_rows=head_rows,
+        )
+    )
+    shape = jax.ShapeDtypeStruct
+    like = lambda array: shape(array.shape, F32)
+    vmem = pl.BlockSpec(memory_space=pltpu.VMEM)
+    smem = pl.BlockSpec(memory_space=pltpu.SMEM)
+    results = pl.pallas_call(
+        finish_kernel,
+        out_shape=(
+            like(patches), like(patches), like(w_query), like(w_key), like(w_value), like(w_out),
+            like(w_gate), like(w_up), like(w_down), like(w_ckey), like(w_cvalue), like(w_ada),
+            like(b_ada), like(g_attn_in), like(g_attn_out), like(g_ffn_in), like(g_ffn_out),
+            like(g_query), like(g_key), like(g_ckey), shape((1, 128), F32), like(band_table),
+        ),
+        in_specs=[vmem] * 14 + [smem, vmem],
+        out_specs=[vmem] * 22,
+        compiler_params=pltpu.CompilerParams(vmem_limit_bytes=VMEM_LIMIT),
+        name="finish",
+    )(*done.values(), head_rows, band_table, item_band, w_ada)
+    results = list(results)
+    results[20] = results[20][0, : cross_gate.shape[0]]
+    return tuple(results)
+
+
 def solution(mesh):
+    lanes = mesh.shape["sp"] // SPLIT
+    body = local if lanes == 4 and mesh.shape["tp"] == 2 else local_any
     in_specs = (
         P("sp", None),
         P(),
@@ -469,4 +1915,4 @@
         P("tp"),
         P(None, "sp"),
     )
-    return jax.shard_map(local, mesh=mesh, in_specs=in_specs, out_specs=out_specs, check_vma=False)
+    return jax.shard_map(body, mesh=mesh, in_specs=in_specs, out_specs=out_specs, check_vma=False)

time: 1140 us -> 325 us (0.29); the launches traced: 1120 us -> 324 us
  waiting for transfers between devices: 638 us -> 0 us
  Pallas kernels: 0 us -> 306 us
  blocking collectives: 195 us -> 0 us
  matrix products: 106 us -> 0 us
  local copies, waits for them, and re-layouts: 115 us -> 17.3 us
  other arithmetic: 42.8 us -> 0.08 us
  between operations: 15.9 us -> 0.69 us
  starting transfers between devices: 12.3 us -> 0 us
    pallas_call x0 -> x2, Pallas kernels: none -> 306 us  [the longest x1 299 us: layer_call(): pl.pallas_call(functools.partial(layer_kernel, names), out_shape=tuple(ou...]
    reduce_scatter x10 -> x0, waiting for transfers between devices: 211 us -> none  [the longest x4 108 us: scatter_z(): lax.psum_scatter(block, 'sp', axis_index_groups=along_z, scatter_dimensio...]
    unnamed x21 -> x0, waiting for transfers between devices: 157 us -> none
    all_gather x5 -> x0, waiting for transfers between devices: 139 us -> none  [the longest x4 139 us: gather_z(): lax.all_gather(block, 'sp', axis_index_groups=along_z, axis=0, tiled=False)]
    psum x2 -> x0, waiting for transfers between devices: 130 us -> none  [the longest x1 130 us: local(): lax.psum((jnp.stack([jnp.concatenate([jnp.sum(jnp.where((own_items == ite...]
    all_gather x12 -> x0, blocking collectives: 113 us -> none  [the longest x4 45.7 us: gather_z(): lax.all_gather(block, 'sp', axis_index_groups=along_z, axis=0, tiled=False)]
    dot_general x40 -> x0, matrix products: 95.6 us -> none  [the longest x10 20.3 us: bdot(): return jnp.dot(left, right, preferred_element_type=F32)]
    psum x2 -> x0, blocking collectives: 82 us -> none  [the longest x1 60.1 us: local(): modulation = lax.psum(bdot(cond_low, w_ada), 'sp') + b_ada]
  transfers between devices with their start and end apart: 21 -> 0, of which waited for: 16 -> 0; matrix products, arithmetic and copies ran while one was open for 9% -> 0% of each run, Pallas kernels for 0% -> 0%
where the time goes in v4:
time: 325 us; the launch traced here: 324 us
  Pallas kernels  306 us (94%)
  local copies, waits for them, and re-layouts  17.3 us (5%)
    pallas_call x1, Pallas kernels, layer_call(): pl.pallas_call(functools.partial(layer_kernel, names), out_shape=tuple(ou...  299 us
    unnamed x4, local copies, waits for them, and re-layouts  8.02 us
    pallas_call x1, Pallas kernels, local(): pl.pallas_call(finish_kernel, out_shape=(like(patches), like(patches), li...  7.64 us

profile of v4, /device:TPU:0, one launch (start us, length us, event | category | flops | bytes accessed | tf_op | source)
XLA Modules:
  0.0 324.4 jit_solution(10610906754835330136)
XLA Ops:
  0.7 0.7 broadcast_in_dim.8
  1.4 0.8 reshape.60
  2.2 0.8 reshape.59
  2.9 0.1 pad_maximum_fusion
  3.0 0.8 reshape.61
  3.8 0.1 broadcast_in_dim.9
  3.9 0.1 broadcast_in_dim.10
  4.0 0.7 stack.27
  4.7 0.7 stack.28
  5.4 0.7 stack.29
  6.1 0.7 stack.30
  6.8 0.8 reshape.58
  7.5 0.7 concatenate.12.refs_17_
  8.2 0.7 stack.35.refs_18_.head_rows
  8.9 1.7 copy.52.refs_10_
  10.6 2.0 copy.53.refs_13_
  12.6 298.6 %layer.1 = (f32[64,1536]{1,0:T(8,128)}, bf16[2,64,1536]{2,1,0:T(8,128)(2,1)}, f32[64,1536]{1,0:T(8,128)}, bf16[2,64,1536]{2,1,0:T(8,128)(2,1)}, bf16[4,96,1536]{...) custom-call(bf16[128,1536]{1,0:T(8,128)(2,1)} %refs_0_.1, ...), custom_call_target="tpu_custom_call" | custom-call | tf_op jit(solution)/shard_map/layer/pallas_call | solution.py:1418
  311.3 7.6 %finish.1 = (f32[128,1536]{1,0:T(8,128)}, f32[128,1536]{1,0:T(8,128)}, f32[96,768]{1,0:T(8,128)}, f32[96,768]{1,0:T(8,128)}, f32[96,768]{1,0:T(8,128)}, /*index=...) custom-call(f32[64,1536]{1,0:T(8,128)} %get-tuple-element.56.out_own, ...), custom_call_target="tpu_custom_call" | custom-call | tf_op jit(solution)/shard_map/finish/pallas_call | solution.py:1845
  318.9 1.2 slice_bitcast_fusion
  320.1 1.9 copy.54
  321.9 2.4 copy.55
  (8 shorter events, 0.1 us)

commit v5 on v4

--- a/solution.py
+++ b/solution.py
@@ -266,43 +266,61 @@
         return total
 
 
-def flow(place, gather, scatter, work, carry, between=None):
-    def order(i):
-        return place.block(i if gather is not None else 3 - i)
-
+def flow(place, gather, work, carry, between=None):
     def step(i, carry):
-        if gather is not None:
-
-            @pl.when((i >= 1) & (i < 3))
-            def _():
-                gather.pass_on(i + 1)
-
-            gather.arrive(i)
+        @pl.when(i < 3)
+        def _():
+            gather.pass_on(i + 1)
+
+        gather.arrive(i)
         if between is not None:
-            pl.when(i == 2)(between)
-        z = order(i)
+            between(i)
+        return work(place.block(i), carry)
+
+    return lax.fori_loop(0, SPLIT, step, carry)
+
+
+def flow_and_sum(place, gather, scatter, work, before=None):
+    def start(i):
+        scatter.across(place.block(jnp.int32(i))).start()
+
+    def pass_on(i):
+        scatter.pass_on(place.block(jnp.int32(i)))
+
+    def begin(i):
+        if before is not None:
+            pl.when(i == 0)(before)
+
+        @pl.when(i == 3)
+        def _():
+            start(2)
+            start(1)
+
+    def step(z, carry):
+        work(z, carry)
+        return carry
+
+    flow(place, gather, step, 0, begin)
+    start(3)
+    pass_on(2)
+    start(0)
+    pass_on(1)
+    pass_on(3)
+
+
+def work_and_sum(place, scatter, work, carry):
+    def step(i, carry):
+        z = place.block(3 - i)
         carry = work(z, carry)
-        if scatter is not None:
-            scatter.across(z).start()
-        if gather is not None:
-
-            @pl.when(i == 0)
-            def _():
-                gather.pass_on(1)
-
-        if scatter is not None:
-            first = 2 if gather is not None else 1
-
-            @pl.when(i >= first)
-            def _():
-                scatter.pass_on(order(i - 1))
+        scatter.across(z).start()
+
+        @pl.when(i >= 1)
+        def _():
+            scatter.pass_on(place.block(4 - i))
 
         return carry
 
-    carry = lax.fori_loop(0, SPLIT, step, carry)
-    if scatter is not None and gather is not None:
-        scatter.pass_on(order(jnp.int32(3)))
-    return carry
+    return lax.fori_loop(0, SPLIT, step, carry)
 
 
 class LaneGather:
@@ -507,6 +525,93 @@
         self.keep.wait()
 
 
+class HomeByZ:
+    def __init__(self, place, part, from_c, from_y, land, send, recv):
+        self.place, self.part, self.from_c, self.from_y = place, part, from_c, from_y
+        self.land, self.send, self.recv = land, send, recv
+
+    def blocks(self, at):
+        return self.part.at[at, :, pl.ds(0, self.from_y.shape[2])]
+
+    def to_c(self, z):
+        place = self.place
+        return remote(
+            self.blocks(pl.ds(z * 4 + (1 - place.c) * 2, 2)),
+            self.from_c.at[pl.ds(z * 2, 2)],
+            self.send.at[z],
+            self.recv.at[z],
+            place.c_peer,
+        )
+
+    def to_y(self, z):
+        place = self.place
+        return remote(
+            self.blocks(z * 4 + place.c * 2 + 1 - place.y),
+            self.from_y.at[z],
+            self.send.at[4 + z],
+            self.recv.at[4 + z],
+            place.y_peer,
+        )
+
+    def to_z(self, z):
+        place = self.place
+        return remote(
+            self.blocks(z * 4 + place.c * 2 + place.y),
+            self.land.at[place.z],
+            self.send.at[8 + z],
+            self.recv.at[8 + place.z],
+            place.at_z(z),
+        )
+
+    def keep(self):
+        place = self.place
+        return pltpu.make_async_copy(
+            self.blocks(place.z * 4 + place.c * 2 + place.y),
+            self.land.at[place.z],
+            self.recv.at[8 + place.z],
+        )
+
+    def start(self, z):
+        self.to_c(z).start()
+
+    def step(self, z):
+        self.to_c(z).wait_recv()
+        place = self.place
+        at = z * 4 + place.c * 2 + 1 - place.y
+        near = self.blocks(at)[...].astype(F32) + self.from_c[z * 2 + 1 - place.y].astype(F32)
+        self.blocks(at)[...] = near.astype(BF)
+        self.to_y(z).start()
+
+    def leave(self, z):
+        place = self.place
+        self.to_y(z).wait_recv()
+        at = z * 4 + place.c * 2 + place.y
+        near = self.blocks(at)[...].astype(F32) + self.from_c[z * 2 + place.y].astype(F32)
+        self.blocks(at)[...] = (near + self.from_y[z].astype(F32)).astype(BF)
+
+        @pl.when(z == place.z)
+        def _():
+            self.keep().start()
+
+        @pl.when(z != place.z)
+        def _():
+            self.to_z(z).start()
+
+    def finish(self):
+        place = self.place
+        self.keep().wait()
+        for d in (1, 2, 3):
+            z = place.z_to(d)
+            block = self.land.at[z]
+            remote(
+                block, block, self.send.at[8 + z], self.recv.at[8 + z], place.at_z(z)
+            ).wait_recv()
+            self.to_z(z).wait_send()
+        for z in range(SPLIT):
+            self.to_c(z).wait_send()
+            self.to_y(z).wait_send()
+
+
 class SpreadZ:
     def __init__(self, place, buf, send, recv):
         own = buf.at[place.z]
@@ -569,6 +674,15 @@
 
 def of_head(value, head):
     return jnp.where(head_lanes(value.shape, head), value, jnp.zeros_like(value))
+
+
+def gate_lanes(cross_gate, z, wq):
+    heads = wq // HEAD
+    lane = lax.broadcasted_iota(jnp.int32, (1, wq), 1) // HEAD
+    gates = jnp.zeros((1, wq), F32)
+    for head in range(heads):
+        gates = jnp.where(lane == head, cross_gate[z * heads + head], gates)
+    return gates
 
 
 def lane_order(g):
@@ -598,29 +712,31 @@
         at = slice(i * wq, (i + 1) * wq)
         r.qkvo_in[i, :, 0:wq] = r.w_key[:, at]
         r.qkvo_in[i, :, wq:two] = r.w_query[:, at]
-        r.qkvo_in[i, :, two : two + wq] = r.w_out[at, :].T
+        r.qkvo_in[i, :, two : two + wq] = r.w_out[:, at]
         r.qkvo_in[i, :, two + wq : 2 * two] = r.w_value[:, at]
     pl.semaphore_wait(barrier, len(peers))
 
+    pre, sig = conditioning(r.band_table, r.item_band)
+    act = jnp.concatenate([pre * sig, jnp.zeros((6, pre.shape[1]), F32)], axis=0).astype(BF)
+    r.m_acc[0] = bdot(act, r.w_ada[...])[:ITEMS]
+    along = [place.c_peer, place.y_peer, place.z_pair, place.z_far]
+    sums = AllSum(along, r.m_acc, r.m_land, r.m_send, r.m_recv)
+    sums.start()
     weights = WeightGather(place, r.qkvo_in, r.qkvo, r.w_send, r.w_recv)
     weights.start(1)
     mine = pl.ds(pl.multiple_of(x * rows, rows), rows)
     tokens = Gather(place, r.x_buf, r.x_send, r.x_recv)
     tokens.own[...] = r.patches[mine]
     tokens.start()
-    along = [place.c_peer, place.y_peer, place.z_pair, place.z_far]
-    sums = AllSum(along, r.m_acc, r.m_land, r.m_send, r.m_recv)
-    pre, sig = conditioning(r.band_table, r.item_band)
-    act = jnp.concatenate([pre * sig, jnp.zeros((6, pre.shape[1]), F32)], axis=0).astype(BF)
-    r.m_acc[0] = bdot(act, r.w_ada[...])[:ITEMS]
-    sums.start()
+    for i in (2, 3):
+        weights.start(i)
     spots = SpreadZ(place, r.pos_buf, r.pos_send, r.pos_recv)
     spots.own[...] = jnp.concatenate(
         [r.positions[...].astype(F32), jnp.zeros((6, tok_rows), F32)], axis=0
     )
     spots.start()
     weights.pass_own()
-    weights.start(2)
+    sums.step()
     text_copy.wait()
     words = r.cap_part.shape[1]
     caption = LaneScatter(place, r.cap_part, r.cap_fc, r.cap_fy, r.cap_s, r.cap_r)
@@ -633,15 +749,6 @@
                     lane_g * words : (lane_g + 1) * words, i * wq : (i + 1) * wq
                 ]
     caption.start()
-    for i in range(SPLIT):
-        at = slice(i * wf, (i + 1) * wf)
-        r.ffn_in[i, :, 0:wf] = r.w_gate[:, at]
-        r.ffn_in[i, :, wf : 2 * wf] = r.w_up[:, at]
-        r.ffn_in[i, :, 2 * wf : 3 * wf] = r.w_down[at, :].T
-    sums.step()
-    sums.step()
-    caption.step()
-    weights.start(3)
     tokens.pass_on(1)
     weights.pass_z(1)
     sums.step()
@@ -661,20 +768,47 @@
     r.items[...] = token_item
     for i in range(4):
         r.key_items[i] = key_item[:, i * group : (i + 1) * group]
+        column = jnp.zeros((group, 1), jnp.int32)
+        for j in range(SPLIT * blocks):
+            value = r.block_item[(j // blocks * place.lanes + i) * blocks + j % blocks]
+            column = jnp.where(token == j, value, column)
+        r.key_cols[i] = column
+    for i in range(SPLIT):
+        at = slice(i * wf, (i + 1) * wf)
+        r.ffn_in[i, :, 0:wf] = r.w_gate[:, at]
+        r.ffn_in[i, :, wf : 2 * wf] = r.w_up[:, at]
+        r.ffn_in[i, :, 2 * wf : 3 * wf] = r.w_down[:, at]
+    tokens.pass_on(2)
+    weights.pass_z(2)
+    sums.step()
+
     own_at = pl.ds(pl.multiple_of(z * tok_rows + x * rows, rows), rows)
 
     mean = segments(two)
     mean_q = segments(wq)
     lane = lax.broadcasted_iota(jnp.int32, (1, two), 1)
-    gain_kq = r.head_rows[z, 0:1]
-    gain_ckey = r.head_rows[z, 1:2]
-    gates = jnp.tanh(r.head_rows[z, 2:3])[:, :wq]
-    freqs = r.head_rows[z, 3:4][:, : 2 * HEAD]
-    gain_in, gain_attn = r.rows_in[0:1], r.rows_in[1:2]
-    gain_ffn, gain_out = r.rows_in[2:3], r.rows_in[3:4]
+    gain_in, gain_attn, gain_ffn, gain_out = (
+        ref[...].reshape(1, width) for ref in (r.g_attn_in, r.g_attn_out, r.g_ffn_in, r.g_ffn_out)
+    )
+
+    def own_heads(ref):
+        whole = ref[...].reshape(1, SPLIT * wq)
+        part = whole[:, 0:wq]
+        for i in range(1, SPLIT):
+            part = jnp.where(z == i, whole[:, i * wq : (i + 1) * wq], part)
+        return part
+
+    gain_kq = jnp.concatenate([own_heads(r.g_key), own_heads(r.g_query)], axis=1)
+    gain_ckey = own_heads(r.g_ckey)
+    gain_ckey = jnp.concatenate([gain_ckey, jnp.zeros_like(gain_ckey)], axis=1)
+    gates = jnp.tanh(gate_lanes(r.cross_gate, z, wq))
+    lane_row = lax.broadcasted_iota(jnp.int32, (1, 2 * HEAD), 1)
+    quarter = HEAD // 4
+    freqs = jnp.ones((1, 2 * HEAD), F32)
+    for i in range(1, quarter):
+        freqs = jnp.where(lane_row % quarter == i, FREQ_BASE ** (-i / quarter), freqs)
 
     spots.finish()
-    lane_row = lax.broadcasted_iota(jnp.int32, (1, 2 * HEAD), 1)
     by_row = (lane_row // (HEAD // 2)) % 2 == 0
     sign = jnp.where((lane_row // (HEAD // 4)) % 2 == 0, -1.0, 1.0)
     for i in range(SPLIT):
@@ -683,36 +817,19 @@
         r.cos_t[i] = jnp.cos(angle)
         r.sin_t[i] = jnp.sin(angle) * sign
 
-    caption.finish()
-    cap_turn = TurnZ(place, r.cap_part, caption.base, r.cap_z, r.cz_send, r.cz_recv)
-    cap_turn.start()
-    for i in (2, 3):
-        tokens.pass_on(i)
-        weights.pass_z(i)
-    for i in range(4):
-        weights.pass_y(i)
+    tokens.pass_on(3)
+    weights.pass_z(3)
     feed = WeightGather(place, r.ffn_in, r.ffn, r.f_send, r.f_recv)
     for i in (1, 2, 3):
         feed.start(i)
-    feed.pass_own()
-    r.mod[...] = sums.step() + jnp.concatenate(
-        [r.rows_in[4 + i : 5 + i] for i in range(4)], axis=1
-    )
-    cap_turn.finish()
-    cap_raw = (r.cap_z[0].astype(F32) + r.cap_z[1].astype(F32)) + (
-        r.cap_z[2].astype(F32) + r.cap_z[3].astype(F32)
-    )
-    cap_recip = lax.rsqrt(head_mean(cap_raw * cap_raw, mean) + EPS)
-    cap_hat = cap_raw * cap_recip
-    r.cap_hat[...] = cap_hat
-    r.cap_recip[...] = cap_recip
-    cap_gather = LaneGather(place, r.cap_kv, r.ckv_send, r.ckv_recv)
-    cap_gather.own[...] = jnp.where(lane < wq, cap_hat * gain_ckey, cap_raw).astype(BF)
-    cap_gather.start()
+    for i in range(4):
+        weights.pass_y(i)
+    r.mod[...] = sums.step() + r.b_ada[...].reshape(1, 4 * width)
     for i in range(4):
         tokens.arrive(i)
-    cap_gather.pass_on()
+    caption.step()
     weights.finish()
+    feed.pass_own()
 
     keep = LaneGather(place, r.kv, r.kv_send, r.kv_recv)
 
@@ -731,6 +848,7 @@
         factor = gain_in * (1.0 + item_rows(r.mod, r.items[span(i)], 0, width))
         norm = (unit * factor).astype(BF)
         r.norm_in[i] = norm
+        r.hat_in[i] = unit.astype(BF)
         raw = bdot(norm, w_kq())
         own_v = bdot(norm, w_ov())
         recip = lax.rsqrt(head_mean(raw * raw, mean) + EPS)
@@ -747,6 +865,10 @@
 
     lax.fori_loop(0, SPLIT, project, 0)
     keep.start()
+
+    caption.finish()
+    cap_turn = TurnZ(place, r.cap_part, caption.base, r.cap_z, r.cz_send, r.cz_recv)
+    cap_turn.start()
     slot_lane = lax.broadcasted_iota(jnp.int32, (1, r.totals.shape[1]), 1)
     ones = jnp.where(lax.broadcasted_iota(jnp.int32, (1, HEAD), 1) == 0, 1.0, 0.0).astype(BF)
 
@@ -785,20 +907,34 @@
         ref[...] = jnp.zeros_like(ref)
     split_lump(g)
     attend_into(g)
+    cap_turn.finish()
+    cap_raw = (r.cap_z[0].astype(F32) + r.cap_z[1].astype(F32)) + (
+        r.cap_z[2].astype(F32) + r.cap_z[3].astype(F32)
+    )
+    cap_recip = lax.rsqrt(head_mean(cap_raw * cap_raw, mean) + EPS)
+    cap_hat = cap_raw * cap_recip
+    r.cap_hat[...] = cap_hat
+    r.cap_recip[...] = cap_recip
+    cap_gather = LaneGather(place, r.cap_kv, r.ckv_send, r.ckv_recv)
+    cap_gather.own[...] = jnp.where(lane < wq, cap_hat * gain_ckey, cap_raw).astype(BF)
+    cap_gather.start()
+    keep.from_c.wait_recv()
+    split_lump(place.g_c)
+    attend_into(place.g_c)
+    cap_gather.pass_on()
+    keep.pass_on()
+    feed.pass_z(1)
+    split_lump(place.g_y)
+    attend_into(place.g_y)
+    feed.pass_z(2)
+    feed.pass_y(0)
     cap_gather.finish()
     kv_text = r.cap_kv[...].reshape(4 * words, two)
     r.cap_k[...] = kv_text[:, :wq]
     r.cap_v[...] = with_ones(kv_text[:, wq:])
-    feed.pass_z(1)
-    keep.from_c.wait_recv()
-    split_lump(place.g_c)
-    attend_into(place.g_c)
-    feed.pass_z(2)
-    keep.pass_on()
-    split_lump(place.g_y)
-    attend_into(place.g_y)
+    lax.fori_loop(0, heads, cross, 0)
     feed.pass_z(3)
-    lax.fori_loop(0, heads, cross, 0)
+    feed.pass_y(1)
     keep.from_diagonal.wait_recv()
     split_lump(place.g_yc)
     attend_into(place.g_yc)
@@ -828,8 +964,8 @@
         return Scatter(place, r.part, r.from_x, r.from_z, send, recv)
 
     out_sum = scatter_of(r.s1, r.r1)
-    flow(place, None, out_sum, blend, 0)
-    for i in range(4):
+    work_and_sum(place, out_sum, blend, 0)
+    for i in (2, 3):
         feed.pass_y(i)
     branch = out_sum.finish()
 
@@ -844,7 +980,6 @@
     norms.start()
     tokens.finish()
     keep.sent()
-    feed.finish()
 
     def f_weights(index):
         return r.ffn[:, :, index * wf : (index + 1) * wf].reshape(width, wf)
@@ -861,7 +996,7 @@
         return carry
 
     down = scatter_of(r.s2, r.r2)
-    flow(place, norms, down, forward, 0)
+    flow_and_sum(place, norms, down, forward, feed.finish)
     ffn = down.finish()
     norms.finish()
 
@@ -904,25 +1039,30 @@
         return carry
 
     back = scatter_of(r.s3, r.r3)
-    flow(place, grads, back, backward, 0)
+    flow_and_sum(place, grads, back, backward)
 
     block_rows = r.ffn.shape[1]
     step_cols = 4 * block_rows
 
+    f_home = HomeByZ(place, r.ffn, r.f_fc, r.f_fy, r.f_land, r.f_s, r.f_r)
+
     def ffn_matrices(i, carry):
-        cols = pl.ds(pl.multiple_of(i * step_cols, step_cols), step_cols)
+        target = place.block(3 - i)
+        cols = pl.ds(pl.multiple_of(target * step_cols, step_cols), step_cols)
         norm = r.n_buf[:, :, cols].reshape(group, step_cols)
         grad = r.g_buf[:, :, cols].reshape(group, step_cols)
         for j, (left, right) in enumerate(((norm, r.gg_s), (norm, r.gu_s), (grad, r.hid_s))):
             block = t_dot(left, right[...].reshape(group, wf)).astype(BF)
             block = block.reshape(4, block_rows, wf)
             for other in range(4):
-                r.ffn[lane_order(other) * SPLIT + i, :, j * wf : (j + 1) * wf] = block[other]
+                at = target * 4 + lane_order(other)
+                r.ffn[at, :, j * wf : (j + 1) * wf] = block[other]
+        f_home.start(target)
         return carry
 
     lax.fori_loop(0, SPLIT, ffn_matrices, 0)
-    f_home = LaneScatter(place, r.ffn, r.f_fc, r.f_fy, r.fh_s, r.fh_r)
-    f_home.start()
+    f_home.step(place.block(jnp.int32(3)))
+    f_home.step(place.block(jnp.int32(2)))
     grad_norm = back.finish()
     grads.finish()
     d_resid = grad_out + normed_back(grad_norm * factor_three, hat_three, recip_three)
@@ -941,12 +1081,12 @@
     r.e_acc[0, 5:6] = gate_sums[1]
     r.e_acc[0, 6:7] = scale_sums[0]
     r.e_acc[0, 7:8] = scale_sums[1]
+    early.start()
 
     r.dk_acc[...] = jnp.zeros_like(r.dk_acc)
     r.dv_acc[...] = jnp.zeros_like(r.dv_acc)
     r.dck_acc[...] = jnp.zeros_like(r.dck_acc)
     r.dcv_acc[...] = jnp.zeros_like(r.dcv_acc)
-    f_home.step()
 
     def attend_back(i, gate_sum):
         at = span(i)
@@ -957,60 +1097,97 @@
         delta = head_mean(mix_f * r.attn_self[at], mean_q) * HEAD
         gate_sum = gate_sum + jnp.sum(mix_f * r.attn_cross[at], axis=0, keepdims=True)
         query = r.queries[at]
-        logs = r.totals[at]
-        cross_logs = r.cross_logs[at]
+        per_row = jnp.zeros((tok_rows, 128), F32)
+        for head in range(heads):
+            stack = slice(head * tok_rows, (head + 1) * tok_rows)
+            r.q_stack[stack] = of_head(query, head)
+            r.c_stack[stack] = of_head(d_cross, head)
+            r.m_stack[stack] = of_head(d_mix, head)
+            for part, column in enumerate(
+                (
+                    r.totals[at][:, head : head + 1],
+                    delta[:, head * HEAD : head * HEAD + 1],
+                    r.cross_logs[at][:, head : head + 1],
+                )
+            ):
+                per_row = per_row + jnp.where(slot_lane == part * heads + head, column, 0.0)
+        per_row = per_row.T
+        logs, deltas, cross_logs = (
+            jnp.concatenate(
+                [per_row[part * heads + head : part * heads + head + 1] for head in range(heads)],
+                axis=1,
+            )
+            for part in range(3)
+        )
+        item_row = jnp.concatenate(
+            [r.key_items[g, :, pl.ds(pl.multiple_of(i * tok_rows, 128), tok_rows)]] * heads, axis=1
+        )
+        query_s, cross_s, mix_s = r.q_stack[...], r.c_stack[...], r.m_stack[...]
+        probs = jnp.exp(dot_t(r.cap_k[...], query_s) - cross_logs)
+        d_probs = dot_t(r.cap_v[:, :wq], cross_s)
+        inner = jnp.sum(probs * d_probs, axis=0, keepdims=True)
+        d_scores = (probs * (d_probs - inner)).astype(BF)
+        r.dck_acc[...] += bdot(d_scores, query_s)
+        r.dcv_acc[...] += bdot(probs.astype(BF), cross_s)
+        r.dq_stack[...] = t_dot(d_scores, r.cap_k[...])
+
+        def keys(j, carry):
+            same = r.key_cols[j] == item_row
+            scores = jnp.where(same, dot_t(r.k_all[j], query_s), NEG)
+            probs = jnp.exp(scores - logs)
+            d_probs = dot_t(r.v_all[j, :, :wq], mix_s)
+            d_scores = (probs * (d_probs - deltas)).astype(BF)
+            r.dk_acc[j] += bdot(d_scores, query_s)
+            r.dv_acc[j] += bdot(probs.astype(BF), mix_s)
+            r.dq_stack[...] += t_dot(d_scores, r.k_all[j])
+            return carry
+
+        lax.fori_loop(0, 4, keys, 0)
         dq = jnp.zeros((tok_rows, wq), F32)
         for head in range(heads):
             stack = slice(head * tok_rows, (head + 1) * tok_rows)
-            query_h = of_head(query, head)
-            cross_h = of_head(d_cross, head)
-            r.q_stack[stack] = query_h
-            r.c_stack[stack] = cross_h
-            r.m_stack[stack] = of_head(d_mix, head)
-            probs = jnp.exp(dot_t(query_h, r.cap_k[...]) - cross_logs[:, head : head + 1])
-            d_probs = dot_t(cross_h, r.cap_v[:, :wq])
-            inner = jnp.sum(probs * d_probs, axis=1, keepdims=True)
-            d_scores = (probs * (d_probs - inner)).astype(BF)
-            r.cp_stack[stack] = probs.astype(BF)
-            r.cs_stack[stack] = d_scores
-            dq = dq + of_head(bdot(d_scores, r.cap_k[...]), head)
-        r.dck_acc[...] += t_dot(r.cs_stack[...], r.q_stack[...])
-        r.dcv_acc[...] += t_dot(r.cp_stack[...], r.c_stack[...])
-        for j in range(4):
-            same = r.items[at] == r.key_items[j]
-            for head in range(heads):
-                stack = slice(head * tok_rows, (head + 1) * tok_rows)
-                scores = jnp.where(same, dot_t(r.q_stack[stack], r.k_all[j]), NEG)
-                probs = jnp.exp(scores - logs[:, head : head + 1])
-                d_probs = dot_t(r.m_stack[stack], r.v_all[j, :, :wq])
-                d_scores = (probs * (d_probs - delta[:, head * HEAD : head * HEAD + 1])).astype(BF)
-                r.p_stack[stack] = probs.astype(BF)
-                r.s_stack[stack] = d_scores
-                dq = dq + of_head(bdot(d_scores, r.k_all[j]), head)
-            r.dk_acc[j] += t_dot(r.s_stack[...], r.q_stack[...])
-            r.dv_acc[j] += t_dot(r.p_stack[...], r.m_stack[...])
+            dq = dq + of_head(r.dq_stack[stack], head)
         r.dq_s[at] = (dq * scale).astype(BF)
         return gate_sum
 
-    f_turn = TurnZ(place, r.ffn, f_home.base, r.f_land, r.fz_s, r.fz_r)
-
-    def turn_ffn():
-        f_home.finish()
-        f_turn.start()
-
-    gate_sum = flow(place, attn_grads, None, attend_back, jnp.zeros((1, wq), F32), turn_ffn)
-    early.start()
-
+    def ffn_home(i):
+        for step in range(4):
+
+            @pl.when(i == step)
+            def _():
+                early.step()
+
+        @pl.when(i < 2)
+        def _():
+            f_home.step(place.block(1 - i))
+
+        @pl.when(i >= 1)
+        def _():
+            f_home.leave(place.block(4 - i))
+
+    gate_sum = flow(place, attn_grads, attend_back, jnp.zeros((1, wq), F32), ffn_home)
     keys_home = LaneScatter(place, r.kv, r.kv_fc, r.kv_fy, r.kvh_s, r.kvh_r)
-    for i in range(4):
-        r.kv[lane_order(i)] = jnp.concatenate([r.dk_acc[i], r.dv_acc[i]], axis=1).astype(BF)
-    keys_home.start()
+
+    def store_keys(i, carry):
+        lane_c, lane_y = lax.rem(place.c + 1 + lax.div(i, 2), 2), lax.rem(i, 2)
+        both = [r.dk_acc[lane_y * 2 + lane_c], r.dv_acc[lane_y * 2 + lane_c]]
+        r.kv[lane_c * 2 + lane_y] = jnp.concatenate(both, axis=1).astype(BF)
+
+        @pl.when(i == 1)
+        def _():
+            keys_home.start()
+
+        return carry
+
+    lax.fori_loop(0, 4, store_keys, 0)
     cap_home = LaneScatter(place, r.t_part, r.t_fc, r.t_fy, r.t_s, r.t_r)
     for i in range(4):
         at = slice(i * words, (i + 1) * words)
         d_cap = jnp.concatenate([r.dck_acc[at], r.dcv_acc[at]], axis=1)
         r.t_part[lane_order(i)] = d_cap.astype(BF)
     cap_home.start()
+
+    key_lanes = lane < wq
 
     def turn_back(i, grad):
         cos = jnp.concatenate([r.cos_t[i]] * heads, axis=1)
@@ -1029,85 +1206,84 @@
         r.dq_raw[span(i)] = grad
         return query_sum + gain_sum
 
+    query_sum = lax.fori_loop(0, SPLIT, raw_queries, jnp.zeros((1, two), F32))
     keys_home.step()
-    early.step()
-    cap_home.step()
-    query_sum = lax.fori_loop(0, SPLIT, raw_queries, jnp.zeros((1, two), F32))
-
-    def store_part(part, i, block):
+    f_home.leave(place.block(jnp.int32(0)))
+
+    def store_part(home, target, block):
         block = block.astype(BF).reshape(4, block_rows, two)
         for other in range(4):
-            part[lane_order(other) * SPLIT + i] = block[other]
+            home.blocks(target * 4 + lane_order(other))[...] = block[other]
+        home.start(target)
+
+    a_home = HomeByZ(place, r.a_part, r.a_fc, r.a_fy, r.a_land, r.a_s, r.a_r)
+    b_home = HomeByZ(place, r.qkvo, r.b_fc, r.b_fy, r.b_land, r.b_s, r.b_r)
 
     def matrices_oq(i, carry):
-        cols = pl.ds(pl.multiple_of(i * step_cols, step_cols), step_cols)
+        target = place.block(3 - i)
+        cols = pl.ds(pl.multiple_of(target * step_cols, step_cols), step_cols)
         above = r.x_buf[:, :, cols].reshape(group, step_cols)
         left = r.norm_in[:, :, cols].reshape(group, step_cols)
-        store_part(r.a_part, i, t_dot(above, r.mix_s[...]) + t_dot(left, r.dq_raw[...]))
+        store_part(a_home, target, t_dot(above, r.mix_s[...]) + t_dot(left, r.dq_raw[...]))
         return carry
 
     lax.fori_loop(0, SPLIT, matrices_oq, 0)
-    a_home = LaneScatter(place, r.a_part, r.a_fc, r.a_fy, r.ah_s, r.ah_r)
-    a_home.start()
-    early.step()
-    a_home.step()
+    cap_home.step()
+    keys_home.finish()
+
+    def raw_keys(i, carry):
+        key_sum, first, second = carry
+        total = r.kv[keys_home.base, span(i)].astype(F32)
+        grad, gain_sum = turn_back(i, jnp.where(key_lanes, total, 0.0))
+        r.dkv_raw[span(i)] = jnp.where(key_lanes, grad.astype(F32), total).astype(BF)
+        d_kq = jnp.where(key_lanes, grad.astype(F32), r.dq_raw[span(i)].astype(F32)).astype(BF)
+        d_ov = jnp.where(key_lanes, 0.0, total).astype(BF)
+        d_norm = dot_t(d_kq, w_kq()) + dot_t(d_ov, w_ov())
+        r.part[i] = d_norm.astype(BF).reshape(2, rows, width)
+        by_item = item_sums(d_norm * r.hat_in[i].astype(F32), r.items[span(i)])
+        return key_sum + gain_sum, first + by_item[0], second + by_item[1]
+
+    in_sum = scatter_of(r.s4, r.r4)
+    zeros = jnp.zeros((1, width), F32)
+    key_sum, *item_parts = work_and_sum(
+        place, in_sum, raw_keys, (jnp.zeros((1, two), F32), zeros, zeros)
+    )
+    late = AllSum(everywhere, r.l_acc, r.l_land, r.l_send, r.l_recv)
+    r.l_acc[0] = jnp.concatenate(item_parts, axis=0)
+    late.start()
 
     cap_home.finish()
     d_cap = r.t_part[cap_home.base].astype(F32)
     hat = r.cap_hat[...]
-    key_lanes = lane < wq
     cap_sum = jnp.sum(jnp.where(key_lanes, d_cap * hat, 0.0), axis=0, keepdims=True)
     d_hat = d_cap * jnp.where(key_lanes, gain_ckey, 0.0)
     d_raw = r.cap_recip[...] * (d_hat - hat * head_mean(d_hat * hat, mean))
     cap_spread = SpreadZ(place, r.t_z, r.tz_s, r.tz_r)
     cap_spread.own[...] = jnp.where(key_lanes, d_raw, d_cap).astype(BF)
     cap_spread.start()
-    keys_home.finish()
-
-    def raw_keys(i, key_sum):
-        total = r.kv[keys_home.base, span(i)].astype(F32)
-        grad, gain_sum = turn_back(i, jnp.where(key_lanes, total, 0.0))
-        r.dkv_raw[span(i)] = jnp.where(key_lanes, grad.astype(F32), total).astype(BF)
-        d_kq = jnp.where(key_lanes, grad.astype(F32), r.dq_raw[span(i)].astype(F32)).astype(BF)
-        d_ov = jnp.where(key_lanes, 0.0, total).astype(BF)
-        r.part[i] = (
-            (dot_t(d_kq, w_kq()) + dot_t(d_ov, w_ov())).astype(BF).reshape(2, rows, width)
-        )
-        return key_sum + gain_sum
-
-    in_sum = scatter_of(r.s4, r.r4)
-    key_sum = flow(place, None, in_sum, raw_keys, jnp.zeros((1, two), F32))
+    for i in range(4):
+        a_home.step(place.block(jnp.int32(3 - i)))
 
     def matrices_kv(i, carry):
-        cols = pl.ds(pl.multiple_of(i * step_cols, step_cols), step_cols)
+        target = place.block(3 - i)
+        cols = pl.ds(pl.multiple_of(target * step_cols, step_cols), step_cols)
         left = r.norm_in[:, :, cols].reshape(group, step_cols)
-        store_part(r.b_part, i, t_dot(left, r.dkv_raw[...]))
+        store_part(b_home, target, t_dot(left, r.dkv_raw[...]))
         return carry
 
     lax.fori_loop(0, SPLIT, matrices_kv, 0)
-    b_home = LaneScatter(place, r.b_part, r.b_fc, r.b_fy, r.bh_s, r.bh_r)
-    b_home.start()
     heads_sum = AllSum(along[:2], r.h_acc, r.h_land, r.h_send, r.h_recv)
     r.h_acc[0] = jnp.zeros(r.h_acc.shape[1:], F32)
     r.h_acc[0, 0:1] = jnp.where(key_lanes, key_sum, query_sum)
     r.h_acc[0, 1:2] = cap_sum
     r.h_acc[0, 2:3] = jnp.concatenate([gate_sum, jnp.zeros_like(gate_sum)], axis=1)
     heads_sum.start()
-    a_home.finish()
-    a_turn = TurnZ(place, r.a_part, a_home.base, r.a_land, r.az_s, r.az_r)
-    a_turn.start()
-    cap_spread.finish()
-    cap_all = LaneGather(place, r.t_all, r.ta_s, r.ta_r)
-    cap_all.own[...] = r.t_z[...]
-    cap_all.start()
-    b_home.step()
-    heads_sum.step()
-    heads_spread = SpreadZ(place, r.h_slots, r.hz_send, r.hz_recv)
-    heads_spread.own[...] = heads_sum.step()
-    heads_spread.start()
-    early.step()
-    early.step()
-    cap_all.pass_on()
+    late.step()
+    for i in range(4):
+        b_home.step(place.block(jnp.int32(3 - i)))
+    late.step()
+    for i in range(4):
+        a_home.leave(place.block(jnp.int32(3 - i)))
 
     d_norm = in_sum.finish()
     hat, recip = normed_pair(r.patches[mine].astype(F32))
@@ -1117,33 +1293,43 @@
     r.dp_half[0] = d_patches.astype(BF)
     dp_copy = remote(r.dp_half.at[0], r.dp_half.at[1], r.dp_send, r.dp_recv, place.x_peer)
     dp_copy.start()
-    scale_sums = item_sums(d_norm * hat * gain_in, item)
-    late = AllSum(everywhere, r.l_acc, r.l_land, r.l_send, r.l_recv)
-    r.l_acc[0] = jnp.zeros(r.l_acc.shape[1:], F32)
-    r.l_acc[0, 0:1] = jnp.sum(d_norm * hat * factor, axis=0, keepdims=True)
-    r.l_acc[0, 1:2] = scale_sums[0]
-    r.l_acc[0, 2:3] = scale_sums[1]
-    late.start()
-    b_home.finish()
-    b_turn = TurnZ(place, r.b_part, b_home.base, r.b_land, r.bz_s, r.bz_r)
-    b_turn.start()
-    for _ in range(4):
-        late.step()
+    late.step()
+    heads_sum.step()
+    for i in range(4):
+        b_home.leave(place.block(jnp.int32(3 - i)))
+    late.step()
+    cap_spread.finish()
+    cap_all = LaneGather(place, r.t_all, r.ta_s, r.ta_r)
+    cap_all.own[...] = r.t_z[...]
+    cap_all.start()
+    heads_spread = SpreadZ(place, r.h_slots, r.hz_send, r.hz_recv)
+    heads_spread.own[...] = heads_sum.step()
+    heads_spread.start()
+    total = late.step()
+    cap_all.pass_on()
+    factors = 1.0 + r.mod[:, 0:width]
+    r.late[...] = jnp.concatenate(
+        [
+            jnp.sum(total * factors, axis=0, keepdims=True),
+            total * gain_in,
+            jnp.zeros((5, width), F32),
+        ],
+        axis=0,
+    )
     out_copy.wait()
     attn_grads.finish()
     r.early[...] = early.step()
     heads_spread.finish()
-    f_turn.finish()
-    a_turn.finish()
+    f_home.finish()
+    a_home.finish()
     cap_all.finish()
     dp_copy.wait()
-    r.late[...] = late.step()
-    b_turn.finish()
+    b_home.finish()
 
 
 def finish_kernel(
     out_own, out_half, dp_own, dp_half, f_land, a_land, b_land, t_all, early, late, heads_in, text,
-    head_rows, band_table, item_band, w_ada,
+    cross_gate, band_table, item_band, w_ada,
     output, d_patches, d_query, d_key, d_value, d_out, d_gate, d_up, d_down, d_ckey, d_cvalue,
     d_ada, d_b_ada, d_attn_in, d_attn_out, d_ffn_in, d_ffn_out, d_g_query, d_g_key, d_g_ckey,
     d_cross, d_band,
@@ -1163,9 +1349,9 @@
         at = slice(z * wf, (z + 1) * wf)
         d_gate[:, at] = f_land[z, :, 0:wf].astype(F32)
         d_up[:, at] = f_land[z, :, wf : 2 * wf].astype(F32)
-        d_down[at] = f_land[z, :, 2 * wf : 3 * wf].astype(F32).T
+        d_down[:, at] = f_land[z, :, 2 * wf : 3 * wf].astype(F32)
         at = slice(z * wq, (z + 1) * wq)
-        d_out[at] = a_land[z, :, 0:wq].astype(F32).T
+        d_out[:, at] = a_land[z, :, 0:wq].astype(F32)
         d_query[:, at] = a_land[z, :, wq : 2 * wq].astype(F32)
         d_key[:, at] = b_land[z, :, 0:wq].astype(F32)
         d_value[:, at] = b_land[z, :, wq : 2 * wq].astype(F32)
@@ -1208,12 +1394,12 @@
     col = lax.broadcasted_iota(jnp.int32, (wq, 128), 1)
     total = jnp.zeros((8, 128), F32)
     for z in range(SPLIT):
-        gate = jnp.tanh(head_rows[z, 2:3, :wq])
+        gate = jnp.tanh(gate_lanes(cross_gate, z, wq))
         terms = heads_in[z, 2:3, :wq] * (1.0 - gate * gate)
         terms = jnp.concatenate([terms, jnp.zeros((7, wq), F32)], axis=0)
         pick = jnp.where(col == lane + z * heads, 1.0, 0.0)
         total = total + jnp.dot(terms, pick, precision=HIGH, preferred_element_type=F32)
-    d_cross[...] = total[0:1]
+    d_cross[...] = total[0:1, : d_cross.shape[0]].reshape(d_cross.shape)
 
 
 def conditioning(band_table, item_band):
@@ -1290,8 +1476,8 @@
         e_land=sum_tile((16, width), 5),
         e_send=sem(6),
         e_recv=sem(6),
-        l_acc=sum_tile((8, width), 5),
-        l_land=sum_tile((8, width), 5),
+        l_acc=sum_tile((ITEMS, width), 5),
+        l_land=sum_tile((ITEMS, width), 5),
         l_send=sem(6),
         l_recv=sem(6),
         h_acc=sum_tile((8, two), 2),
@@ -1321,9 +1507,11 @@
         cap_v=tile((text, wq + HEAD), BF),
         items=tile((group, 1), jnp.int32),
         key_items=tile((lanes, 1, group), jnp.int32),
+        key_cols=tile((lanes, group, 1), jnp.int32),
         cos_t=tile(both + (2 * HEAD,), F32),
         sin_t=tile(both + (2 * HEAD,), F32),
         norm_in=tile(both + (width,), BF),
+        hat_in=tile(both + (width,), BF),
         kq_hat=tile(both + (two,), F32),
         kq_recip=tile(both + (two,), F32),
         kv=tile((lanes, group, two), BF),
@@ -1348,24 +1536,17 @@
         dp_recv=pltpu.SemaphoreType.DMA,
         f_fc=tile((2 * SPLIT, row_dev, 3 * wf), BF),
         f_fy=tile((SPLIT, row_dev, 3 * wf), BF),
-        fh_s=sem(2),
-        fh_r=sem(2),
-        fz_s=sem(4),
-        fz_r=sem(4),
+        f_s=sem(12),
+        f_r=sem(12),
         a_part=tile((4 * SPLIT, row_dev, two), BF),
         a_fc=tile((2 * SPLIT, row_dev, two), BF),
         a_fy=tile((SPLIT, row_dev, two), BF),
-        ah_s=sem(2),
-        ah_r=sem(2),
-        az_s=sem(4),
-        az_r=sem(4),
-        b_part=tile((4 * SPLIT, row_dev, two), BF),
+        a_s=sem(12),
+        a_r=sem(12),
         b_fc=tile((2 * SPLIT, row_dev, two), BF),
         b_fy=tile((SPLIT, row_dev, two), BF),
-        bh_s=sem(2),
-        bh_r=sem(2),
-        bz_s=sem(4),
-        bz_r=sem(4),
+        b_s=sem(12),
+        b_r=sem(12),
         kv_fc=tile((2, group, two), BF),
         kv_fy=tile((1, group, two), BF),
         kvh_s=sem(2),
@@ -1387,10 +1568,7 @@
         q_stack=tile((heads * tok_rows, wq), BF),
         c_stack=tile((heads * tok_rows, wq), BF),
         m_stack=tile((heads * tok_rows, wq), BF),
-        cp_stack=tile((heads * tok_rows, text), BF),
-        cs_stack=tile((heads * tok_rows, text), BF),
-        p_stack=tile((heads * tok_rows, group), BF),
-        s_stack=tile((heads * tok_rows, group), BF),
+        dq_stack=tile((heads * tok_rows, wq), F32),
         dq_s=tile((group, wq), BF),
         dq_raw=tile((group, two), BF),
         dkv_raw=tile((group, two), BF),
@@ -1413,7 +1591,7 @@
     vmem = pl.BlockSpec(memory_space=pltpu.VMEM)
     hbm = pl.BlockSpec(memory_space=pl.ANY)
     smem = pl.BlockSpec(memory_space=pltpu.SMEM)
-    places = dict(caption=hbm, block_item=smem, item_band=smem)
+    places = dict(caption=hbm, block_item=smem, item_band=smem, cross_gate=smem)
     names = list(ins) + list(outs) + list(scratch)
     results = pl.pallas_call(
         functools.partial(layer_kernel, names),
@@ -1797,24 +1975,6 @@
     g_ckey,
     cross_gate,
 ):
-    width = patches.shape[1]
-    wq = w_query.shape[1] // SPLIT
-    rows_in = jnp.concatenate(
-        [jnp.stack([g_attn_in, g_attn_out, g_ffn_in, g_ffn_out]), b_ada.reshape(4, width)]
-    )
-    gains = [vector.reshape(SPLIT, wq) for vector in (g_key, g_query, g_ckey)]
-    pad = jnp.zeros((SPLIT, wq), F32)
-    freqs = FREQ_BASE ** (-(jnp.arange(2 * wq) % (HEAD // 4)).astype(F32) / (HEAD // 4))
-    head_rows = jnp.stack(
-        [
-            jnp.concatenate([gains[0], gains[1]], axis=1),
-            jnp.concatenate([gains[2], pad], axis=1),
-            jnp.concatenate([jnp.repeat(cross_gate, HEAD).reshape(SPLIT, wq), pad], axis=1),
-            jnp.broadcast_to(freqs, (SPLIT, 2 * wq)),
-        ]
-        + [jnp.zeros((SPLIT, 2 * wq), F32)] * 4,
-        axis=1,
-    )
     done = layer_call(
         dict(
             patches=patches,
@@ -1827,15 +1987,22 @@
             w_query=w_query,
             w_key=w_key,
             w_value=w_value,
-            w_out=w_out,
+            w_out=w_out.T,
             w_gate=w_gate,
             w_up=w_up,
-            w_down=w_down,
+            w_down=w_down.T,
             w_ckey=w_ckey,
             w_cvalue=w_cvalue,
             w_ada=w_ada,
-            rows_in=rows_in,
-            head_rows=head_rows,
+            b_ada=b_ada,
+            g_attn_in=g_attn_in,
+            g_attn_out=g_attn_out,
+            g_ffn_in=g_ffn_in,
+            g_ffn_out=g_ffn_out,
+            g_query=g_query,
+            g_key=g_key,
+            g_ckey=g_ckey,
+            cross_gate=cross_gate,
         )
     )
     shape = jax.ShapeDtypeStruct
@@ -1845,18 +2012,18 @@
     results = pl.pallas_call(
         finish_kernel,
         out_shape=(
-            like(patches), like(patches), like(w_query), like(w_key), like(w_value), like(w_out),
-            like(w_gate), like(w_up), like(w_down), like(w_ckey), like(w_cvalue), like(w_ada),
+            like(patches), like(patches), like(w_query), like(w_key), like(w_value), like(w_out.T),
+            like(w_gate), like(w_up), like(w_down.T), like(w_ckey), like(w_cvalue), like(w_ada),
             like(b_ada), like(g_attn_in), like(g_attn_out), like(g_ffn_in), like(g_ffn_out),
-            like(g_query), like(g_key), like(g_ckey), shape((1, 128), F32), like(band_table),
+            like(g_query), like(g_key), like(g_ckey), like(cross_gate), like(band_table),
         ),
-        in_specs=[vmem] * 14 + [smem, vmem],
+        in_specs=[vmem] * 12 + [smem, vmem, smem, vmem],
         out_specs=[vmem] * 22,
         compiler_params=pltpu.CompilerParams(vmem_limit_bytes=VMEM_LIMIT),
         name="finish",
-    )(*done.values(), head_rows, band_table, item_band, w_ada)
+    )(*done.values(), cross_gate, band_table, item_band, w_ada)
     results = list(results)
-    results[20] = results[20][0, : cross_gate.shape[0]]
+    results[5], results[8] = results[5].T, results[8].T
     return tuple(results)
 
 

time: 325 us -> 293 us (0.902)
  local copies, waits for them, and re-layouts: 17.3 us -> 0 us
  Pallas kernels: 306 us -> 292 us
    pallas_call x1, Pallas kernels: 299 us -> 284 us  [layer_call(): pl.pallas_call(functools.partial(layer_kernel, names), out_shape=tuple(ou...]
    unnamed x4 -> x0, local copies, waits for them, and re-layouts: 8.02 us -> none
    another operation x10 -> x0, local copies, waits for them, and re-layouts: 3.5 us -> none  [the longest x4 2.81 us: local(): jnp.stack([g_attn_in, g_attn_out, g_ffn_in, g_ffn_out])]
where the time goes in v5:
time: 293 us; the launch traced here: 292 us
  Pallas kernels  292 us (100%)
    pallas_call x1, Pallas kernels, layer_call(): pl.pallas_call(functools.partial(layer_kernel, names), out_shape=tuple(ou...  284 us
    pallas_call x1, Pallas kernels, local(): pl.pallas_call(finish_kernel, out_shape=(like(patches), like(patches), li...  7.44 us

profile of v5, /device:TPU:0, one launch (start us, length us, event | category | flops | bytes accessed | tf_op | source)
XLA Modules:
  0.0 292.5 jit_solution(12078216876300698599)
XLA Ops:
  0.7 284.2 %layer.1 = (f32[64,1536]{1,0:T(8,128)}, bf16[2,64,1536]{2,1,0:T(8,128)(2,1)}, f32[64,1536]{1,0:T(8,128)}, bf16[2,64,1536]{2,1,0:T(8,128)(2,1)}, bf16[4,96,1536]{...) custom-call(bf16[128,1536]{1,0:T(8,128)(2,1)} %refs_0_.1, ...), custom_call_target="tpu_custom_call" | custom-call | tf_op jit(solution)/shard_map/layer/pallas_call | solution.py:1596
  284.9 7.4 %finish.1 = (f32[128,1536]{1,0:T(8,128)}, f32[128,1536]{1,0:T(8,128)}, f32[96,768]{1,0:T(8,128)}, f32[96,768]{1,0:T(8,128)}, f32[96,768]{1,0:T(8,128)}, /*index=...) custom-call(f32[64,1536]{1,0:T(8,128)} %get-tuple-element.56.out_own, ...), custom_call_target="tpu_custom_call" | custom-call | tf_op jit(solution)/shard_map/finish/pallas_call | solution.py:2012

commit v6 on v5

--- a/solution.py
+++ b/solution.py
@@ -259,11 +259,13 @@
                 block, block, self.send.at[4 + z], self.recv.at[4 + z], place.at_z(z)
             ).wait_recv()
             total = total + self.from_z[z].astype(F32)
+        return total
+
+    def sent(self):
         for z in range(SPLIT):
             self.across(z).wait_send()
         for d in (1, 2, 3):
-            self.along(place.z_to(d)).wait_send()
-        return total
+            self.along(self.place.z_to(d)).wait_send()
 
 
 def flow(place, gather, work, carry, between=None):
@@ -778,6 +780,8 @@
         r.ffn_in[i, :, 0:wf] = r.w_gate[:, at]
         r.ffn_in[i, :, wf : 2 * wf] = r.w_up[:, at]
         r.ffn_in[i, :, 2 * wf : 3 * wf] = r.w_down[:, at]
+    feed = WeightGather(place, r.ffn_in, r.ffn, r.f_send, r.f_recv)
+    feed.start(1)
     tokens.pass_on(2)
     weights.pass_z(2)
     sums.step()
@@ -819,9 +823,8 @@
 
     tokens.pass_on(3)
     weights.pass_z(3)
-    feed = WeightGather(place, r.ffn_in, r.ffn, r.f_send, r.f_recv)
-    for i in (1, 2, 3):
-        feed.start(i)
+    feed.start(2)
+    feed.pass_own()
     for i in range(4):
         weights.pass_y(i)
     r.mod[...] = sums.step() + r.b_ada[...].reshape(1, 4 * width)
@@ -829,7 +832,6 @@
         tokens.arrive(i)
     caption.step()
     weights.finish()
-    feed.pass_own()
 
     keep = LaneGather(place, r.kv, r.kv_send, r.kv_recv)
 
@@ -907,6 +909,7 @@
         ref[...] = jnp.zeros_like(ref)
     split_lump(g)
     attend_into(g)
+    feed.start(3)
     cap_turn.finish()
     cap_raw = (r.cap_z[0].astype(F32) + r.cap_z[1].astype(F32)) + (
         r.cap_z[2].astype(F32) + r.cap_z[3].astype(F32)
@@ -978,6 +981,7 @@
     norms = Gather(place, r.n_buf, r.n_send, r.n_recv)
     norms.own[...] = (hat_three * factor_three).astype(BF)
     norms.start()
+    out_sum.sent()
     tokens.finish()
     keep.sent()
 
@@ -1007,11 +1011,11 @@
     grads = Gather(place, r.g_buf, r.g_send, r.g_recv)
     grads.own[...] = normed_back(grad_four * gain_out, hat_four, recip_four).astype(BF)
     grads.start()
+    down.sent()
     output = resid + tanh_two * hat_four * gain_out
     r.out_own[...] = output
     r.out_half[0] = output.astype(BF)
     out_copy = remote(r.out_half.at[0], r.out_half.at[1], r.o_send, r.o_recv, place.x_peer)
-    out_copy.start()
     everywhere = along[:2] + [place.x_peer] + along[2:]
     early = AllSum(everywhere, r.e_acc, r.e_land, r.e_send, r.e_recv)
     r.e_acc[0] = jnp.zeros(r.e_acc.shape[1:], F32)
@@ -1062,7 +1066,6 @@
 
     lax.fori_loop(0, SPLIT, ffn_matrices, 0)
     f_home.step(place.block(jnp.int32(3)))
-    f_home.step(place.block(jnp.int32(2)))
     grad_norm = back.finish()
     grads.finish()
     d_resid = grad_out + normed_back(grad_norm * factor_three, hat_three, recip_three)
@@ -1070,6 +1073,7 @@
     attn_grads = Gather(place, r.x_buf, r.a_send, r.a_recv)
     attn_grads.own[...] = normed_back(grad_two * gain_attn, hat_two, recip_two).astype(BF)
     attn_grads.start()
+    back.sent()
     r.dp_own[...] = d_resid
     scale_sums = item_sums(grad_norm * hat_three * gain_ffn, item)
     gate_sums = item_sums(d_resid * hat_two * gain_attn * (1.0 - tanh_one * tanh_one), item)
@@ -1157,9 +1161,9 @@
             def _():
                 early.step()
 
-        @pl.when(i < 2)
+        @pl.when(i < 3)
         def _():
-            f_home.step(place.block(1 - i))
+            f_home.step(place.block(2 - i))
 
         @pl.when(i >= 1)
         def _():
@@ -1180,6 +1184,7 @@
         return carry
 
     lax.fori_loop(0, 4, store_keys, 0)
+    out_copy.start()
     cap_home = LaneScatter(place, r.t_part, r.t_fc, r.t_fy, r.t_s, r.t_r)
     for i in range(4):
         at = slice(i * words, (i + 1) * words)
@@ -1293,6 +1298,7 @@
     r.dp_half[0] = d_patches.astype(BF)
     dp_copy = remote(r.dp_half.at[0], r.dp_half.at[1], r.dp_send, r.dp_recv, place.x_peer)
     dp_copy.start()
+    in_sum.sent()
     late.step()
     heads_sum.step()
     for i in range(4):

time: 293 us -> 290 us (0.990)
  Pallas kernels: 292 us -> 289 us
where the time goes in v6:
time: 290 us
  Pallas kernels  289 us (100%)
    pallas_call x1, Pallas kernels, layer_call(): pl.pallas_call(functools.partial(layer_kernel, names), out_shape=tuple(ou...  282 us
    pallas_call x1, Pallas kernels, local(): pl.pallas_call(finish_kernel, out_shape=(like(patches), like(patches), li...  7.44 us

profile of v6, /device:TPU:0, one launch (start us, length us, event | category | flops | bytes accessed | tf_op | source)
XLA Modules:
  0.0 290.2 jit_solution(11127017900252817385)
XLA Ops:
  0.7 281.9 %layer.1 = (f32[64,1536]{1,0:T(8,128)}, bf16[2,64,1536]{2,1,0:T(8,128)(2,1)}, f32[64,1536]{1,0:T(8,128)}, bf16[2,64,1536]{2,1,0:T(8,128)(2,1)}, bf16[4,96,1536]{...) custom-call(bf16[128,1536]{1,0:T(8,128)(2,1)} %refs_0_.1, ...), custom_call_target="tpu_custom_call" | custom-call | tf_op jit(solution)/shard_map/layer/pallas_call | solution.py:1602
  282.6 7.4 %finish.1 = (f32[128,1536]{1,0:T(8,128)}, f32[128,1536]{1,0:T(8,128)}, f32[96,768]{1,0:T(8,128)}, f32[96,768]{1,0:T(8,128)}, f32[96,768]{1,0:T(8,128)}, /*index=...) custom-call(f32[64,1536]{1,0:T(8,128)} %get-tuple-element.56.out_own, ...), custom_call_target="tpu_custom_call" | custom-call | tf_op jit(solution)/shard_map/finish/pallas_call | solution.py:2018
